TPU v7x, 32 devices: a whole 2x2x4 slice. The times are simulated.
32 devices in a mesh: groups: 2 (over y), blk: 4 (over z), rep: 4 (over x, core).
Axes of the slice: x: 2, y: 2, z: 4, core: 2. Of those that a mesh axis runs over, the one named last changes fastest.
Arguments:
- features: bfloat16 [4096, 512], P(('groups', 'blk', 'rep')), parts along dimension 0, may hold values from -6 to 6
- order_weights: bfloat16 [3, 512, 512], replicated, may hold values from -0.15625 to 0.15625
- laplacian_blocks: bfloat16 [8, 4, 4, 4, 128, 128], P(('groups', 'blk'), 'rep'), parts along dimension 0, may hold values from -0.15625 to 0.15625
- tile_place: int32 [8, 4, 4, 4], P(('groups', 'blk'), 'rep'), parts along dimension 0, may hold values from 0 to 3, as said below
- tile_count: int32 [8, 4, 4], P(('groups', 'blk'), 'rep'), parts along dimension 0, may hold values from 1 to 4
Outputs:
- mixed: bfloat16 [4096, 512], P(('groups', 'blk', 'rep')), parts along dimension 0
There are 2 independent parts, one for each index of `groups`. A program takes and returns all parts, laid end to end along the dimension named above; an argument that names none is the same for every part. Nothing has to cross between parts.
Inputs may be any that keep to these rules, and one draw needn't show every extreme that they name: `tile_place`: within each strip, lane and source strip the 4 positions are distinct numbers below 4; only the first tile_count slots are live.
All inputs are finite; a program needn't handle non-finite values.
Results may differ from a plain program's by a relative error of at most 0.0055.
Values may be sent and summed in bfloat16 or wider, within the bound.
No kernel may reach another device: no remote copies, remote signals or barrier semaphores. Data moves between devices by JAX's collectives and lax.ppermute only.
A program may use at most 64 MiB of HBM per device.

v0:
```python
import jax
import jax.numpy as jnp
from jax import lax
from jax.sharding import PartitionSpec as P


def from_behind(array, axis, by):
    peers = lax.axis_size(axis)
    return lax.ppermute(array, axis, [(i, (i + by) % peers) for i in range(peers)])


def build_dense(blocks_all, place_all, count_all, row_tiles, col_tiles):
    blk_count = blocks_all.shape[0]
    slot_count = blocks_all.shape[1]
    tile_size = blocks_all.shape[-1]
    live_mask = jnp.arange(slot_count)[None, :] < count_all[:, None]
    spots = jnp.arange(row_tiles * col_tiles)
    hits = (place_all[..., None] == spots[None, None, :]) & live_mask[..., None]
    selector = (
        jnp.where(hits, 1.0, 0.0)
        .astype(jnp.bfloat16)
        .reshape(blk_count, slot_count, row_tiles, col_tiles)
    )
    dense = jnp.einsum(
        "jcrq,jcab->rajqb", selector, blocks_all, preferred_element_type=jnp.bfloat16
    )
    return dense.reshape(row_tiles * tile_size, blk_count * col_tiles * tile_size)


def apply_lap(panel_begin, dense_strip):
    blk_count = lax.axis_size("blk")
    own_index = lax.axis_index("blk")
    rows_dev = panel_begin.shape[0]
    feat_width = panel_begin.shape[1]

    def store(panels_now, current_panel, source):
        return lax.dynamic_update_index_in_dim(panels_now, current_panel, source, 0)

    panels = jnp.zeros((blk_count, rows_dev, feat_width), panel_begin.dtype)
    panels = store(panels, panel_begin, own_index)

    def advance(offset, loop_state):
        current_panel, panels_now = loop_state
        current_panel = from_behind(current_panel, "blk", 1)
        return (current_panel, store(panels_now, current_panel, (own_index - offset) % blk_count))

    panel_end, panels = lax.fori_loop(1, blk_count, advance, (panel_begin, panels))
    running_value = jnp.dot(
        dense_strip,
        panels.reshape(blk_count * rows_dev, feat_width),
        preferred_element_type=jnp.float32,
    )
    return lax.psum_scatter(running_value, "rep", scatter_dimension=0, tiled=True)


def per_device(features, order_weights, laplacian_blocks, tile_place, tile_count):
    blocks_all = laplacian_blocks[0, 0]
    place_all = tile_place[0, 0]
    count_all = tile_count[0, 0]
    tile_size = blocks_all.shape[-1]
    col_tiles = features.shape[0] // tile_size
    row_tiles = features.shape[0] * lax.axis_size("rep") // tile_size
    dense_strip = build_dense(blocks_all, place_all, count_all, row_tiles, col_tiles)
    first = apply_lap(features, dense_strip).astype(jnp.bfloat16)
    second_sum = apply_lap(first, dense_strip)
    second = (2.0 * second_sum - features.astype(jnp.float32)).astype(jnp.bfloat16)
    stacked = jnp.concatenate([features, first, second], axis=1)
    feat_width = features.shape[1]
    mixed = jnp.dot(
        stacked,
        order_weights.reshape(3 * feat_width, feat_width),
        preferred_element_type=jnp.float32,
    )
    return mixed.astype(jnp.bfloat16)


def solution(mesh):
    in_specs = (
        P(("groups", "blk", "rep"), None),
        P(),
        P(("groups", "blk"), "rep", None, None, None, None),
        P(("groups", "blk"), "rep", None, None),
        P(("groups", "blk"), "rep", None),
    )
    out_specs = P(("groups", "blk", "rep"), None)
    return jax.shard_map(
        per_device, mesh=mesh, in_specs=in_specs, out_specs=out_specs, check_vma=False
    )
```

profile of v0, /device:TPU:0, one launch (start us, length us, event | category | flops | bytes accessed | tf_op | source)
XLA Modules:
  0.0 111.1 jit_solution(14809424864039489733)
XLA Ops:
  6.5 0.0 copy-start
  6.5 0.0 copy-start.1
  6.5 0.0 reduce-scatter.3.cloned.1.call-start
  6.5 0.9 iota_compare_fusion.1
  7.4 0.0 copy-start.2
  7.4 1.6 %convolution_bitcast_fusion = bf16[4,128,4,1,128]{4,0,1,2,3:T(4,128)(2,1)S(1)} fusion(bf16[4,4,128,128]{3,2,1,0:T(8,128)(2,1)} %bitcast.45, s32[4,4]{1,0:T(4,128)} %bitcast.46, pred[4,4]{1,0:T(4,128)(4,1)S(1)} %iota_compare_fusion.1), kind=kOutput, calls=%fused_computation.2 | convolution fusion | flops 2097408 | bytes 1048656 | tf_op jit(solution)/shard_map/jcrq,jcab->rajqb/dot_general | solution.py:24
  9.0 0.4 copy.8
  9.5 0.0 copy-done.1
  9.5 0.0 copy-done.2
  9.5 22.4 %while.34 = (s32[]{:T(128)}, bf16[128,512]{1,0:T(8,128)(2,1)S(1)}, bf16[4,128,512]{2,1,0:T(8,128)(2,1)S(1)}, s32[]{:T(128)}, s32[]{:T(128)}, /*index=5*/s32[]{:T(128)}, s32[]{:T(128)}, s32[]{:T(128)}) while((s32[]{:T(128)}, bf16[128,512]{1,0:T(8,128)(2,1)S(1)}, bf16[4,128,512]{2,1,0:T(8,128)(2,1)S(1)}, s32[]{:T(128)}, s32[]{:T(128)}, ...), condition=%wide.region_1.2_spmd, body=%wide.region_0.1_spmd.sunk | while | flops 17 | bytes 1048860 | solution.py:47
  9.5 3.1 %collective-permute-start = (bf16[128,512]{1,0:T(8,128)(2,1)S(1)}, bf16[128,512]{1,0:T(8,128)(2,1)S(1)}, u32[]{:S(2)}, u32[]{:S(2)}) collective-permute-start(bf16[128,512]{1,0:T(8,128)(2,1)S(1)} %get-tuple-element.306), channel_id=1, source_target_pairs={{0,4},{4,8},{8,12},{12,0},{1,5},{5,9},{9,13},{13,1},{2,6},{6,10},{... | collective-permute-start | bytes 393224 | tf_op jit(solution)/shard_map/while/body/eval_jaxpr/ppermute | solution.py:9
  12.6 5.5 %collective-permute-done = bf16[128,512]{1,0:T(8,128)(2,1)S(1)} collective-permute-done((bf16[128,512]{1,0:T(8,128)(2,1)S(1)}, bf16[128,512]{1,0:T(8,128)(2,1)S(1)}, u32[]{:S(2)}, u32[]{:S(2)}) %collective-permute-start) | collective-permute-done | bytes 131104 | tf_op jit(solution)/shard_map/while/body/eval_jaxpr/ppermute | solution.py:9
  18.2 0.1 collective-permute-start
  18.3 6.7 %collective-permute-done = bf16[128,512]{1,0:T(8,128)(2,1)S(1)} collective-permute-done((bf16[128,512]{1,0:T(8,128)(2,1)S(1)}, bf16[128,512]{1,0:T(8,128)(2,1)S(1)}, u32[]{:S(2)}, u32[]{:S(2)}) %collective-permute-start) | collective-permute-done | bytes 131104 | tf_op jit(solution)/shard_map/while/body/eval_jaxpr/ppermute | solution.py:9
  25.0 0.1 collective-permute-start
  25.1 6.7 %collective-permute-done = bf16[128,512]{1,0:T(8,128)(2,1)S(1)} collective-permute-done((bf16[128,512]{1,0:T(8,128)(2,1)S(1)}, bf16[128,512]{1,0:T(8,128)(2,1)S(1)}, u32[]{:S(2)}, u32[]{:S(2)}) %collective-permute-start) | collective-permute-done | bytes 131104 | tf_op jit(solution)/shard_map/while/body/eval_jaxpr/ppermute | solution.py:9
  31.9 1.4 %fusion.2 = f32[512,512]{1,0:T(8,128)} fusion(bf16[512,512]{1,0:T(8,128)(2,1)S(1)} %bitcast.44, bf16[64,8,4,128]{3,2,1,0:T(4,128)(2,1)S(1)} %bitcast.41), kind=kOutput, calls=%fused_computation.6 | convolution fusion | flops 268435456 | bytes 2097152 | tf_op jit(solution)/shard_map/dot_general | solution.py:48
  33.3 0.0 reduce-scatter.3.cloned.1.call-update
  33.3 0.0 reduce-scatter.5.cloned.1.call-start
  33.4 23.2 %reduce-scatter.3.cloned.1.call-done = f32[128,512]{1,0:T(8,128)} async-done(((f32[512,512]{1,0:T(8,128)}), f32[128,512]{1,0:T(8,128)}) %reduce-scatter.3.cloned.1.call-update) | async-done | bytes 262160 | tf_op jit(solution)/shard_map/reduce_scatter | solution.py:53
  56.6 1.0 bitcast_dynamic-update-slice_fusion.2
  57.6 20.9 %while.35 = (s32[]{:T(128)}, bf16[128,512]{1,0:T(8,128)(2,1)S(1)}, bf16[4,128,512]{2,1,0:T(8,128)(2,1)S(1)}, s32[]{:T(128)}, s32[]{:T(128)}, /*index=5*/s32[]{:T(128)}, s32[]{:T(128)}, s32[]{:T(128)}) while((s32[]{:T(128)}, bf16[128,512]{1,0:T(8,128)(2,1)S(1)}, bf16[4,128,512]{2,1,0:T(8,128)(2,1)S(1)}, s32[]{:T(128)}, s32[]{:T(128)}, ...), condition=%wide.region_4.5_spmd, body=%wide.region_3.4_spmd.sunk | while | flops 17 | bytes 1048860 | solution.py:47
  57.6 1.6 %collective-permute-start.1 = (bf16[128,512]{1,0:T(8,128)(2,1)S(1)}, bf16[128,512]{1,0:T(8,128)(2,1)S(1)}, u32[]{:S(2)}, u32[]{:S(2)}) collective-permute-start(bf16[128,512]{1,0:T(8,128)(2,1)S(1)} %get-tuple-element.330), channel_id=1, source_target_pairs={{0,4},{4,8},{8,12},{12,0},{1,5},{5,9},{9,13},{13,1},{2,6},{6,10},{... | collective-permute-start | bytes 393224 | tf_op jit(solution)/shard_map/while/body/eval_jaxpr/ppermute | solution.py:9
  59.2 5.5 %collective-permute-done.1 = bf16[128,512]{1,0:T(8,128)(2,1)S(1)} collective-permute-done((bf16[128,512]{1,0:T(8,128)(2,1)S(1)}, bf16[128,512]{1,0:T(8,128)(2,1)S(1)}, u32[]{:S(2)}, u32[]{:S(2)}) %collective-permute-start.1) | collective-permute-done | bytes 131104 | tf_op jit(solution)/shard_map/while/body/eval_jaxpr/ppermute | solution.py:9
  64.8 0.1 collective-permute-start.1
  64.8 6.7 %collective-permute-done.1 = bf16[128,512]{1,0:T(8,128)(2,1)S(1)} collective-permute-done((bf16[128,512]{1,0:T(8,128)(2,1)S(1)}, bf16[128,512]{1,0:T(8,128)(2,1)S(1)}, u32[]{:S(2)}, u32[]{:S(2)}) %collective-permute-start.1) | collective-permute-done | bytes 131104 | tf_op jit(solution)/shard_map/while/body/eval_jaxpr/ppermute | solution.py:9
  71.6 0.1 collective-permute-start.1
  71.7 6.7 %collective-permute-done.1 = bf16[128,512]{1,0:T(8,128)(2,1)S(1)} collective-permute-done((bf16[128,512]{1,0:T(8,128)(2,1)S(1)}, bf16[128,512]{1,0:T(8,128)(2,1)S(1)}, u32[]{:S(2)}, u32[]{:S(2)}) %collective-permute-start.1) | collective-permute-done | bytes 131104 | tf_op jit(solution)/shard_map/while/body/eval_jaxpr/ppermute | solution.py:9
  78.5 1.4 %fusion = f32[512,512]{1,0:T(8,128)} fusion(bf16[512,512]{1,0:T(8,128)(2,1)S(1)} %bitcast.43, bf16[64,8,4,128]{3,2,1,0:T(4,128)(2,1)S(1)} %bitcast.42), kind=kOutput, calls=%fused_computation.4 | convolution fusion | flops 268435456 | bytes 2097152 | tf_op jit(solution)/shard_map/dot_general | solution.py:48
  79.9 0.0 reduce-scatter.5.cloned.1.call-update
  79.9 22.3 %reduce-scatter.5.cloned.1.call-done = f32[128,512]{1,0:T(8,128)} async-done(((f32[512,512]{1,0:T(8,128)}), f32[128,512]{1,0:T(8,128)}) %reduce-scatter.5.cloned.1.call-update) | async-done | bytes 262160 | tf_op jit(solution)/shard_map/reduce_scatter | solution.py:53
  102.2 1.0 subtract_convert_fusion
  103.2 0.0 copy-done
  103.2 1.0 convolution_convert_fusion
  (16 shorter events, 0.3 us)
Async XLA Ops:
  6.5 96.7 %copy-start = (bf16[3,512,512]{2,1,0:T(8,128)(2,1)S(1)}, bf16[3,512,512]{2,1,0:T(8,128)(2,1)}, u32[]{:S(2)}) copy-start(bf16[3,512,512]{2,1,0:T(8,128)(2,1)} %param.10) | copy-start | bytes 4718596
  6.5 2.9 %copy-start.1 = (bf16[128,512]{1,0:T(8,128)(2,1)S(1)}, bf16[128,512]{1,0:T(8,128)(2,1)}, u32[]{:S(2)}) copy-start(bf16[128,512]{1,0:T(8,128)(2,1)} %param.9) | copy-start | bytes 393220
  6.5 50.0 %reduce-scatter.3.cloned.1.call-start = ((), (), s32[]{:S(2)}) async-start(), calls=%async_computation.2 | async-start | bytes 1310720 | tf_op jit(solution)/shard_map/reduce_scatter | solution.py:53
  7.4 2.1 %copy-start.2 = (bf16[128,512]{1,0:T(8,128)(2,1)S(1)}, bf16[128,512]{1,0:T(8,128)(2,1)}, u32[]{:S(2)}) copy-start(bf16[128,512]{1,0:T(8,128)(2,1)} %param.9) | copy-start | bytes 393220
  9.5 8.6 %collective-permute-start = (bf16[128,512]{1,0:T(8,128)(2,1)S(1)}, bf16[128,512]{1,0:T(8,128)(2,1)S(1)}, u32[]{:S(2)}, u32[]{:S(2)}) collective-permute-start(bf16[128,512]{1,0:T(8,128)(2,1)S(1)} %get-tuple-element.306), channel_id=1, source_target_pairs={{0,4},{4,8},{8,12},{12,0},{1,5},{5,9},{9,13},{13,1},{2,6},{6,10},{... | collective-permute-start | bytes 393224 | tf_op jit(solution)/shard_map/while/body/eval_jaxpr/ppermute | solution.py:9
  18.2 6.8 %collective-permute-start = (bf16[128,512]{1,0:T(8,128)(2,1)S(1)}, bf16[128,512]{1,0:T(8,128)(2,1)S(1)}, u32[]{:S(2)}, u32[]{:S(2)}) collective-permute-start(bf16[128,512]{1,0:T(8,128)(2,1)S(1)} %get-tuple-element.306), channel_id=1, source_target_pairs={{0,4},{4,8},{8,12},{12,0},{1,5},{5,9},{9,13},{13,1},{2,6},{6,10},{... | collective-permute-start | bytes 393224 | tf_op jit(solution)/shard_map/while/body/eval_jaxpr/ppermute | solution.py:9
  25.0 6.8 %collective-permute-start = (bf16[128,512]{1,0:T(8,128)(2,1)S(1)}, bf16[128,512]{1,0:T(8,128)(2,1)S(1)}, u32[]{:S(2)}, u32[]{:S(2)}) collective-permute-start(bf16[128,512]{1,0:T(8,128)(2,1)S(1)} %get-tuple-element.306), channel_id=1, source_target_pairs={{0,4},{4,8},{8,12},{12,0},{1,5},{5,9},{9,13},{13,1},{2,6},{6,10},{... | collective-permute-start | bytes 393224 | tf_op jit(solution)/shard_map/while/body/eval_jaxpr/ppermute | solution.py:9
  33.3 68.9 %reduce-scatter.5.cloned.1.call-start = ((), (), s32[]{:S(2)}) async-start(), calls=%async_computation.3 | async-start | bytes 1310720 | tf_op jit(solution)/shard_map/reduce_scatter | solution.py:53
  57.6 7.1 %collective-permute-start.1 = (bf16[128,512]{1,0:T(8,128)(2,1)S(1)}, bf16[128,512]{1,0:T(8,128)(2,1)S(1)}, u32[]{:S(2)}, u32[]{:S(2)}) collective-permute-start(bf16[128,512]{1,0:T(8,128)(2,1)S(1)} %get-tuple-element.330), channel_id=1, source_target_pairs={{0,4},{4,8},{8,12},{12,0},{1,5},{5,9},{9,13},{13,1},{2,6},{6,10},{... | collective-permute-start | bytes 393224 | tf_op jit(solution)/shard_map/while/body/eval_jaxpr/ppermute | solution.py:9
  64.8 6.8 %collective-permute-start.1 = (bf16[128,512]{1,0:T(8,128)(2,1)S(1)}, bf16[128,512]{1,0:T(8,128)(2,1)S(1)}, u32[]{:S(2)}, u32[]{:S(2)}) collective-permute-start(bf16[128,512]{1,0:T(8,128)(2,1)S(1)} %get-tuple-element.330), channel_id=1, source_target_pairs={{0,4},{4,8},{8,12},{12,0},{1,5},{5,9},{9,13},{13,1},{2,6},{6,10},{... | collective-permute-start | bytes 393224 | tf_op jit(solution)/shard_map/while/body/eval_jaxpr/ppermute | solution.py:9
  71.6 6.8 %collective-permute-start.1 = (bf16[128,512]{1,0:T(8,128)(2,1)S(1)}, bf16[128,512]{1,0:T(8,128)(2,1)S(1)}, u32[]{:S(2)}, u32[]{:S(2)}) collective-permute-start(bf16[128,512]{1,0:T(8,128)(2,1)S(1)} %get-tuple-element.330), channel_id=1, source_target_pairs={{0,4},{4,8},{8,12},{12,0},{1,5},{5,9},{9,13},{13,1},{2,6},{6,10},{... | collective-permute-start | bytes 393224 | tf_op jit(solution)/shard_map/while/body/eval_jaxpr/ppermute | solution.py:9
Sparse Core Ops, SparseCore 0:
  33.4 23.0 reduce-scatter.2
  80.0 22.1 reduce-scatter.4
where the time goes:
time: 111 us
  waiting for transfers between devices  83.5 us (75%)
  between operations  13.5 us (12%)
  matrix products  5.44 us (5%)
  starting transfers between devices  4.91 us (4%)
  other arithmetic  2.82 us (3%)
    reduce_scatter x2, waiting for transfers between devices, apply_lap(): lax.psum_scatter(running_value, 'rep', scatter_dimension=0, tiled=True)  45.5 us
    ppermute x6, waiting for transfers between devices, from_behind(): lax.ppermute(array, axis, [(i, (i + by) % peers) for i in range(peers)])  38 us
    ppermute x6, starting transfers between devices, from_behind(): lax.ppermute(array, axis, [(i, (i + by) % peers) for i in range(peers)])  4.87 us
    dot_general x2, matrix products, apply_lap(): jnp.dot(dense_strip, panels.reshape(blk_count * rows_dev, feat_width), pr...  2.81 us
  transfers between devices with their start and end apart: 8, of which 8 were waited for; matrix products, arithmetic and copies ran while one was open for 0% of the time, Pallas kernels for 0%

commit v1 on v0

v1 whole, which is shorter than its diff:
```python
import functools

import jax
import jax.numpy as jnp
from jax import lax
from jax.experimental import pallas as pl
from jax.experimental.pallas import tpu as pltpu
from jax.sharding import PartitionSpec as P

BF16 = jnp.bfloat16
F32 = jnp.float32


def swap(array, axis, mask):
    peers = lax.axis_size(axis)
    return lax.ppermute(array, axis, [(i, i ^ mask) for i in range(peers)])


def call(kernel, out_shapes, *args, scalars=0, scratch=(), vmem=None, flops=0):
    smem = pl.BlockSpec(memory_space=pltpu.SMEM)
    whole = pl.BlockSpec(memory_space=pltpu.VMEM)
    size = sum(a.size * a.dtype.itemsize for a in args)
    return pl.pallas_call(
        kernel,
        out_shape=out_shapes,
        in_specs=[smem] * scalars + [whole] * (len(args) - scalars),
        out_specs=jax.tree.map(lambda _: whole, out_shapes),
        scratch_shapes=list(scratch),
        compiler_params=pltpu.CompilerParams(vmem_limit_bytes=vmem or (16 << 20)),
        cost_estimate=pl.CostEstimate(flops=flops, bytes_accessed=size, transcendentals=0),
    )(*args)


def dense_kernel(where_ref, place_ref, count_ref, blocks_ref, dense_ref):
    n_blk, cap, tile, _ = blocks_ref.shape
    own = where_ref[0]
    dense_ref[...] = jnp.zeros_like(dense_ref)
    for m in range(n_blk):
        j = own ^ m
        for slot in range(cap):

            @pl.when(slot < count_ref[j])
            def _():
                row = pl.multiple_of(place_ref[j, slot] * tile, tile)
                dense_ref[pl.ds(row, tile), m * tile : (m + 1) * tile] = blocks_ref[j, slot]


def dot(a, b):
    return jnp.dot(a, b, preferred_element_type=F32)


def first_kernel(n_blk, n_rep, tile, *refs):
    lanes, refs = refs[:n_rep], refs[n_rep:]
    pieces, out_ref = refs[:-1], refs[-1]
    chips = n_rep // 2
    total = None
    for m in range(n_blk):
        for k in range(n_rep):
            part = dot(lanes[k][:, m * tile : (m + 1) * tile], pieces[m * chips + k // 2][k % 2])
            total = part if total is None else total + part
    out_ref[...] = total.astype(BF16)


def second_kernel(n_blk, n_rep, tile, where_ref, *refs):
    lanes, refs = refs[:n_rep], refs[n_rep:]
    firsts, refs = refs[:n_blk], refs[n_blk:]
    chips = n_rep // 2
    feats, out_ref, total_ref = refs[:chips], refs[chips], refs[chips + 1]
    rep = where_ref[1]
    total = None
    for m in range(n_blk):
        for k in range(n_rep):
            rows = pl.ds(pl.multiple_of((rep ^ k) * tile, tile), tile)
            part = dot(lanes[k][:, m * tile : (m + 1) * tile], firsts[m][rows, :])
            total = part if total is None else total + part
    total_ref[...] = total
    for k in range(n_rep):
        rows = pl.ds(pl.multiple_of((rep ^ k) * tile, tile), tile)
        out_ref[rows, :] = (2.0 * total_ref[rows, :] - feats[k // 2][k % 2].astype(F32)).astype(BF16)


def weigh(rep, n_rep, near_ref, far_ref, weight_ref, order):
    chips, _, width = near_ref.shape
    total = None
    for k in range(n_rep):
        lane = rep ^ k
        at = (lane % 2) * chips + lane // 2
        rows = pl.ds(pl.multiple_of(at * width, width), width)
        piece = far_ref[k // 2] if k % 2 else near_ref[k // 2]
        part = dot(piece, weight_ref[order, rows, :])
        total = part if total is None else total + part
    return total


def early_kernel(n_rep, where_ref, feats_ref, near_ref, far_ref, weight_ref, out_ref):
    total = dot(feats_ref[...], weight_ref[0])
    out_ref[...] = total + weigh(where_ref[1], n_rep, near_ref, far_ref, weight_ref, 1)


def last_kernel(n_rep, where_ref, early_ref, near_ref, far_ref, weight_ref, out_ref):
    total = early_ref[...] + weigh(where_ref[1], n_rep, near_ref, far_ref, weight_ref, 2)
    out_ref[...] = total.astype(BF16)


def to_owners(strip, rep, n_rep, tile):
    chips = n_rep // 2
    x, c = rep // 2, rep % 2
    got = []
    for i in range(chips):
        rows = lax.dynamic_slice_in_dim(strip, (x ^ i) * 2 * tile, 2 * tile, 0)
        got.append(swap(rows, "rep", 2 * i) if i else rows)
    got = jnp.stack(got).reshape(chips, 2, tile, strip.shape[1])
    near = lax.dynamic_index_in_dim(got, c, 1, keepdims=False)
    far = swap(lax.dynamic_index_in_dim(got, 1 - c, 1, keepdims=False), "rep", 1)
    return near, far


def per_device(features, order_weights, laplacian_blocks, tile_place, tile_count):
    n_blk, n_rep = lax.axis_size("blk"), lax.axis_size("rep")
    blk, rep = lax.axis_index("blk"), lax.axis_index("rep")
    chips = n_rep // 2
    x, c = rep // 2, rep % 2
    tile, feat = features.shape
    strip = n_rep * tile
    width = feat // n_rep
    half = feat // 2
    where = jnp.stack([blk, rep]).astype(jnp.int32)
    vmem = max(16 << 20, int(1.25 * (strip * n_blk * strip + 4 * n_blk * strip * 128) * 2) + (12 << 20))

    kept = lax.dynamic_slice_in_dim(features, c * half, half, 1)
    given = lax.dynamic_slice_in_dim(features, (1 - c) * half, half, 1)
    chip_rows = jnp.stack([kept, swap(given, "rep", 1)])
    pieces = []
    for i in range(chips):
        piece = lax.dynamic_slice_in_dim(chip_rows, (x ^ i) * width, width, 2)
        pieces.append(swap(piece, "rep", 2 * i) if i else piece)

    dense = call(
        dense_kernel,
        jax.ShapeDtypeStruct((strip, n_blk * tile), BF16),
        where, tile_place[0, 0], tile_count[0, 0], laplacian_blocks[0, 0],
        scalars=3, vmem=vmem,
    )
    lanes = []
    for i in range(chips):
        got = swap(dense, "rep", 2 * i) if i else dense
        lanes += [got, swap(got, "rep", 1)]

    gathered = []
    for m in range(n_blk):
        gathered += [swap(piece, "blk", m) if m else piece for piece in pieces]
    strip_shape = jax.ShapeDtypeStruct((strip, width), BF16)
    macs = 2 * strip * n_blk * strip * width
    first = call(
        functools.partial(first_kernel, n_blk, n_rep, tile), strip_shape, *lanes, *gathered,
        vmem=vmem, flops=macs,
    )
    firsts = [swap(first, "blk", m) if m else first for m in range(n_blk)]
    early_near, early_far = to_owners(first, rep, n_rep, tile)
    early = call(
        functools.partial(early_kernel, n_rep),
        jax.ShapeDtypeStruct((tile, feat), F32),
        where, features, early_near, early_far, order_weights,
        scalars=1,
    )
    second = call(
        functools.partial(second_kernel, n_blk, n_rep, tile), strip_shape, where, *lanes, *firsts, *pieces,
        scalars=1, scratch=[pltpu.VMEM((strip, width), F32)], vmem=vmem, flops=macs,
    )
    near, far = to_owners(second, rep, n_rep, tile)
    return call(
        functools.partial(last_kernel, n_rep),
        jax.ShapeDtypeStruct((tile, feat), BF16),
        where, early, near, far, order_weights,
        scalars=1,
    )


def solution(mesh):
    in_specs = (
        P(("groups", "blk", "rep"), None),
        P(),
        P(("groups", "blk"), "rep", None, None, None, None),
        P(("groups", "blk"), "rep", None, None),
        P(("groups", "blk"), "rep", None),
    )
    out_specs = P(("groups", "blk", "rep"), None)
    return jax.shard_map(
        per_device, mesh=mesh, in_specs=in_specs, out_specs=out_specs, check_vma=False
    )
```

time: 111 us -> 60.2 us (0.54)
  waiting for transfers between devices: 83.5 us -> 27.9 us
  starting transfers between devices: 4.91 us -> 23.4 us
  between operations: 13.5 us -> 0.13 us
  matrix products: 5.44 us -> 0 us
  Pallas kernels: 0 us -> 5.16 us
  other arithmetic: 2.82 us -> 0.12 us
  local copies, waits for them, and re-layouts: 0.67 us -> 3.3 us
    reduce_scatter x2 -> x0, waiting for transfers between devices: 45.5 us -> none  [apply_lap(): lax.psum_scatter(running_value, 'rep', scatter_dimension=0, tiled=True)]
    ppermute x6 -> x18, starting transfers between devices: 4.87 us -> 23.4 us  [swap(): return lax.ppermute(array, axis, [(i, i ^ mask) for i in range(peers)])]
    ppermute x6 -> x18, waiting for transfers between devices: 38 us -> 27.9 us  [swap(): return lax.ppermute(array, axis, [(i, i ^ mask) for i in range(peers)])]
    dot_general x4 -> x0, matrix products: 5.44 us -> none  [the longest x2 2.81 us: apply_lap(): jnp.dot(dense_strip, panels.reshape(blk_count * rows_dev, feat_width), pr...]
    pallas_call x0 -> x5, Pallas kernels: none -> 5.16 us  [call(): pl.pallas_call(kernel, out_shape=out_shapes, in_specs=[smem] * scalars +...]
    unnamed x7 -> x10, local copies, waits for them, and re-layouts: 0.02 us -> 2.39 us
  transfers between devices with their start and end apart: 8 -> 18, of which waited for: 8 -> 9; matrix products, arithmetic and copies ran while one was open for 0% -> 2% of each run, Pallas kernels for 0% -> 4%
where the time goes in v1:
time: 60.2 us; the launch traced here: 59.9 us
  waiting for transfers between devices  27.9 us (46%)
  starting transfers between devices  23.4 us (39%)
  Pallas kernels  5.16 us (9%)
  local copies, waits for them, and re-layouts  3.3 us (5%)
    ppermute x18, waiting for transfers between devices, swap(): return lax.ppermute(array, axis, [(i, i ^ mask) for i in range(peers)])  27.9 us
    ppermute x18, starting transfers between devices, swap(): return lax.ppermute(array, axis, [(i, i ^ mask) for i in range(peers)])  23.4 us
    pallas_call x5, Pallas kernels, call(): pl.pallas_call(kernel, out_shape=out_shapes, in_specs=[smem] * scalars +...  5.16 us
    unnamed x10, local copies, waits for them, and re-layouts  2.39 us
  transfers between devices with their start and end apart: 18, of which 9 were waited for; matrix products, arithmetic and copies ran while one was open for 2% of the time, Pallas kernels for 4%

profile of v1, /device:TPU:0, one launch (start us, length us, event | category | flops | bytes accessed | tf_op | source)
XLA Modules:
  0.0 59.9 jit_solution(7111896021963056430)
XLA Ops:
  0.0 0.1 pad_add_fusion.where_ref
  0.1 0.0 copy-start.1
  0.1 1.0 %copy-done.1 = bf16[1,1,4,4,128,128]{5,4,3,2,1,0:T(8,128)(2,1)S(1)} copy-done((bf16[1,1,4,4,128,128]{5,4,3,2,1,0:T(8,128)(2,1)S(1)}, bf16[1,1,4,4,128,128]{5,4,3,2,1,0:T(8,128)(2,1)}, u32[]{:S(2)}) %copy-start.1) | copy-done | bytes 524312
  1.1 0.0 copy-start.3
  1.1 0.7 %copy-done.3 = s32[1,1,4,4]{3,2,1,0:T(4,128)S(1)} copy-done((s32[1,1,4,4]{3,2,1,0:T(4,128)S(1)}, s32[1,1,4,4]{3,2,1,0:T(4,128)}, u32[]{:S(2)}) %copy-start.3) | copy-done | bytes 88
  1.8 0.0 copy-start.4
  1.8 0.7 %copy-done.4 = s32[1,1,4]{2,1,0:T(1,128)S(1)} copy-done((s32[1,1,4]{2,1,0:T(1,128)S(1)}, s32[1,1,4]{2,1,0:T(1,128)}, u32[]{:S(2)}) %copy-start.4) | copy-done | bytes 40
  2.5 0.8 %shard_map.55.refs_0_ = bf16[512,512]{1,0:T(8,128)(2,1)S(1)} custom-call(s32[2]{0:T(128)S(1)} %pad_add_fusion.where_ref, s32[4,4]{1,0:T(4,128)S(1)} %bitcast.25, s32[4]{0:T(128)S(1)} %bitcast.26, bf16[4,4,128,128]{3,2,1,0:T(8,128)(2,1)S(1)} %bitcast.24), custom_call_target="tpu_custom_call" | custom-call | bytes 524376 | tf_op jit(solution)/shard_map/pallas_call | solution.py:23
  3.3 3.0 %collective-permute-start.1 = (bf16[512,512]{1,0:T(8,128)(2,1)S(1)}, bf16[512,512]{1,0:T(8,128)(2,1)S(1)}, u32[]{:S(2)}, u32[]{:S(2)}) collective-permute-start(bf16[512,512]{1,0:T(8,128)(2,1)S(1)} %shard_map.55.refs_0_), channel_id=1, source_target_pairs={{0,2},{1,3},{2,0},{3,1},{4,6},{5,7},{6,4},{7,5},{8,10},{9,11},{10,... | collective-permute-start | bytes 1572872 | tf_op jit(solution)/shard_map/ppermute | solution.py:16
  6.3 0.0 collective-permute-start
  6.3 11.9 %collective-permute-done.1.refs_2_ = bf16[512,512]{1,0:T(8,128)(2,1)S(1)} collective-permute-done((bf16[512,512]{1,0:T(8,128)(2,1)S(1)}, bf16[512,512]{1,0:T(8,128)(2,1)S(1)}, u32[]{:S(2)}, u32[]{:S(2)}) %collective-permute-start.1) | collective-permute-done | bytes 524320 | tf_op jit(solution)/shard_map/ppermute | solution.py:16
  18.2 0.0 collective-permute-start.2
  18.2 0.9 %constant_dynamic-slice_fusion.4 = (bf16[128,256]{1,0:T(8,128)(2,1)S(1)}, bf16[1,128,256]{2,1,0:T(8,128)(2,1)S(1)}) fusion(bf16[128,512]{1,0:T(8,128)(2,1)} %feats_ref.1, s32[]{:T(128)S(6)} %select_n.48, s32[]{:T(128)S(6)} %select_n.47), kind=kLoop, calls=%fused_computation.27 | loop fusion | bytes 262152 | tf_op jit(solution)/shard_map/dynamic_slice | solution.py:131
  19.1 0.6 collective-permute-start.3
  19.7 0.9 %collective-permute-done.3 = bf16[128,256]{1,0:T(8,128)(2,1)S(1)} collective-permute-done((bf16[128,256]{1,0:T(8,128)(2,1)S(1)}, bf16[128,256]{1,0:T(8,128)(2,1)S(1)}, u32[]{:S(2)}, u32[]{:S(2)}) %collective-permute-start.3) | collective-permute-done | bytes 65568 | tf_op jit(solution)/shard_map/ppermute | solution.py:16
  20.6 1.8 %collective-permute-start.4 = (bf16[2,128,128]{2,1,0:T(8,128)(2,1)S(1)}, bf16[2,128,128]{2,1,0:T(8,128)(2,1)S(1)}, u32[]{:S(2)}, u32[]{:S(2)}) collective-permute-start(bf16[2,128,128]{2,1,0:T(8,128)(2,1)S(1)} %get-tuple-element.13), channel_id=1, source_target_pairs={{0,2},{1,3},{2,0},{3,1},{4,6},{5,7},{6,4},{7,5},{8,10},{9,11},{10,... | collective-permute-start | bytes 196616 | tf_op jit(solution)/shard_map/ppermute | solution.py:16
  22.4 1.6 %collective-permute-start.5 = (bf16[2,128,128]{2,1,0:T(8,128)(2,1)S(1)}, bf16[2,128,128]{2,1,0:T(8,128)(2,1)S(1)}, u32[]{:S(2)}, u32[]{:S(2)}) collective-permute-start(bf16[2,128,128]{2,1,0:T(8,128)(2,1)S(1)} %get-tuple-element.14.refs_4_.refs_8_), channel_id=1, source_target_pairs={{0,4},{4,0},{8,12},{12,8},{1,5},{5,1},{9,13},{13,9},{2,6},{6,2},{1... | collective-permute-start | bytes 196616 | tf_op jit(solution)/shard_map/ppermute | solution.py:16
  24.0 2.6 %collective-permute-start.7 = (bf16[2,128,128]{2,1,0:T(8,128)(2,1)S(1)}, bf16[2,128,128]{2,1,0:T(8,128)(2,1)S(1)}, u32[]{:S(2)}, u32[]{:S(2)}) collective-permute-start(bf16[2,128,128]{2,1,0:T(8,128)(2,1)S(1)} %get-tuple-element.14.refs_4_.refs_8_), channel_id=1, source_target_pairs={{0,8},{4,12},{8,0},{12,4},{1,9},{5,13},{9,1},{13,5},{2,10},{6,14},... | collective-permute-start | bytes 196616 | tf_op jit(solution)/shard_map/ppermute | solution.py:16
  26.6 0.0 collective-permute-done.4.refs_5_.refs_9_
  26.6 2.3 %collective-permute-start.9 = (bf16[2,128,128]{2,1,0:T(8,128)(2,1)S(1)}, bf16[2,128,128]{2,1,0:T(8,128)(2,1)S(1)}, u32[]{:S(2)}, u32[]{:S(2)}) collective-permute-start(bf16[2,128,128]{2,1,0:T(8,128)(2,1)S(1)} %get-tuple-element.14.refs_4_.refs_8_), channel_id=1, source_target_pairs={{0,12},{4,8},{8,4},{12,0},{1,13},{5,9},{9,5},{13,1},{2,14},{6,10},... | collective-permute-start | bytes 196616 | tf_op jit(solution)/shard_map/ppermute | solution.py:16
  28.9 0.0 collective-permute-done.5.refs_6_
  28.9 2.1 %collective-permute-start.10 = (bf16[2,128,128]{2,1,0:T(8,128)(2,1)S(1)}, bf16[2,128,128]{2,1,0:T(8,128)(2,1)S(1)}, u32[]{:S(2)}, u32[]{:S(2)}) collective-permute-start(bf16[2,128,128]{2,1,0:T(8,128)(2,1)S(1)} %collective-permute-done.4.refs_5_.refs_9_), channel_id=1, source_target_pairs={{0,12},{4,8},{8,4},{12,0},{1,13},{5,9},{9,5},{13,1},{2,14},{6,10},... | collective-permute-start | bytes 196616 | tf_op jit(solution)/shard_map/ppermute | solution.py:16
  31.0 0.5 collective-permute-done.7.refs_8_
  31.5 0.0 collective-permute-start.6
  31.5 1.5 %collective-permute-done.9.refs_10_ = bf16[2,128,128]{2,1,0:T(8,128)(2,1)S(1)} collective-permute-done((bf16[2,128,128]{2,1,0:T(8,128)(2,1)S(1)}, bf16[2,128,128]{2,1,0:T(8,128)(2,1)S(1)}, u32[]{:S(2)}, u32[]{:S(2)}) %collective-permute-start.9) | collective-permute-done | bytes 65568 | tf_op jit(solution)/shard_map/ppermute | solution.py:16
  33.0 3.9 %collective-permute-start.8 = (bf16[2,128,128]{2,1,0:T(8,128)(2,1)S(1)}, bf16[2,128,128]{2,1,0:T(8,128)(2,1)S(1)}, u32[]{:S(2)}, u32[]{:S(2)}) collective-permute-start(bf16[2,128,128]{2,1,0:T(8,128)(2,1)S(1)} %collective-permute-done.4.refs_5_.refs_9_), channel_id=1, source_target_pairs={{0,8},{4,12},{8,0},{12,4},{1,9},{5,13},{9,1},{13,5},{2,10},{6,14},... | collective-permute-start | bytes 196616 | tf_op jit(solution)/shard_map/ppermute | solution.py:16
  36.9 0.0 collective-permute-done.10.refs_11_
  36.9 0.0 collective-permute-done.6.refs_7_
  36.9 2.9 %collective-permute-done.8.refs_9_ = bf16[2,128,128]{2,1,0:T(8,128)(2,1)S(1)} collective-permute-done((bf16[2,128,128]{2,1,0:T(8,128)(2,1)S(1)}, bf16[2,128,128]{2,1,0:T(8,128)(2,1)S(1)}, u32[]{:S(2)}, u32[]{:S(2)}) %collective-permute-start.8) | collective-permute-done | bytes 65568 | tf_op jit(solution)/shard_map/ppermute | solution.py:16
  39.8 0.0 collective-permute-done.refs_1_
  39.8 0.0 collective-permute-done.2.refs_3_
  39.8 0.7 %shard_map.56.refs_4_ = bf16[512,128]{1,0:T(8,128)(2,1)S(1)} custom-call(bf16[512,512]{1,0:T(8,128)(2,1)S(1)} %shard_map.55.refs_0_, bf16[512,512]{1,0:T(8,128)(2,1)S(1)} %collective-permute-done.refs_1_, bf16[512,512]{1,0:T(8,128)(2,1)S(1)} %collective-permute-done.1.refs_2_, bf16[512,512]{1,0:T(8,128)(2,1)S(1)} %collective-permute-done.2.refs_3_, ...), custom_call_target="tpu_custom_call" | custom-call | flops 268435456 | bytes 2621440 | tf_op jit(solution)/shard_map/pallas_call | solution.py:23
  40.5 0.4 collective-permute-start.13
  40.9 2.5 %collective-permute-start.14 = (bf16[512,128]{1,0:T(8,128)(2,1)S(1)}, bf16[512,128]{1,0:T(8,128)(2,1)S(1)}, u32[]{:S(2)}, u32[]{:S(2)}) collective-permute-start(bf16[512,128]{1,0:T(8,128)(2,1)S(1)} %shard_map.56.refs_4_), channel_id=1, source_target_pairs={{0,8},{4,12},{8,0},{12,4},{1,9},{5,13},{9,1},{13,5},{2,10},{6,14},... | collective-permute-start | bytes 393224 | tf_op jit(solution)/shard_map/ppermute | solution.py:16
  43.4 1.6 %collective-permute-start.15 = (bf16[512,128]{1,0:T(8,128)(2,1)S(1)}, bf16[512,128]{1,0:T(8,128)(2,1)S(1)}, u32[]{:S(2)}, u32[]{:S(2)}) collective-permute-start(bf16[512,128]{1,0:T(8,128)(2,1)S(1)} %shard_map.56.refs_4_), channel_id=1, source_target_pairs={{0,12},{4,8},{8,4},{12,0},{1,13},{5,9},{9,5},{13,1},{2,14},{6,10},... | collective-permute-start | bytes 393224 | tf_op jit(solution)/shard_map/ppermute | solution.py:16
  45.0 0.0 copy-start
  45.0 0.0 copy-start.2
  45.0 0.3 collective-permute-start.11
  45.4 2.2 %collective-permute-done.13.refs_5_ = bf16[512,128]{1,0:T(8,128)(2,1)S(1)} collective-permute-done((bf16[512,128]{1,0:T(8,128)(2,1)S(1)}, bf16[512,128]{1,0:T(8,128)(2,1)S(1)}, u32[]{:S(2)}, u32[]{:S(2)}) %collective-permute-start.13) | collective-permute-done | bytes 131104 | tf_op jit(solution)/shard_map/ppermute | solution.py:16
  47.6 3.9 %collective-permute-done.14.refs_6_ = bf16[512,128]{1,0:T(8,128)(2,1)S(1)} collective-permute-done((bf16[512,128]{1,0:T(8,128)(2,1)S(1)}, bf16[512,128]{1,0:T(8,128)(2,1)S(1)}, u32[]{:S(2)}, u32[]{:S(2)}) %collective-permute-start.14) | collective-permute-done | bytes 131104 | tf_op jit(solution)/shard_map/ppermute | solution.py:16
  51.5 0.0 collective-permute-done.15.refs_7_
  51.5 1.3 %shard_map.58 = bf16[512,128]{1,0:T(8,128)(2,1)S(1)} custom-call(s32[2]{0:T(128)S(1)} %pad_add_fusion.where_ref, bf16[512,512]{1,0:T(8,128)(2,1)S(1)} %shard_map.55.refs_0_, bf16[512,512]{1,0:T(8,128)(2,1)S(1)} %collective-permute-done.refs_1_, bf16[512,512]{1,0:T(8,128)(2,1)S(1)} %collective-permute-done.1.refs_2_, ...), custom_call_target="tpu_custom_call" | custom-call | flops 268435456 | bytes 2752520 | tf_op jit(solution)/shard_map/pallas_call | solution.py:23
  52.8 0.6 collective-permute-start.16
  53.4 0.0 collective-permute-done.11
  53.4 0.1 collective-permute-start.12
  53.5 3.6 %collective-permute-done.16 = bf16[256,128]{1,0:T(8,128)(2,1)S(1)} collective-permute-done((bf16[256,128]{1,0:T(8,128)(2,1)S(1)}, bf16[256,128]{1,0:T(8,128)(2,1)S(1)}, u32[]{:S(2)}, u32[]{:S(2)}) %collective-permute-start.16) | collective-permute-done | bytes 65568 | tf_op jit(solution)/shard_map/ppermute | solution.py:16
  57.1 0.1 collective-permute-start.17
  57.2 0.0 collective-permute-done.12.far_ref
  57.2 0.0 copy-done
  57.2 0.0 copy-done.2
  57.2 0.9 %shard_map.57.early_ref = f32[128,512]{1,0:T(8,128)S(1)} custom-call(s32[2]{0:T(128)S(1)} %pad_add_fusion.where_ref, bf16[128,512]{1,0:T(8,128)(2,1)S(1)} %copy-done.2, bf16[2,128,128]{2,1,0:T(8,128)(2,1)S(1)} %get-tuple-element.10.near_ref, bf16[2,128,128]{2,1,0:T(8,128)(2,1)S(1)} %collective-permute-done.12.far_ref, bf16[3,512,512]{2,1,0:T(8,128)(2,1)S(1)} %copy-done), custom_call_target="tpu_custom_call" | custom-call | bytes 1835016 | tf_op jit(solution)/shard_map/pallas_call | solution.py:23
  58.2 0.3 collective-permute-done.17.far_ref
  58.5 1.5 %shard_map.59 = bf16[128,512]{1,0:T(8,128)(2,1)} custom-call(s32[2]{0:T(128)S(1)} %pad_add_fusion.where_ref, f32[128,512]{1,0:T(8,128)S(1)} %shard_map.57.early_ref, bf16[2,128,128]{2,1,0:T(8,128)(2,1)S(1)} %get-tuple-element.6.near_ref, bf16[2,128,128]{2,1,0:T(8,128)(2,1)S(1)} %collective-permute-done.17.far_ref, bf16[3,512,512]{2,1,0:T(8,128)(2,1)S(1)} %copy-done), custom_call_target="tpu_custom_call" | custom-call | bytes 1966088 | tf_op jit(solution)/shard_map/pallas_call | solution.py:23
  (5 shorter events, 0.1 us)
Async XLA Ops:
  0.1 1.0 %copy-start.1 = (bf16[1,1,4,4,128,128]{5,4,3,2,1,0:T(8,128)(2,1)S(1)}, bf16[1,1,4,4,128,128]{5,4,3,2,1,0:T(8,128)(2,1)}, u32[]{:S(2)}) copy-start(bf16[1,1,4,4,128,128]{5,4,3,2,1,0:T(8,128)(2,1)} %param.7) | copy-start | bytes 1572868
  1.1 0.7 %copy-start.3 = (s32[1,1,4,4]{3,2,1,0:T(4,128)S(1)}, s32[1,1,4,4]{3,2,1,0:T(4,128)}, u32[]{:S(2)}) copy-start(s32[1,1,4,4]{3,2,1,0:T(4,128)} %param.8) | copy-start | bytes 196
  1.8 0.7 %copy-start.4 = (s32[1,1,4]{2,1,0:T(1,128)S(1)}, s32[1,1,4]{2,1,0:T(1,128)}, u32[]{:S(2)}) copy-start(s32[1,1,4]{2,1,0:T(1,128)} %param.9) | copy-start | bytes 52
  3.3 14.9 %collective-permute-start.1 = (bf16[512,512]{1,0:T(8,128)(2,1)S(1)}, bf16[512,512]{1,0:T(8,128)(2,1)S(1)}, u32[]{:S(2)}, u32[]{:S(2)}) collective-permute-start(bf16[512,512]{1,0:T(8,128)(2,1)S(1)} %shard_map.55.refs_0_), channel_id=1, source_target_pairs={{0,2},{1,3},{2,0},{3,1},{4,6},{5,7},{6,4},{7,5},{8,10},{9,11},{10,... | collective-permute-start | bytes 1572872 | tf_op jit(solution)/shard_map/ppermute | solution.py:16
  6.3 33.5 %collective-permute-start = (bf16[512,512]{1,0:T(8,128)(2,1)S(1)}, bf16[512,512]{1,0:T(8,128)(2,1)S(1)}, u32[]{:S(2)}, u32[]{:S(2)}) collective-permute-start(bf16[512,512]{1,0:T(8,128)(2,1)S(1)} %shard_map.55.refs_0_), channel_id=1, source_target_pairs={{0,1},{1,0},{2,3},{3,2},{4,5},{5,4},{6,7},{7,6},{8,9},{9,8},{10,11... | collective-permute-start | bytes 1572872 | tf_op jit(solution)/shard_map/ppermute | solution.py:16
  18.2 21.6 %collective-permute-start.2 = (bf16[512,512]{1,0:T(8,128)(2,1)S(1)}, bf16[512,512]{1,0:T(8,128)(2,1)S(1)}, u32[]{:S(2)}, u32[]{:S(2)}) collective-permute-start(bf16[512,512]{1,0:T(8,128)(2,1)S(1)} %collective-permute-done.1.refs_2_), channel_id=1, source_target_pairs={{0,1},{1,0},{2,3},{3,2},{4,5},{5,4},{6,7},{7,6},{8,9},{9,8},{10,11... | collective-permute-start | bytes 1572872 | tf_op jit(solution)/shard_map/ppermute | solution.py:16
  19.1 1.5 %collective-permute-start.3 = (bf16[128,256]{1,0:T(8,128)(2,1)S(1)}, bf16[128,256]{1,0:T(8,128)(2,1)S(1)}, u32[]{:S(2)}, u32[]{:S(2)}) collective-permute-start(bf16[128,256]{1,0:T(8,128)(2,1)S(1)} %get-tuple-element.15), channel_id=1, source_target_pairs={{0,1},{1,0},{2,3},{3,2},{4,5},{5,4},{6,7},{7,6},{8,9},{9,8},{10,11... | collective-permute-start | bytes 196616 | tf_op jit(solution)/shard_map/ppermute | solution.py:16
  20.6 6.0 %collective-permute-start.4 = (bf16[2,128,128]{2,1,0:T(8,128)(2,1)S(1)}, bf16[2,128,128]{2,1,0:T(8,128)(2,1)S(1)}, u32[]{:S(2)}, u32[]{:S(2)}) collective-permute-start(bf16[2,128,128]{2,1,0:T(8,128)(2,1)S(1)} %get-tuple-element.13), channel_id=1, source_target_pairs={{0,2},{1,3},{2,0},{3,1},{4,6},{5,7},{6,4},{7,5},{8,10},{9,11},{10,... | collective-permute-start | bytes 196616 | tf_op jit(solution)/shard_map/ppermute | solution.py:16
  22.4 6.5 %collective-permute-start.5 = (bf16[2,128,128]{2,1,0:T(8,128)(2,1)S(1)}, bf16[2,128,128]{2,1,0:T(8,128)(2,1)S(1)}, u32[]{:S(2)}, u32[]{:S(2)}) collective-permute-start(bf16[2,128,128]{2,1,0:T(8,128)(2,1)S(1)} %get-tuple-element.14.refs_4_.refs_8_), channel_id=1, source_target_pairs={{0,4},{4,0},{8,12},{12,8},{1,5},{5,1},{9,13},{13,9},{2,6},{6,2},{1... | collective-permute-start | bytes 196616 | tf_op jit(solution)/shard_map/ppermute | solution.py:16
  24.0 7.5 %collective-permute-start.7 = (bf16[2,128,128]{2,1,0:T(8,128)(2,1)S(1)}, bf16[2,128,128]{2,1,0:T(8,128)(2,1)S(1)}, u32[]{:S(2)}, u32[]{:S(2)}) collective-permute-start(bf16[2,128,128]{2,1,0:T(8,128)(2,1)S(1)} %get-tuple-element.14.refs_4_.refs_8_), channel_id=1, source_target_pairs={{0,8},{4,12},{8,0},{12,4},{1,9},{5,13},{9,1},{13,5},{2,10},{6,14},... | collective-permute-start | bytes 196616 | tf_op jit(solution)/shard_map/ppermute | solution.py:16
  26.6 6.4 %collective-permute-start.9 = (bf16[2,128,128]{2,1,0:T(8,128)(2,1)S(1)}, bf16[2,128,128]{2,1,0:T(8,128)(2,1)S(1)}, u32[]{:S(2)}, u32[]{:S(2)}) collective-permute-start(bf16[2,128,128]{2,1,0:T(8,128)(2,1)S(1)} %get-tuple-element.14.refs_4_.refs_8_), channel_id=1, source_target_pairs={{0,12},{4,8},{8,4},{12,0},{1,13},{5,9},{9,5},{13,1},{2,14},{6,10},... | collective-permute-start | bytes 196616 | tf_op jit(solution)/shard_map/ppermute | solution.py:16
  28.9 8.0 %collective-permute-start.10 = (bf16[2,128,128]{2,1,0:T(8,128)(2,1)S(1)}, bf16[2,128,128]{2,1,0:T(8,128)(2,1)S(1)}, u32[]{:S(2)}, u32[]{:S(2)}) collective-permute-start(bf16[2,128,128]{2,1,0:T(8,128)(2,1)S(1)} %collective-permute-done.4.refs_5_.refs_9_), channel_id=1, source_target_pairs={{0,12},{4,8},{8,4},{12,0},{1,13},{5,9},{9,5},{13,1},{2,14},{6,10},... | collective-permute-start | bytes 196616 | tf_op jit(solution)/shard_map/ppermute | solution.py:16
  31.5 5.4 %collective-permute-start.6 = (bf16[2,128,128]{2,1,0:T(8,128)(2,1)S(1)}, bf16[2,128,128]{2,1,0:T(8,128)(2,1)S(1)}, u32[]{:S(2)}, u32[]{:S(2)}) collective-permute-start(bf16[2,128,128]{2,1,0:T(8,128)(2,1)S(1)} %collective-permute-done.4.refs_5_.refs_9_), channel_id=1, source_target_pairs={{0,4},{4,0},{8,12},{12,8},{1,5},{5,1},{9,13},{13,9},{2,6},{6,2},{1... | collective-permute-start | bytes 196616 | tf_op jit(solution)/shard_map/ppermute | solution.py:16
  33.0 6.8 %collective-permute-start.8 = (bf16[2,128,128]{2,1,0:T(8,128)(2,1)S(1)}, bf16[2,128,128]{2,1,0:T(8,128)(2,1)S(1)}, u32[]{:S(2)}, u32[]{:S(2)}) collective-permute-start(bf16[2,128,128]{2,1,0:T(8,128)(2,1)S(1)} %collective-permute-done.4.refs_5_.refs_9_), channel_id=1, source_target_pairs={{0,8},{4,12},{8,0},{12,4},{1,9},{5,13},{9,1},{13,5},{2,10},{6,14},... | collective-permute-start | bytes 196616 | tf_op jit(solution)/shard_map/ppermute | solution.py:16
  40.5 7.1 %collective-permute-start.13 = (bf16[512,128]{1,0:T(8,128)(2,1)S(1)}, bf16[512,128]{1,0:T(8,128)(2,1)S(1)}, u32[]{:S(2)}, u32[]{:S(2)}) collective-permute-start(bf16[512,128]{1,0:T(8,128)(2,1)S(1)} %shard_map.56.refs_4_), channel_id=1, source_target_pairs={{0,4},{4,0},{8,12},{12,8},{1,5},{5,1},{9,13},{13,9},{2,6},{6,2},{1... | collective-permute-start | bytes 393224 | tf_op jit(solution)/shard_map/ppermute | solution.py:16
  40.9 10.6 %collective-permute-start.14 = (bf16[512,128]{1,0:T(8,128)(2,1)S(1)}, bf16[512,128]{1,0:T(8,128)(2,1)S(1)}, u32[]{:S(2)}, u32[]{:S(2)}) collective-permute-start(bf16[512,128]{1,0:T(8,128)(2,1)S(1)} %shard_map.56.refs_4_), channel_id=1, source_target_pairs={{0,8},{4,12},{8,0},{12,4},{1,9},{5,13},{9,1},{13,5},{2,10},{6,14},... | collective-permute-start | bytes 393224 | tf_op jit(solution)/shard_map/ppermute | solution.py:16
  43.4 8.1 %collective-permute-start.15 = (bf16[512,128]{1,0:T(8,128)(2,1)S(1)}, bf16[512,128]{1,0:T(8,128)(2,1)S(1)}, u32[]{:S(2)}, u32[]{:S(2)}) collective-permute-start(bf16[512,128]{1,0:T(8,128)(2,1)S(1)} %shard_map.56.refs_4_), channel_id=1, source_target_pairs={{0,12},{4,8},{8,4},{12,0},{1,13},{5,9},{9,5},{13,1},{2,14},{6,10},... | collective-permute-start | bytes 393224 | tf_op jit(solution)/shard_map/ppermute | solution.py:16
  45.0 12.2 %copy-start = (bf16[3,512,512]{2,1,0:T(8,128)(2,1)S(1)}, bf16[3,512,512]{2,1,0:T(8,128)(2,1)}, u32[]{:S(2)}) copy-start(bf16[3,512,512]{2,1,0:T(8,128)(2,1)} %weight_ref.3) | copy-start | bytes 4718596
  45.0 12.2 %copy-start.2 = (bf16[128,512]{1,0:T(8,128)(2,1)S(1)}, bf16[128,512]{1,0:T(8,128)(2,1)}, u32[]{:S(2)}) copy-start(bf16[128,512]{1,0:T(8,128)(2,1)} %feats_ref.1) | copy-start | bytes 393220
  45.0 8.4 %collective-permute-start.11 = (bf16[256,128]{1,0:T(8,128)(2,1)S(1)}, bf16[256,128]{1,0:T(8,128)(2,1)S(1)}, u32[]{:S(2)}, u32[]{:S(2)}) collective-permute-start(bf16[256,128]{1,0:T(8,128)(2,1)S(1)} %get-tuple-element.11), channel_id=1, source_target_pairs={{0,2},{1,3},{2,0},{3,1},{4,6},{5,7},{6,4},{7,5},{8,10},{9,11},{10,... | collective-permute-start | bytes 196616 | tf_op jit(solution)/shard_map/ppermute | solution.py:16
  52.8 4.3 %collective-permute-start.16 = (bf16[256,128]{1,0:T(8,128)(2,1)S(1)}, bf16[256,128]{1,0:T(8,128)(2,1)S(1)}, u32[]{:S(2)}, u32[]{:S(2)}) collective-permute-start(bf16[256,128]{1,0:T(8,128)(2,1)S(1)} %get-tuple-element.7), channel_id=1, source_target_pairs={{0,2},{1,3},{2,0},{3,1},{4,6},{5,7},{6,4},{7,5},{8,10},{9,11},{10,... | collective-permute-start | bytes 196616 | tf_op jit(solution)/shard_map/ppermute | solution.py:16
  53.4 3.8 %collective-permute-start.12 = (bf16[2,128,128]{2,1,0:T(8,128)(2,1)S(1)}, bf16[2,128,128]{2,1,0:T(8,128)(2,1)S(1)}, u32[]{:S(2)}, u32[]{:S(2)}) collective-permute-start(bf16[2,128,128]{2,1,0:T(8,128)(2,1)S(1)} %get-tuple-element.9), channel_id=1, source_target_pairs={{0,1},{1,0},{2,3},{3,2},{4,5},{5,4},{6,7},{7,6},{8,9},{9,8},{10,11... | collective-permute-start | bytes 196616 | tf_op jit(solution)/shard_map/ppermute | solution.py:16
  57.1 1.3 %collective-permute-start.17 = (bf16[2,128,128]{2,1,0:T(8,128)(2,1)S(1)}, bf16[2,128,128]{2,1,0:T(8,128)(2,1)S(1)}, u32[]{:S(2)}, u32[]{:S(2)}) collective-permute-start(bf16[2,128,128]{2,1,0:T(8,128)(2,1)S(1)} %get-tuple-element.5), channel_id=1, source_target_pairs={{0,1},{1,0},{2,3},{3,2},{4,5},{5,4},{6,7},{7,6},{8,9},{9,8},{10,11... | collective-permute-start | bytes 196616 | tf_op jit(solution)/shard_map/ppermute | solution.py:16

commit v2 on v1

v2 whole, which is shorter than its diff:
```python
import functools

import jax
import jax.numpy as jnp
from jax import lax
from jax.experimental import pallas as pl
from jax.experimental.pallas import tpu as pltpu
from jax.sharding import PartitionSpec as P

BF16 = jnp.bfloat16
F32 = jnp.float32
MIB = 1 << 20


def swap(array, axis, mask):
    peers = lax.axis_size(axis)
    return lax.ppermute(array, axis, [(i, i ^ mask) for i in range(peers)])


def near_by(array):
    if array.size * array.dtype.itemsize > MIB:
        return array
    return pltpu.with_memory_space_constraint(array, pltpu.VMEM)


def after(values, *earlier):
    left = pl.BlockSpec(memory_space=pl.ANY)
    return pl.pallas_call(
        lambda *refs: None,
        out_shape=[jax.ShapeDtypeStruct(v.shape, v.dtype) for v in values],
        in_specs=[left] * (len(values) + len(earlier)),
        out_specs=[left] * len(values),
        input_output_aliases={i: i for i in range(len(values))},
        compiler_params=pltpu.CompilerParams(vmem_limit_bytes=MIB),
    )(*values, *[near_by(e) for e in earlier])


def call(kernel, out_shapes, *args, scalars=0, scratch=(), vmem=4 * MIB, flops=0, hbm=0, earlier=()):
    smem = pl.BlockSpec(memory_space=pltpu.SMEM)
    whole = pl.BlockSpec(memory_space=pltpu.VMEM)
    left = pl.BlockSpec(memory_space=pl.ANY)
    home = pl.BlockSpec(memory_space=pltpu.HBM)
    size = sum(a.size * a.dtype.itemsize for a in args)
    first_whole = scalars + hbm
    n_args, n_all = len(args), len(args) + len(earlier)

    def body(*refs):
        kernel(*refs[:n_args], *refs[n_all:])

    return pl.pallas_call(
        body,
        out_shape=out_shapes,
        in_specs=[smem] * scalars + [home] * hbm + [whole] * (n_args - scalars - hbm) + [left] * len(earlier),
        out_specs=jax.tree.map(lambda _: whole, out_shapes),
        scratch_shapes=list(scratch),
        compiler_params=pltpu.CompilerParams(vmem_limit_bytes=vmem),
        cost_estimate=pl.CostEstimate(flops=flops, bytes_accessed=size, transcendentals=0),
    )(*args[:first_whole], *[near_by(a) for a in (*args[first_whole:], *earlier)])


def dense_kernel(where_ref, place_hbm, count_hbm, blocks_hbm, *refs):
    halves, (place_ref, count_ref, blocks_ref, sems) = refs[:-4], refs[-4:]
    n_blk, cap, tile = blocks_ref.shape[2:5]
    copies = [
        pltpu.make_async_copy(blocks_hbm, blocks_ref, sems.at[0]),
        pltpu.make_async_copy(place_hbm, place_ref, sems.at[1]),
        pltpu.make_async_copy(count_hbm, count_ref, sems.at[2]),
    ]
    for copy in copies:
        copy.start()
    for half in halves:
        half[...] = jnp.zeros_like(half)
    own = where_ref[0]
    for copy in copies:
        copy.wait()
    each = n_blk // len(halves)
    for m in range(n_blk):
        j = own ^ m
        out_ref, at = halves[m // each], (m % each) * tile
        for slot in range(cap):

            @pl.when(slot < count_ref[0, 0, j])
            def _():
                row = pl.multiple_of(place_ref[0, 0, j, slot] * tile, tile)
                out_ref[pl.ds(row, tile), at : at + tile] = blocks_ref[0, 0, j, slot]


def dot(a, b):
    return jnp.dot(a, b, preferred_element_type=F32)


def apply_lanes(lanes, n_blk, tile, rows_of):
    total = None
    each = n_blk // len(lanes[0])
    for m in range(n_blk):
        at = (m % each) * tile
        left = jnp.concatenate([halves[m // each][:, at : at + tile] for halves in lanes], axis=1)
        right = jnp.concatenate([rows_of(m, k) for k in range(len(lanes))], axis=0)
        part = dot(left, right)
        total = part if total is None else total + part
    return total


def paired(refs, n):
    return [refs[i : i + n] for i in range(0, len(refs), n)]


def part_kernel(n_blk, tile, masks, *refs):
    n = len(masks)
    lanes, pieces, more, out_ref = paired(refs[:n], 1), refs[n : n + n_blk], refs[n + n_blk : -1], refs[-1]
    total = apply_lanes(lanes, n_blk, tile, lambda m, i: pieces[m][masks[i] // 2, masks[i] % 2])
    if more:
        total = total + more[0][...]
    out_ref[...] = total.astype(out_ref.dtype)


def second_kernel(n_blk, n_half, n_rep, tile, where_ref, *refs):
    lanes, refs = paired(refs[: n_rep * n_half], n_half), refs[n_rep * n_half :]
    firsts, feats, out_ref, total_ref = refs[:n_blk], refs[n_blk], refs[n_blk + 1], refs[n_blk + 2]
    rep = where_ref[1]

    def rows(k):
        return pl.ds(pl.multiple_of((rep ^ k) * tile, tile), tile)

    total_ref[...] = apply_lanes(lanes, n_blk, tile, lambda m, k: firsts[m][rows(k), :])
    for k in range(n_rep):
        out_ref[rows(k), :] = (2.0 * total_ref[rows(k), :] - feats[k // 2, k % 2].astype(F32)).astype(BF16)


def weigh(rep, n_rep, near_ref, far_ref, weight_ref, order):
    chips, _, width = near_ref.shape
    total = None
    for k in range(n_rep):
        lane = rep ^ k
        at = (lane % 2) * chips + lane // 2
        rows = pl.ds(pl.multiple_of(at * width, width), width)
        piece = far_ref[k // 2] if k % 2 else near_ref[k // 2]
        part = dot(piece, weight_ref[order, rows, :])
        total = part if total is None else total + part
    return total


def early_kernel(n_rep, where_ref, feats_ref, near_ref, far_ref, weight_ref, out_ref):
    total = dot(feats_ref[...], weight_ref[0])
    out_ref[...] = total + weigh(where_ref[1], n_rep, near_ref, far_ref, weight_ref, 1)


def last_kernel(n_rep, where_ref, early_ref, near_ref, far_ref, weight_ref, out_ref):
    total = early_ref[...] + weigh(where_ref[1], n_rep, near_ref, far_ref, weight_ref, 2)
    out_ref[...] = total.astype(BF16)


def to_owners(parts, rep, n_rep):
    c = rep % 2
    got = jnp.stack([swap(part, "rep", 2 * i) if i else part for i, part in enumerate(parts)])
    got = got.reshape(got.shape[0], 2, -1, got.shape[2])
    near = lax.dynamic_index_in_dim(got, c, 1, keepdims=False)
    far = swap(lax.dynamic_index_in_dim(got, 1 - c, 1, keepdims=False), "rep", 1)
    return near, far


def by_chip(strip, rep, n_rep):
    size = strip.shape[0] * 2 // n_rep
    return [lax.dynamic_slice_in_dim(strip, ((rep // 2) ^ i) * size, size, 0) for i in range(n_rep // 2)]


def per_device(features, order_weights, laplacian_blocks, tile_place, tile_count):
    n_blk, n_rep = lax.axis_size("blk"), lax.axis_size("rep")
    blk, rep = lax.axis_index("blk"), lax.axis_index("rep")
    chips = n_rep // 2
    x, c = rep // 2, rep % 2
    tile, feat = features.shape
    strip = n_rep * tile
    width = feat // n_rep
    half = feat // 2
    n_half = 1
    where = jnp.stack([blk, rep]).astype(jnp.int32)
    lane_bytes = 2 * strip * n_blk * tile
    rows_bytes = 2 * strip * n_blk * max(width, 128)

    kept = lax.dynamic_slice_in_dim(features, c * half, half, 1)
    given = lax.dynamic_slice_in_dim(features, (1 - c) * half, half, 1)
    got = swap(given, "rep", 1)
    chip_rows = jnp.stack([kept, got])
    half_shape = jax.ShapeDtypeStruct((strip, n_blk // n_half * tile), BF16)
    dense = call(
        dense_kernel,
        half_shape,
        where,
        *(pltpu.with_memory_space_constraint(a, pltpu.HBM) for a in (tile_place, tile_count, laplacian_blocks)),
        scalars=1,
        hbm=3,
        vmem=3 * lane_bytes + 2 * MIB,
        scratch=[
            pltpu.SMEM(tile_place.shape, jnp.int32),
            pltpu.SMEM(tile_count.shape, jnp.int32),
            pltpu.VMEM(laplacian_blocks.shape, BF16),
            pltpu.SemaphoreType.DMA((3,)),
        ],
    )
    own_chip = [dense, swap(dense, "rep", 1)]

    pieces = []
    for i in range(chips):
        piece = lax.dynamic_slice_in_dim(chip_rows, (x ^ i) * width, width, 2)
        pieces.append(swap(piece, "rep", 2 * i) if i else piece)
    own_rows = jnp.stack(pieces)
    rows = [swap(own_rows, "blk", m) if m else own_rows for m in range(n_blk)]
    arrived = [swap(after([dense], pieces[i])[0], "rep", 2 * i) for i in range(1, chips)]
    tied = after([*rows[1:], *arrived])
    rows, arrived = [own_rows, *tied[: n_blk - 1]], tied[n_blk - 1 :]
    lanes = [*own_chip]
    for got in arrived:
        lanes += [got, swap(got, "rep", 1)]

    strip_shape = jax.ShapeDtypeStruct((strip, width), BF16)
    vmem = n_rep * lane_bytes + 2 * rows_bytes + 4 * MIB
    macs = 2 * strip * n_blk * strip * width
    soon = [0, 1, *range(2, n_rep, 2)]
    late = [*range(3, n_rep, 2)]
    part = call(
        functools.partial(part_kernel, n_blk, tile, soon), jax.ShapeDtypeStruct((strip, width), F32),
        *[lanes[k] for k in soon], *rows,
        vmem=vmem, flops=macs,
    )
    first = call(
        functools.partial(part_kernel, n_blk, tile, late), strip_shape,
        *[lanes[k] for k in late], *rows, part,
        vmem=vmem, flops=macs,
    )
    firsts = [swap(first, "blk", m) for m in range(1, n_blk)]
    tied = after([*firsts, *by_chip(first, rep, n_rep)])
    firsts, first_parts = [first, *tied[: n_blk - 1]], tied[n_blk - 1 :]
    early_near, early_far = to_owners(first_parts, rep, n_rep)
    early = call(
        functools.partial(early_kernel, n_rep),
        jax.ShapeDtypeStruct((tile, feat), F32),
        where, features, early_near, early_far, order_weights,
        scalars=1,
    )
    second = call(
        functools.partial(second_kernel, n_blk, n_half, n_rep, tile), strip_shape,
        where, *lanes, *firsts, own_rows,
        scalars=1, vmem=vmem, flops=macs,
        scratch=[pltpu.VMEM((strip, width), F32)],
    )
    near, far = to_owners(by_chip(second, rep, n_rep), rep, n_rep)
    return call(
        functools.partial(last_kernel, n_rep),
        jax.ShapeDtypeStruct((tile, feat), BF16),
        where, early, near, far, order_weights,
        scalars=1,
    )


def solution(mesh):
    in_specs = (
        P(("groups", "blk", "rep"), None),
        P(),
        P(("groups", "blk"), "rep", None, None, None, None),
        P(("groups", "blk"), "rep", None, None),
        P(("groups", "blk"), "rep", None),
    )
    out_specs = P(("groups", "blk", "rep"), None)
    return jax.shard_map(
        per_device, mesh=mesh, in_specs=in_specs, out_specs=out_specs, check_vma=False
    )
```

time: 60.2 us -> 48.2 us (0.80)
  starting transfers between devices: 23.4 us -> 16.5 us
  waiting for transfers between devices: 27.9 us -> 24 us
  local copies, waits for them, and re-layouts: 3.3 us -> 0.95 us
  Pallas kernels: 5.16 us -> 6.34 us
    ppermute x18 -> x15, starting transfers between devices: 23.4 us -> 16.5 us  [swap(): return lax.ppermute(array, axis, [(i, i ^ mask) for i in range(peers)])]
    ppermute x18 -> x15, waiting for transfers between devices: 27.9 us -> 24 us  [swap(): return lax.ppermute(array, axis, [(i, i ^ mask) for i in range(peers)])]
    unnamed x10 -> x5, local copies, waits for them, and re-layouts: 2.39 us -> 0.04 us
    pallas_call x5 -> x9, Pallas kernels: 5.16 us -> 6.34 us  [the longest x6 6.34 us: call(): pl.pallas_call(body, out_shape=out_shapes, in_specs=[smem] * scalars + [h...]
  transfers between devices with their start and end apart: 18 -> 15, of which waited for: 9 -> 10; matrix products, arithmetic and copies ran while one was open for 2% -> 0% of each run, Pallas kernels for 4% -> 9%
where the time goes in v2:
time: 48.2 us; the launch traced here: 48.1 us
  waiting for transfers between devices  24 us (50%)
  starting transfers between devices  16.5 us (34%)
  Pallas kernels  6.34 us (13%)
  local copies, waits for them, and re-layouts  0.95 us (2%)
    ppermute x15, waiting for transfers between devices, swap(): return lax.ppermute(array, axis, [(i, i ^ mask) for i in range(peers)])  24 us
    ppermute x15, starting transfers between devices, swap(): return lax.ppermute(array, axis, [(i, i ^ mask) for i in range(peers)])  16.5 us
    pallas_call x6, Pallas kernels, call(): pl.pallas_call(body, out_shape=out_shapes, in_specs=[smem] * scalars + [h...  6.34 us
  transfers between devices with their start and end apart: 15, of which 10 were waited for; matrix products, arithmetic and copies ran while one was open for 0% of the time, Pallas kernels for 9%

profile of v2, /device:TPU:0, one launch (start us, length us, event | category | flops | bytes accessed | tf_op | source)
XLA Modules:
  0.0 48.1 jit_solution(12323639734126568405)
XLA Ops:
  0.0 0.9 %constant_dynamic-slice_fusion.4 = (bf16[128,256]{1,0:T(8,128)(2,1)S(1)}, bf16[1,128,256]{2,1,0:T(8,128)(2,1)S(1)}) fusion(bf16[128,512]{1,0:T(8,128)(2,1)} %refs_1_.3, s32[]{:T(128)S(6)} %select_n.50, s32[]{:T(128)S(6)} %select_n.49), kind=kLoop, calls=%fused_computation.29 | loop fusion | bytes 262152 | tf_op jit(solution)/shard_map/dynamic_slice | solution.py:182
  0.9 0.5 %collective-permute-start = (bf16[128,256]{1,0:T(8,128)(2,1)S(1)}, bf16[128,256]{1,0:T(8,128)(2,1)S(1)}, u32[]{:S(2)}, u32[]{:S(2)}) collective-permute-start(bf16[128,256]{1,0:T(8,128)(2,1)S(1)} %get-tuple-element.33), channel_id=1, source_target_pairs={{0,1},{1,0},{2,3},{3,2},{4,5},{5,4},{6,7},{7,6},{8,9},{9,8},{10,11... | collective-permute-start | bytes 196616 | tf_op jit(solution)/shard_map/ppermute | solution.py:17
  1.4 0.9 %collective-permute-done = bf16[128,256]{1,0:T(8,128)(2,1)S(1)} collective-permute-done((bf16[128,256]{1,0:T(8,128)(2,1)S(1)}, bf16[128,256]{1,0:T(8,128)(2,1)S(1)}, u32[]{:S(2)}, u32[]{:S(2)}) %collective-permute-start) | collective-permute-done | bytes 65568 | tf_op jit(solution)/shard_map/ppermute | solution.py:17
  2.3 2.9 %collective-permute-start.1 = (bf16[2,128,128]{2,1,0:T(8,128)(2,1)S(1)}, bf16[2,128,128]{2,1,0:T(8,128)(2,1)S(1)}, u32[]{:S(2)}, u32[]{:S(2)}) collective-permute-start(bf16[2,128,128]{2,1,0:T(8,128)(2,1)S(1)} %get-tuple-element.32), channel_id=1, source_target_pairs={{0,2},{1,3},{2,0},{3,1},{4,6},{5,7},{6,4},{7,5},{8,10},{9,11},{10,... | collective-permute-start | bytes 196616 | tf_op jit(solution)/shard_map/ppermute | solution.py:17
  5.2 0.1 pad_add_fusion.refs_0_
  5.3 1.8 %shard_map.55.refs_0_.refs_1_ = bf16[512,512]{1,0:T(8,128)(2,1)S(1)} custom-call(s32[2]{0:T(128)S(1)} %pad_add_fusion.refs_0_, s32[1,1,4,4]{3,2,1,0:T(4,128)} %refs_1_.2, s32[1,1,4]{2,1,0:T(1,128)} %refs_2_.1, bf16[1,1,4,4,128,128]{5,4,3,2,1,0:T(8,128)(2,1)} %refs_3_.1), custom_call_target="tpu_custom_call" | custom-call | bytes 524376 | tf_op jit(solution)/shard_map/pallas_call | solution.py:50
  7.2 0.5 collective-permute-done.1.refs_1_
  7.7 1.9 %collective-permute-start.5 = (bf16[512,512]{1,0:T(8,128)(2,1)S(1)}, bf16[512,512]{1,0:T(8,128)(2,1)S(1)}, u32[]{:S(2)}, u32[]{:S(2)}) collective-permute-start(bf16[512,512]{1,0:T(8,128)(2,1)S(1)} %shard_map.56), channel_id=1, source_target_pairs={{0,2},{1,3},{2,0},{3,1},{4,6},{5,7},{6,4},{7,5},{8,10},{9,11},{10,... | collective-permute-start | bytes 1572872 | tf_op jit(solution)/shard_map/ppermute | solution.py:17
  9.5 3.7 %collective-permute-start.4 = (bf16[2,2,128,128]{3,2,1,0:T(8,128)(2,1)S(1)}, bf16[2,2,128,128]{3,2,1,0:T(8,128)(2,1)S(1)}, u32[]{:S(2)}, u32[]{:S(2)}) collective-permute-start(bf16[2,2,128,128]{3,2,1,0:T(8,128)(2,1)S(1)} %pad_maximum_fusion.refs_3_.refs_1_.refs_9_), channel_id=1, source_target_pairs={{0,12},{4,8},{8,4},{12,0},{1,13},{5,9},{9,5},{13,1},{2,14},{6,10},... | collective-permute-start | bytes 393224 | tf_op jit(solution)/shard_map/ppermute | solution.py:17
  13.2 0.0 collective-permute-start.3
  13.2 0.8 %collective-permute-start.2 = (bf16[2,2,128,128]{3,2,1,0:T(8,128)(2,1)S(1)}, bf16[2,2,128,128]{3,2,1,0:T(8,128)(2,1)S(1)}, u32[]{:S(2)}, u32[]{:S(2)}) collective-permute-start(bf16[2,2,128,128]{3,2,1,0:T(8,128)(2,1)S(1)} %pad_maximum_fusion.refs_3_.refs_1_.refs_9_), channel_id=1, source_target_pairs={{0,4},{4,0},{8,12},{12,8},{1,5},{5,1},{9,13},{13,9},{2,6},{6,2},{1... | collective-permute-start | bytes 393224 | tf_op jit(solution)/shard_map/ppermute | solution.py:17
  14.0 0.0 collective-permute-start.7
  14.0 3.7 %collective-permute-done.4.refs_2_ = bf16[2,2,128,128]{3,2,1,0:T(8,128)(2,1)S(1)} collective-permute-done((bf16[2,2,128,128]{3,2,1,0:T(8,128)(2,1)S(1)}, bf16[2,2,128,128]{3,2,1,0:T(8,128)(2,1)S(1)}, u32[]{:S(2)}, u32[]{:S(2)}) %collective-permute-start.4) | collective-permute-done | bytes 131104 | tf_op jit(solution)/shard_map/ppermute | solution.py:17
  17.7 5.5 %collective-permute-done.3.refs_1_ = bf16[2,2,128,128]{3,2,1,0:T(8,128)(2,1)S(1)} collective-permute-done((bf16[2,2,128,128]{3,2,1,0:T(8,128)(2,1)S(1)}, bf16[2,2,128,128]{3,2,1,0:T(8,128)(2,1)S(1)}, u32[]{:S(2)}, u32[]{:S(2)}) %collective-permute-start.3) | collective-permute-done | bytes 131104 | tf_op jit(solution)/shard_map/ppermute | solution.py:17
  23.2 0.0 collective-permute-done.2.refs_0_
  23.2 0.0 collective-permute-done.5.refs_3_
  23.2 0.1 collective-permute-start.6
  23.2 0.0 collective-permute-done.7.refs_1_.refs_2_
  23.2 0.6 %shard_map.58.refs_5_ = f32[512,128]{1,0:T(8,128)S(1)} custom-call(bf16[512,512]{1,0:T(8,128)(2,1)S(1)} %shard_map.55.refs_0_.refs_1_, bf16[512,512]{1,0:T(8,128)(2,1)S(1)} %collective-permute-done.7.refs_1_.refs_2_, bf16[512,512]{1,0:T(8,128)(2,1)S(1)} %get-tuple-element.14.refs_2_.refs_3_, ...), custom_call_target="tpu_custom_call" | custom-call | flops 268435456 | bytes 2097152 | tf_op jit(solution)/shard_map/pallas_call | solution.py:50
  23.8 1.3 %collective-permute-done.6.refs_0_.refs_4_ = bf16[512,512]{1,0:T(8,128)(2,1)S(1)} collective-permute-done((bf16[512,512]{1,0:T(8,128)(2,1)S(1)}, bf16[512,512]{1,0:T(8,128)(2,1)S(1)}, u32[]{:S(2)}, u32[]{:S(2)}) %collective-permute-start.6) | collective-permute-done | bytes 524320 | tf_op jit(solution)/shard_map/ppermute | solution.py:17
  25.1 0.3 shard_map.59.refs_5_
  25.4 2.5 %collective-permute-start.10 = (bf16[512,128]{1,0:T(8,128)(2,1)S(1)}, bf16[512,128]{1,0:T(8,128)(2,1)S(1)}, u32[]{:S(2)}, u32[]{:S(2)}) collective-permute-start(bf16[512,128]{1,0:T(8,128)(2,1)S(1)} %shard_map.59.refs_5_), channel_id=1, source_target_pairs={{0,12},{4,8},{8,4},{12,0},{1,13},{5,9},{9,5},{13,1},{2,14},{6,10},... | collective-permute-start | bytes 393224 | tf_op jit(solution)/shard_map/ppermute | solution.py:17
  28.0 0.0 collective-permute-start.9
  28.0 1.9 %collective-permute-start.8 = (bf16[512,128]{1,0:T(8,128)(2,1)S(1)}, bf16[512,128]{1,0:T(8,128)(2,1)S(1)}, u32[]{:S(2)}, u32[]{:S(2)}) collective-permute-start(bf16[512,128]{1,0:T(8,128)(2,1)S(1)} %shard_map.59.refs_5_), channel_id=1, source_target_pairs={{0,4},{4,0},{8,12},{12,8},{1,5},{5,1},{9,13},{13,9},{2,6},{6,2},{1... | collective-permute-start | bytes 393224 | tf_op jit(solution)/shard_map/ppermute | solution.py:17
  29.9 3.9 %collective-permute-done.10.refs_2_ = bf16[512,128]{1,0:T(8,128)(2,1)S(1)} collective-permute-done((bf16[512,128]{1,0:T(8,128)(2,1)S(1)}, bf16[512,128]{1,0:T(8,128)(2,1)S(1)}, u32[]{:S(2)}, u32[]{:S(2)}) %collective-permute-start.10) | collective-permute-done | bytes 131104 | tf_op jit(solution)/shard_map/ppermute | solution.py:17
  33.8 4.9 %collective-permute-done.9.refs_1_ = bf16[512,128]{1,0:T(8,128)(2,1)S(1)} collective-permute-done((bf16[512,128]{1,0:T(8,128)(2,1)S(1)}, bf16[512,128]{1,0:T(8,128)(2,1)S(1)}, u32[]{:S(2)}, u32[]{:S(2)}) %collective-permute-start.9) | collective-permute-done | bytes 131104 | tf_op jit(solution)/shard_map/ppermute | solution.py:17
  38.7 0.0 collective-permute-done.8.refs_0_
  38.7 0.9 %collective-permute-start.11 = (bf16[256,128]{1,0:T(8,128)(2,1)S(1)}, bf16[256,128]{1,0:T(8,128)(2,1)S(1)}, u32[]{:S(2)}, u32[]{:S(2)}) collective-permute-start(bf16[256,128]{1,0:T(8,128)(2,1)S(1)} %get-tuple-element.19), channel_id=1, source_target_pairs={{0,2},{1,3},{2,0},{3,1},{4,6},{5,7},{6,4},{7,5},{8,10},{9,11},{10,... | collective-permute-start | bytes 196616 | tf_op jit(solution)/shard_map/ppermute | solution.py:17
  39.6 0.0 copy-start
  39.6 0.0 copy-start.1
  39.6 1.3 %shard_map.62 = bf16[512,128]{1,0:T(8,128)(2,1)S(1)} custom-call(s32[2]{0:T(128)S(1)} %pad_add_fusion.refs_0_, bf16[512,512]{1,0:T(8,128)(2,1)S(1)} %shard_map.55.refs_0_.refs_1_, bf16[512,512]{1,0:T(8,128)(2,1)S(1)} %collective-permute-done.7.refs_1_.refs_2_, bf16[512,512]{1,0:T(8,128)(2,1)S(1)} %get-tuple-element.14.refs_2_.refs_3_, ...), custom_call_target="tpu_custom_call" | custom-call | flops 268435456 | bytes 2752520 | tf_op jit(solution)/shard_map/pallas_call | solution.py:50
  40.9 1.2 %collective-permute-start.13 = (bf16[256,128]{1,0:T(8,128)(2,1)S(1)}, bf16[256,128]{1,0:T(8,128)(2,1)S(1)}, u32[]{:S(2)}, u32[]{:S(2)}) collective-permute-start(bf16[256,128]{1,0:T(8,128)(2,1)S(1)} %get-tuple-element.25), channel_id=1, source_target_pairs={{0,2},{1,3},{2,0},{3,1},{4,6},{5,7},{6,4},{7,5},{8,10},{9,11},{10,... | collective-permute-start | bytes 196616 | tf_op jit(solution)/shard_map/ppermute | solution.py:17
  42.1 0.9 %collective-permute-done.11 = bf16[256,128]{1,0:T(8,128)(2,1)S(1)} collective-permute-done((bf16[256,128]{1,0:T(8,128)(2,1)S(1)}, bf16[256,128]{1,0:T(8,128)(2,1)S(1)}, u32[]{:S(2)}, u32[]{:S(2)}) %collective-permute-start.11) | collective-permute-done | bytes 65568 | tf_op jit(solution)/shard_map/ppermute | solution.py:17
  42.9 0.1 collective-permute-start.12
  43.0 2.2 %collective-permute-done.13 = bf16[256,128]{1,0:T(8,128)(2,1)S(1)} collective-permute-done((bf16[256,128]{1,0:T(8,128)(2,1)S(1)}, bf16[256,128]{1,0:T(8,128)(2,1)S(1)}, u32[]{:S(2)}, u32[]{:S(2)}) %collective-permute-start.13) | collective-permute-done | bytes 65568 | tf_op jit(solution)/shard_map/ppermute | solution.py:17
  45.3 0.1 collective-permute-start.14
  45.3 0.0 collective-permute-done.12.refs_3_
  45.3 0.0 copy-done
  45.4 0.0 copy-done.1
  45.4 0.9 %shard_map.61.refs_1_ = f32[128,512]{1,0:T(8,128)S(1)} custom-call(s32[2]{0:T(128)S(1)} %pad_add_fusion.refs_0_, bf16[128,512]{1,0:T(8,128)(2,1)S(1)} %copy-done.1, bf16[2,128,128]{2,1,0:T(8,128)(2,1)S(1)} %get-tuple-element.28.refs_2_, bf16[2,128,128]{2,1,0:T(8,128)(2,1)S(1)} %collective-permute-done.12.refs_3_, bf16[3,512,512]{2,1,0:T(8,128)(2,1)S(1)} %copy-done), custom_call_target="tpu_custom_call" | custom-call | bytes 1835016 | tf_op jit(solution)/shard_map/pallas_call | solution.py:50
  46.3 0.3 collective-permute-done.14.refs_3_
  46.6 1.5 %shard_map.63 = bf16[128,512]{1,0:T(8,128)(2,1)} custom-call(s32[2]{0:T(128)S(1)} %pad_add_fusion.refs_0_, f32[128,512]{1,0:T(8,128)S(1)} %shard_map.61.refs_1_, bf16[2,128,128]{2,1,0:T(8,128)(2,1)S(1)} %get-tuple-element.24.refs_2_, bf16[2,128,128]{2,1,0:T(8,128)(2,1)S(1)} %collective-permute-done.14.refs_3_, bf16[3,512,512]{2,1,0:T(8,128)(2,1)S(1)} %copy-done), custom_call_target="tpu_custom_call" | custom-call | bytes 1966088 | tf_op jit(solution)/shard_map/pallas_call | solution.py:50
  (10 shorter events, 0.1 us)
Async XLA Ops:
  0.9 1.4 %collective-permute-start = (bf16[128,256]{1,0:T(8,128)(2,1)S(1)}, bf16[128,256]{1,0:T(8,128)(2,1)S(1)}, u32[]{:S(2)}, u32[]{:S(2)}) collective-permute-start(bf16[128,256]{1,0:T(8,128)(2,1)S(1)} %get-tuple-element.33), channel_id=1, source_target_pairs={{0,1},{1,0},{2,3},{3,2},{4,5},{5,4},{6,7},{7,6},{8,9},{9,8},{10,11... | collective-permute-start | bytes 196616 | tf_op jit(solution)/shard_map/ppermute | solution.py:17
  2.3 5.3 %collective-permute-start.1 = (bf16[2,128,128]{2,1,0:T(8,128)(2,1)S(1)}, bf16[2,128,128]{2,1,0:T(8,128)(2,1)S(1)}, u32[]{:S(2)}, u32[]{:S(2)}) collective-permute-start(bf16[2,128,128]{2,1,0:T(8,128)(2,1)S(1)} %get-tuple-element.32), channel_id=1, source_target_pairs={{0,2},{1,3},{2,0},{3,1},{4,6},{5,7},{6,4},{7,5},{8,10},{9,11},{10,... | collective-permute-start | bytes 196616 | tf_op jit(solution)/shard_map/ppermute | solution.py:17
  7.7 15.5 %collective-permute-start.5 = (bf16[512,512]{1,0:T(8,128)(2,1)S(1)}, bf16[512,512]{1,0:T(8,128)(2,1)S(1)}, u32[]{:S(2)}, u32[]{:S(2)}) collective-permute-start(bf16[512,512]{1,0:T(8,128)(2,1)S(1)} %shard_map.56), channel_id=1, source_target_pairs={{0,2},{1,3},{2,0},{3,1},{4,6},{5,7},{6,4},{7,5},{8,10},{9,11},{10,... | collective-permute-start | bytes 1572872 | tf_op jit(solution)/shard_map/ppermute | solution.py:17
  9.5 8.2 %collective-permute-start.4 = (bf16[2,2,128,128]{3,2,1,0:T(8,128)(2,1)S(1)}, bf16[2,2,128,128]{3,2,1,0:T(8,128)(2,1)S(1)}, u32[]{:S(2)}, u32[]{:S(2)}) collective-permute-start(bf16[2,2,128,128]{3,2,1,0:T(8,128)(2,1)S(1)} %pad_maximum_fusion.refs_3_.refs_1_.refs_9_), channel_id=1, source_target_pairs={{0,12},{4,8},{8,4},{12,0},{1,13},{5,9},{9,5},{13,1},{2,14},{6,10},... | collective-permute-start | bytes 393224 | tf_op jit(solution)/shard_map/ppermute | solution.py:17
  13.2 10.0 %collective-permute-start.3 = (bf16[2,2,128,128]{3,2,1,0:T(8,128)(2,1)S(1)}, bf16[2,2,128,128]{3,2,1,0:T(8,128)(2,1)S(1)}, u32[]{:S(2)}, u32[]{:S(2)}) collective-permute-start(bf16[2,2,128,128]{3,2,1,0:T(8,128)(2,1)S(1)} %pad_maximum_fusion.refs_3_.refs_1_.refs_9_), channel_id=1, source_target_pairs={{0,8},{4,12},{8,0},{12,4},{1,9},{5,13},{9,1},{13,5},{2,10},{6,14},... | collective-permute-start | bytes 393224 | tf_op jit(solution)/shard_map/ppermute | solution.py:17
  13.2 10.0 %collective-permute-start.2 = (bf16[2,2,128,128]{3,2,1,0:T(8,128)(2,1)S(1)}, bf16[2,2,128,128]{3,2,1,0:T(8,128)(2,1)S(1)}, u32[]{:S(2)}, u32[]{:S(2)}) collective-permute-start(bf16[2,2,128,128]{3,2,1,0:T(8,128)(2,1)S(1)} %pad_maximum_fusion.refs_3_.refs_1_.refs_9_), channel_id=1, source_target_pairs={{0,4},{4,0},{8,12},{12,8},{1,5},{5,1},{9,13},{13,9},{2,6},{6,2},{1... | collective-permute-start | bytes 393224 | tf_op jit(solution)/shard_map/ppermute | solution.py:17
  14.0 9.3 %collective-permute-start.7 = (bf16[512,512]{1,0:T(8,128)(2,1)S(1)}, bf16[512,512]{1,0:T(8,128)(2,1)S(1)}, u32[]{:S(2)}, u32[]{:S(2)}) collective-permute-start(bf16[512,512]{1,0:T(8,128)(2,1)S(1)} %shard_map.55.refs_0_.refs_1_), channel_id=1, source_target_pairs={{0,1},{1,0},{2,3},{3,2},{4,5},{5,4},{6,7},{7,6},{8,9},{9,8},{10,11... | collective-permute-start | bytes 1572872 | tf_op jit(solution)/shard_map/ppermute | solution.py:17
  23.2 2.0 %collective-permute-start.6 = (bf16[512,512]{1,0:T(8,128)(2,1)S(1)}, bf16[512,512]{1,0:T(8,128)(2,1)S(1)}, u32[]{:S(2)}, u32[]{:S(2)}) collective-permute-start(bf16[512,512]{1,0:T(8,128)(2,1)S(1)} %get-tuple-element.14.refs_2_.refs_3_), channel_id=1, source_target_pairs={{0,1},{1,0},{2,3},{3,2},{4,5},{5,4},{6,7},{7,6},{8,9},{9,8},{10,11... | collective-permute-start | bytes 1572872 | tf_op jit(solution)/shard_map/ppermute | solution.py:17
  25.4 8.3 %collective-permute-start.10 = (bf16[512,128]{1,0:T(8,128)(2,1)S(1)}, bf16[512,128]{1,0:T(8,128)(2,1)S(1)}, u32[]{:S(2)}, u32[]{:S(2)}) collective-permute-start(bf16[512,128]{1,0:T(8,128)(2,1)S(1)} %shard_map.59.refs_5_), channel_id=1, source_target_pairs={{0,12},{4,8},{8,4},{12,0},{1,13},{5,9},{9,5},{13,1},{2,14},{6,10},... | collective-permute-start | bytes 393224 | tf_op jit(solution)/shard_map/ppermute | solution.py:17
  28.0 10.7 %collective-permute-start.9 = (bf16[512,128]{1,0:T(8,128)(2,1)S(1)}, bf16[512,128]{1,0:T(8,128)(2,1)S(1)}, u32[]{:S(2)}, u32[]{:S(2)}) collective-permute-start(bf16[512,128]{1,0:T(8,128)(2,1)S(1)} %shard_map.59.refs_5_), channel_id=1, source_target_pairs={{0,8},{4,12},{8,0},{12,4},{1,9},{5,13},{9,1},{13,5},{2,10},{6,14},... | collective-permute-start | bytes 393224 | tf_op jit(solution)/shard_map/ppermute | solution.py:17
  28.0 10.7 %collective-permute-start.8 = (bf16[512,128]{1,0:T(8,128)(2,1)S(1)}, bf16[512,128]{1,0:T(8,128)(2,1)S(1)}, u32[]{:S(2)}, u32[]{:S(2)}) collective-permute-start(bf16[512,128]{1,0:T(8,128)(2,1)S(1)} %shard_map.59.refs_5_), channel_id=1, source_target_pairs={{0,4},{4,0},{8,12},{12,8},{1,5},{5,1},{9,13},{13,9},{2,6},{6,2},{1... | collective-permute-start | bytes 393224 | tf_op jit(solution)/shard_map/ppermute | solution.py:17
  38.7 4.3 %collective-permute-start.11 = (bf16[256,128]{1,0:T(8,128)(2,1)S(1)}, bf16[256,128]{1,0:T(8,128)(2,1)S(1)}, u32[]{:S(2)}, u32[]{:S(2)}) collective-permute-start(bf16[256,128]{1,0:T(8,128)(2,1)S(1)} %get-tuple-element.19), channel_id=1, source_target_pairs={{0,2},{1,3},{2,0},{3,1},{4,6},{5,7},{6,4},{7,5},{8,10},{9,11},{10,... | collective-permute-start | bytes 196616 | tf_op jit(solution)/shard_map/ppermute | solution.py:17
  39.6 5.8 %copy-start = (bf16[3,512,512]{2,1,0:T(8,128)(2,1)S(1)}, bf16[3,512,512]{2,1,0:T(8,128)(2,1)}, u32[]{:S(2)}) copy-start(bf16[3,512,512]{2,1,0:T(8,128)(2,1)} %refs_4_.3) | copy-start | bytes 4718596
  39.6 5.8 %copy-start.1 = (bf16[128,512]{1,0:T(8,128)(2,1)S(1)}, bf16[128,512]{1,0:T(8,128)(2,1)}, u32[]{:S(2)}) copy-start(bf16[128,512]{1,0:T(8,128)(2,1)} %refs_1_.3) | copy-start | bytes 393220
  40.9 4.3 %collective-permute-start.13 = (bf16[256,128]{1,0:T(8,128)(2,1)S(1)}, bf16[256,128]{1,0:T(8,128)(2,1)S(1)}, u32[]{:S(2)}, u32[]{:S(2)}) collective-permute-start(bf16[256,128]{1,0:T(8,128)(2,1)S(1)} %get-tuple-element.25), channel_id=1, source_target_pairs={{0,2},{1,3},{2,0},{3,1},{4,6},{5,7},{6,4},{7,5},{8,10},{9,11},{10,... | collective-permute-start | bytes 196616 | tf_op jit(solution)/shard_map/ppermute | solution.py:17
  42.9 2.4 %collective-permute-start.12 = (bf16[2,128,128]{2,1,0:T(8,128)(2,1)S(1)}, bf16[2,128,128]{2,1,0:T(8,128)(2,1)S(1)}, u32[]{:S(2)}, u32[]{:S(2)}) collective-permute-start(bf16[2,128,128]{2,1,0:T(8,128)(2,1)S(1)} %get-tuple-element.27), channel_id=1, source_target_pairs={{0,1},{1,0},{2,3},{3,2},{4,5},{5,4},{6,7},{7,6},{8,9},{9,8},{10,11... | collective-permute-start | bytes 196616 | tf_op jit(solution)/shard_map/ppermute | solution.py:17
  45.3 1.3 %collective-permute-start.14 = (bf16[2,128,128]{2,1,0:T(8,128)(2,1)S(1)}, bf16[2,128,128]{2,1,0:T(8,128)(2,1)S(1)}, u32[]{:S(2)}, u32[]{:S(2)}) collective-permute-start(bf16[2,128,128]{2,1,0:T(8,128)(2,1)S(1)} %get-tuple-element.23), channel_id=1, source_target_pairs={{0,1},{1,0},{2,3},{3,2},{4,5},{5,4},{6,7},{7,6},{8,9},{9,8},{10,11... | collective-permute-start | bytes 196616 | tf_op jit(solution)/shard_map/ppermute | solution.py:17

commit v3 on v2

v3 whole, which is shorter than its diff:
```python
import functools

import jax
import jax.numpy as jnp
from jax import lax
from jax.experimental import pallas as pl
from jax.experimental.pallas import tpu as pltpu
from jax.sharding import PartitionSpec as P

BF16 = jnp.bfloat16
F32 = jnp.float32
MIB = 1 << 20


def swap(array, axis, mask):
    peers = lax.axis_size(axis)
    return lax.ppermute(array, axis, [(i, i ^ mask) for i in range(peers)])


def near_by(array):
    if array.size * array.dtype.itemsize > MIB:
        return array
    return pltpu.with_memory_space_constraint(array, pltpu.VMEM)


def after(values, *earlier):
    left = pl.BlockSpec(memory_space=pl.ANY)
    return pl.pallas_call(
        lambda *refs: None,
        out_shape=[jax.ShapeDtypeStruct(v.shape, v.dtype) for v in values],
        in_specs=[left] * (len(values) + len(earlier)),
        out_specs=[left] * len(values),
        input_output_aliases={i: i for i in range(len(values))},
        compiler_params=pltpu.CompilerParams(vmem_limit_bytes=MIB),
    )(*values, *[near_by(e) for e in earlier])


def call(kernel, out_shapes, *args, scratch=(), vmem=4 * MIB, flops=0, hbm=0, earlier=()):
    whole = pl.BlockSpec(memory_space=pltpu.VMEM)
    left = pl.BlockSpec(memory_space=pl.ANY)
    home = pl.BlockSpec(memory_space=pltpu.HBM)
    size = sum(a.size * a.dtype.itemsize for a in args)
    n_args, n_all = len(args), len(args) + len(earlier)

    def body(*refs):
        kernel(*refs[:n_args], *refs[n_all:])

    return pl.pallas_call(
        body,
        out_shape=out_shapes,
        in_specs=[home] * hbm + [whole] * (n_args - hbm) + [left] * len(earlier),
        out_specs=jax.tree.map(lambda _: whole, out_shapes),
        scratch_shapes=list(scratch),
        compiler_params=pltpu.CompilerParams(vmem_limit_bytes=vmem),
        cost_estimate=pl.CostEstimate(flops=flops, bytes_accessed=size, transcendentals=0),
    )(*args[:hbm], *[near_by(a) for a in (*args[hbm:], *earlier)])


def dense_kernel(place_hbm, count_hbm, blocks_hbm, feats_hbm, dense_ref, cut_ref, *scratch):
    place_ref, count_ref, blocks_ref, feats_ref, sems = scratch
    n_blk, cap, tile = blocks_ref.shape[2:5]
    chips, width = cut_ref.shape[0], cut_ref.shape[2]
    pairs = [(blocks_hbm, blocks_ref), (place_hbm, place_ref), (count_hbm, count_ref), (feats_hbm, feats_ref)]
    copies = [pltpu.make_async_copy(a, b, sems.at[i]) for i, (a, b) in enumerate(pairs)]
    for copy in copies:
        copy.start()
    dense_ref[...] = jnp.zeros_like(dense_ref)
    own, rep = lax.axis_index("blk"), lax.axis_index("rep")
    for copy in copies:
        copy.wait()
    for i in range(chips):
        if width % 128 == 0:
            cut_ref[i] = feats_ref[:, pl.ds(pl.multiple_of((rep ^ 2 * i) * width, width), width)]
        else:
            for lane in range(feats_ref.shape[1] // width):

                @pl.when(lane == rep ^ 2 * i)
                def _():
                    cut_ref[i] = feats_ref[:, lane * width : (lane + 1) * width]

    for m in range(n_blk):
        j = own ^ m
        at = m * tile
        for slot in range(cap):

            @pl.when(slot < count_ref[0, 0, j])
            def _():
                row = pl.multiple_of(place_ref[0, 0, j, slot] * tile, tile)
                dense_ref[pl.ds(row, tile), at : at + tile] = blocks_ref[0, 0, j, slot]


def dot(a, b):
    return jnp.dot(a, b, preferred_element_type=F32)


def apply_lanes(lanes, n_blk, tile, rows_of):
    total = None
    each = n_blk // len(lanes[0])
    for m in range(n_blk):
        at = (m % each) * tile
        left = jnp.concatenate([halves[m // each][:, at : at + tile] for halves in lanes], axis=1)
        right = jnp.concatenate([rows_of(m, k) for k in range(len(lanes))], axis=0)
        part = dot(left, right)
        total = part if total is None else total + part
    return total


def paired(refs, n):
    return [refs[i : i + n] for i in range(0, len(refs), n)]


def part_kernel(n_blk, tile, masks, *refs):
    n = len(masks)
    lanes, pieces, more, out_ref = paired(refs[:n], 1), refs[n : n + n_blk], refs[n + n_blk : -1], refs[-1]
    total = apply_lanes(lanes, n_blk, tile, lambda m, i: pieces[m][masks[i] // 2, masks[i] % 2])
    if more:
        total = total + more[0][...]
    out_ref[...] = total.astype(out_ref.dtype)


def second_kernel(n_blk, n_rep, tile, chip, *refs):
    lanes, refs = refs[:n_rep], refs[n_rep:]
    firsts, feats, out_ref, total_ref = refs[:n_blk], refs[n_blk], refs[n_blk + 1], refs[n_blk + 2]
    rep = lax.axis_index("rep")
    size = 2 * tile
    mine = pl.ds(pl.multiple_of((rep // 2 ^ chip) * size, size), size)
    total = None
    for m in range(n_blk):
        left = jnp.concatenate([lane[mine, m * tile : (m + 1) * tile] for lane in lanes], axis=1)
        rows = [pl.ds(pl.multiple_of((rep ^ k) * tile, tile), tile) for k in range(n_rep)]
        part = dot(left, jnp.concatenate([firsts[m][r, :] for r in rows], axis=0))
        total = part if total is None else total + part
    total_ref[...] = total
    for i in range(2):
        rows = pl.ds(pl.multiple_of((rep % 2 ^ i) * tile, tile), tile)
        out_ref[i] = (2.0 * total_ref[rows, :] - feats[chip, i].astype(F32)).astype(BF16)


def weigh(rep, n_rep, near_ref, far_ref, weight_ref, order):
    width = near_ref.shape[2]
    pieces, weights = [], []
    for k in range(n_rep):
        pieces.append(far_ref[k // 2] if k % 2 else near_ref[k // 2])
        weights.append(weight_ref[order, pl.ds(pl.multiple_of((rep ^ k) * width, width), width), :])
    return dot(jnp.concatenate(pieces, axis=1), jnp.concatenate(weights, axis=0))


def early_kernel(n_rep, feats_ref, near_ref, far_ref, weight_ref, out_ref):
    total = dot(feats_ref[...], weight_ref[0])
    out_ref[...] = total + weigh(lax.axis_index("rep"), n_rep, near_ref, far_ref, weight_ref, 1)


def last_kernel(n_rep, early_ref, near_ref, far_ref, weight_ref, out_ref):
    total = early_ref[...] + weigh(lax.axis_index("rep"), n_rep, near_ref, far_ref, weight_ref, 2)
    out_ref[...] = total.astype(BF16)


def to_owners(parts):
    near = jnp.stack([swap(part, "rep", 2 * i) if i else part for i, part in enumerate(parts)])
    return near[:, 0], swap(near[:, 1], "rep", 1)


def per_device(features, order_weights, laplacian_blocks, tile_place, tile_count):
    n_blk, n_rep = lax.axis_size("blk"), lax.axis_size("rep")
    rep = lax.axis_index("rep")
    chips = n_rep // 2
    tile, feat = features.shape
    strip = n_rep * tile
    width = feat // n_rep
    lane_bytes = 2 * strip * n_blk * tile
    rows_bytes = 2 * strip * n_blk * max(width, 128)

    dense, own_cut = call(
        dense_kernel,
        (jax.ShapeDtypeStruct((strip, n_blk * tile), BF16), jax.ShapeDtypeStruct((chips, tile, width), BF16)),
        *(pltpu.with_memory_space_constraint(a, pltpu.HBM) for a in (tile_place, tile_count, laplacian_blocks, features)),
        hbm=4,
        vmem=3 * lane_bytes + 3 * MIB,
        scratch=[
            pltpu.SMEM(tile_place.shape, jnp.int32),
            pltpu.SMEM(tile_count.shape, jnp.int32),
            pltpu.VMEM(laplacian_blocks.shape, BF16),
            pltpu.VMEM(features.shape, BF16),
            pltpu.SemaphoreType.DMA((4,)),
        ],
    )

    got = swap(features, "rep", 1)
    cut = lambda i: jnp.stack([own_cut[i], lax.dynamic_slice_in_dim(got, (rep ^ 2 * i) * width, width, 1)])
    pieces = [swap(cut(i), "rep", 2 * i) if i else cut(i) for i in range(chips)]
    own_rows, mate = after([jnp.stack(pieces), swap(dense, "rep", 1)])
    own_chip = [dense, mate]
    rows = [swap(own_rows, "blk", m) if m else own_rows for m in range(n_blk)]
    arrived = [swap(after([dense], pieces[i])[0], "rep", 2 * i) for i in range(1, chips)]
    lanes = [*own_chip]
    for got in arrived:
        lanes += [got, swap(got, "rep", 1)]

    strip_shape = jax.ShapeDtypeStruct((strip, width), BF16)
    vmem = n_rep * lane_bytes + 2 * rows_bytes + 4 * MIB
    macs = 2 * strip * n_blk * strip * width
    soon = [0, 1, *range(2, n_rep, 2)]
    late = [*range(3, n_rep, 2)]
    part = call(
        functools.partial(part_kernel, n_blk, tile, soon), jax.ShapeDtypeStruct((strip, width), F32),
        *[lanes[k] for k in soon], *rows,
        vmem=vmem, flops=1 << 35,
    )
    first = call(
        functools.partial(part_kernel, n_blk, tile, late), strip_shape,
        *[lanes[k] for k in late], *rows, part,
        vmem=vmem, flops=macs,
    )
    firsts = [swap(first, "blk", m) for m in range(1, n_blk)]
    lane_rows = lambda k: lax.dynamic_slice_in_dim(first, (rep ^ k) * tile, tile, 0)
    parts = [jnp.stack([lane_rows(2 * i), lane_rows(2 * i + 1)]) for i in range(chips)]
    tied = after([*firsts, *parts])
    firsts, parts = [first, *tied[: n_blk - 1]], tied[n_blk - 1 :]
    early_near, early_far = to_owners(parts)
    early = call(
        functools.partial(early_kernel, n_rep),
        jax.ShapeDtypeStruct((tile, feat), F32),
        features, early_near, early_far, order_weights,
    )
    parts = [None] * chips
    for i in [*range(1, chips), 0]:
        parts[i] = call(
            functools.partial(second_kernel, n_blk, n_rep, tile, i),
            jax.ShapeDtypeStruct((2, tile, width), BF16),
            *lanes, *firsts, own_rows,
            vmem=vmem, flops=2 * macs // n_rep,
            scratch=[pltpu.VMEM((2 * tile, width), F32)],
        )
    near, far = to_owners(parts)
    return call(
        functools.partial(last_kernel, n_rep),
        jax.ShapeDtypeStruct((tile, feat), BF16),
        early, near, far, order_weights,
    )


def solution(mesh):
    in_specs = (
        P(("groups", "blk", "rep"), None),
        P(),
        P(("groups", "blk"), "rep", None, None, None, None),
        P(("groups", "blk"), "rep", None, None),
        P(("groups", "blk"), "rep", None),
    )
    out_specs = P(("groups", "blk", "rep"), None)
    return jax.shard_map(
        per_device, mesh=mesh, in_specs=in_specs, out_specs=out_specs, check_vma=False
    )
```

time: 48.2 us -> 46.4 us (0.963)
  Pallas kernels: 6.34 us -> 4.28 us
  waiting for transfers between devices: 24 us -> 24.9 us
  local copies, waits for them, and re-layouts: 0.95 us -> 0.08 us
    pallas_call x6 -> x7, Pallas kernels: 6.34 us -> 4.28 us  [call(): pl.pallas_call(body, out_shape=out_shapes, in_specs=[home] * hbm + [whole...]
    dynamic_slice x3 -> x0, local copies, waits for them, and re-layouts: 0.91 us -> none  [the longest x1 0.88 us: per_device(): given = lax.dynamic_slice_in_dim(features, (1 - c) * half, half, 1)]
    ppermute x15, waiting for transfers between devices: 24 us -> 24.9 us  [swap(): return lax.ppermute(array, axis, [(i, i ^ mask) for i in range(peers)])]
  transfers between devices with their start and end apart: 15 -> 15, of which waited for: 10 -> 8; matrix products, arithmetic and copies ran while one was open for 0% -> 0% of each run, Pallas kernels for 9% -> 7%
where the time goes in v3:
time: 46.4 us; the launch traced here: 46.2 us
  waiting for transfers between devices  24.9 us (54%)
  starting transfers between devices  16.7 us (36%)
  Pallas kernels  4.28 us (9%)
    ppermute x15, waiting for transfers between devices, swap(): return lax.ppermute(array, axis, [(i, i ^ mask) for i in range(peers)])  24.9 us
    ppermute x15, starting transfers between devices, swap(): return lax.ppermute(array, axis, [(i, i ^ mask) for i in range(peers)])  16.7 us
    pallas_call x7, Pallas kernels, call(): pl.pallas_call(body, out_shape=out_shapes, in_specs=[home] * hbm + [whole...  4.28 us
  transfers between devices with their start and end apart: 15, of which 8 were waited for; matrix products, arithmetic and copies ran while one was open for 0% of the time, Pallas kernels for 7%

profile of v3, /device:TPU:0, one launch (start us, length us, event | category | flops | bytes accessed | tf_op | source)
XLA Modules:
  0.0 46.2 jit_solution(16592313451166225482)
XLA Ops:
  0.0 0.5 collective-permute-start
  0.5 1.3 %shard_map.55 = (bf16[512,512]{1,0:T(8,128)(2,1)S(1)}, bf16[2,128,128]{2,1,0:T(8,128)(2,1)S(1)}) custom-call(s32[1,1,4,4]{3,2,1,0:T(4,128)} %refs_0_.2, s32[1,1,4]{2,1,0:T(1,128)} %refs_1_.1, bf16[1,1,4,4,128,128]{5,4,3,2,1,0:T(8,128)(2,1)} %refs_2_.1, bf16[128,512]{1,0:T(8,128)(2,1)} %refs_0_.3), custom_call_target="tpu_custom_call" | custom-call | bytes 655440 | tf_op jit(solution)/shard_map/pallas_call | solution.py:48
  1.8 0.1 collective-permute-start.4
  1.9 0.0 collective-permute-done
  1.9 3.0 %collective-permute-start.1 = (bf16[2,128,128]{2,1,0:T(8,128)(2,1)S(1)}, bf16[2,128,128]{2,1,0:T(8,128)(2,1)S(1)}, u32[]{:S(2)}, u32[]{:S(2)}) collective-permute-start(bf16[2,128,128]{2,1,0:T(8,128)(2,1)S(1)} %pad_maximum_fusion.3), channel_id=1, source_target_pairs={{0,2},{1,3},{2,0},{3,1},{4,6},{5,7},{6,4},{7,5},{8,10},{9,11},{10,... | collective-permute-start | bytes 196616 | tf_op jit(solution)/shard_map/ppermute | solution.py:17
  5.0 2.3 %collective-permute-done.1.refs_1_ = bf16[2,128,128]{2,1,0:T(8,128)(2,1)S(1)} collective-permute-done((bf16[2,128,128]{2,1,0:T(8,128)(2,1)S(1)}, bf16[2,128,128]{2,1,0:T(8,128)(2,1)S(1)}, u32[]{:S(2)}, u32[]{:S(2)}) %collective-permute-start.1) | collective-permute-done | bytes 65568 | tf_op jit(solution)/shard_map/ppermute | solution.py:17
  7.3 2.0 %collective-permute-start.2 = (bf16[512,512]{1,0:T(8,128)(2,1)S(1)}, bf16[512,512]{1,0:T(8,128)(2,1)S(1)}, u32[]{:S(2)}, u32[]{:S(2)}) collective-permute-start(bf16[512,512]{1,0:T(8,128)(2,1)S(1)} %shard_map.56), channel_id=1, source_target_pairs={{0,2},{1,3},{2,0},{3,1},{4,6},{5,7},{6,4},{7,5},{8,10},{9,11},{10,... | collective-permute-start | bytes 1572872 | tf_op jit(solution)/shard_map/ppermute | solution.py:17
  9.3 0.0 collective-permute-done.4.refs_1_
  9.3 3.6 %collective-permute-start.7 = (bf16[2,2,128,128]{3,2,1,0:T(8,128)(2,1)S(1)}, bf16[2,2,128,128]{3,2,1,0:T(8,128)(2,1)S(1)}, u32[]{:S(2)}, u32[]{:S(2)}) collective-permute-start(bf16[2,2,128,128]{3,2,1,0:T(8,128)(2,1)S(1)} %get-tuple-element.16.refs_3_.refs_1_.refs_8_), channel_id=1, source_target_pairs={{0,12},{4,8},{8,4},{12,0},{1,13},{5,9},{9,5},{13,1},{2,14},{6,10},... | collective-permute-start | bytes 393224 | tf_op jit(solution)/shard_map/ppermute | solution.py:17
  12.9 0.0 collective-permute-start.6
  12.9 0.8 %collective-permute-start.5 = (bf16[2,2,128,128]{3,2,1,0:T(8,128)(2,1)S(1)}, bf16[2,2,128,128]{3,2,1,0:T(8,128)(2,1)S(1)}, u32[]{:S(2)}, u32[]{:S(2)}) collective-permute-start(bf16[2,2,128,128]{3,2,1,0:T(8,128)(2,1)S(1)} %get-tuple-element.16.refs_3_.refs_1_.refs_8_), channel_id=1, source_target_pairs={{0,4},{4,0},{8,12},{12,8},{1,5},{5,1},{9,13},{13,9},{2,6},{6,2},{1... | collective-permute-start | bytes 393224 | tf_op jit(solution)/shard_map/ppermute | solution.py:17
  13.7 6.9 %collective-permute-done.2.refs_2_ = bf16[512,512]{1,0:T(8,128)(2,1)S(1)} collective-permute-done((bf16[512,512]{1,0:T(8,128)(2,1)S(1)}, bf16[512,512]{1,0:T(8,128)(2,1)S(1)}, u32[]{:S(2)}, u32[]{:S(2)}) %collective-permute-start.2) | collective-permute-done | bytes 524320 | tf_op jit(solution)/shard_map/ppermute | solution.py:17
  20.6 0.0 collective-permute-start.3
  20.6 0.0 collective-permute-done.7.refs_6_.refs_4_
  20.6 2.2 %collective-permute-done.6.refs_5_.refs_3_ = bf16[2,2,128,128]{3,2,1,0:T(8,128)(2,1)S(1)} collective-permute-done((bf16[2,2,128,128]{3,2,1,0:T(8,128)(2,1)S(1)}, bf16[2,2,128,128]{3,2,1,0:T(8,128)(2,1)S(1)}, u32[]{:S(2)}, u32[]{:S(2)}) %collective-permute-start.6) | collective-permute-done | bytes 131104 | tf_op jit(solution)/shard_map/ppermute | solution.py:17
  22.8 0.0 collective-permute-done.5.refs_4_.refs_2_
  22.8 0.6 %shard_map.58.refs_5_ = f32[512,128]{1,0:T(8,128)S(1)} custom-call(bf16[512,512]{1,0:T(8,128)(2,1)S(1)} %get-tuple-element.14.refs_0_, bf16[512,512]{1,0:T(8,128)(2,1)S(1)} %get-tuple-element.17.refs_1_, bf16[512,512]{1,0:T(8,128)(2,1)S(1)} %collective-permute-done.2.refs_2_, bf16[2,2,128,128]{3,2,1,0:T(8,128)(2,1)S(1)} %get-tuple-element.16.refs_3_.refs_1_.refs_8_, ...), custom_call_target="tpu_custom_call" | custom-call | flops 34359738368 | bytes 2097152 | tf_op jit(solution)/shard_map/pallas_call | solution.py:48
  23.4 0.0 collective-permute-done.3.refs_0_.refs_3_
  23.4 0.3 shard_map.59.refs_4_
  23.7 2.7 %collective-permute-start.10 = (bf16[512,128]{1,0:T(8,128)(2,1)S(1)}, bf16[512,128]{1,0:T(8,128)(2,1)S(1)}, u32[]{:S(2)}, u32[]{:S(2)}) collective-permute-start(bf16[512,128]{1,0:T(8,128)(2,1)S(1)} %shard_map.59.refs_4_), channel_id=1, source_target_pairs={{0,12},{4,8},{8,4},{12,0},{1,13},{5,9},{9,5},{13,1},{2,14},{6,10},... | collective-permute-start | bytes 393224 | tf_op jit(solution)/shard_map/ppermute | solution.py:17
  26.3 0.0 collective-permute-start.9
  26.3 1.8 %collective-permute-start.8 = (bf16[512,128]{1,0:T(8,128)(2,1)S(1)}, bf16[512,128]{1,0:T(8,128)(2,1)S(1)}, u32[]{:S(2)}, u32[]{:S(2)}) collective-permute-start(bf16[512,128]{1,0:T(8,128)(2,1)S(1)} %shard_map.59.refs_4_), channel_id=1, source_target_pairs={{0,4},{4,0},{8,12},{12,8},{1,5},{5,1},{9,13},{13,9},{2,6},{6,2},{1... | collective-permute-start | bytes 393224 | tf_op jit(solution)/shard_map/ppermute | solution.py:17
  28.2 3.8 %collective-permute-done.10.refs_2_ = bf16[512,128]{1,0:T(8,128)(2,1)S(1)} collective-permute-done((bf16[512,128]{1,0:T(8,128)(2,1)S(1)}, bf16[512,128]{1,0:T(8,128)(2,1)S(1)}, u32[]{:S(2)}, u32[]{:S(2)}) %collective-permute-start.10) | collective-permute-done | bytes 131104 | tf_op jit(solution)/shard_map/ppermute | solution.py:17
  32.0 5.7 %collective-permute-done.9.refs_1_ = bf16[512,128]{1,0:T(8,128)(2,1)S(1)} collective-permute-done((bf16[512,128]{1,0:T(8,128)(2,1)S(1)}, bf16[512,128]{1,0:T(8,128)(2,1)S(1)}, u32[]{:S(2)}, u32[]{:S(2)}) %collective-permute-start.9) | collective-permute-done | bytes 131104 | tf_op jit(solution)/shard_map/ppermute | solution.py:17
  37.7 0.0 collective-permute-done.8.refs_0_
  37.7 1.5 %collective-permute-start.11 = (bf16[2,128,128]{2,1,0:T(8,128)(2,1)S(1)}, bf16[2,128,128]{2,1,0:T(8,128)(2,1)S(1)}, u32[]{:S(2)}, u32[]{:S(2)}) collective-permute-start(bf16[2,128,128]{2,1,0:T(8,128)(2,1)S(1)} %get-tuple-element.19), channel_id=1, source_target_pairs={{0,2},{1,3},{2,0},{3,1},{4,6},{5,7},{6,4},{7,5},{8,10},{9,11},{10,... | collective-permute-start | bytes 196616 | tf_op jit(solution)/shard_map/ppermute | solution.py:17
  39.2 0.5 shard_map.63
  39.7 0.0 copy-start
  39.7 0.0 copy-start.1
  39.7 0.6 %collective-permute-start.13 = (bf16[2,128,128]{2,1,0:T(8,128)(2,1)S(1)}, bf16[2,128,128]{2,1,0:T(8,128)(2,1)S(1)}, u32[]{:S(2)}, u32[]{:S(2)}) collective-permute-start(bf16[2,128,128]{2,1,0:T(8,128)(2,1)S(1)} %shard_map.63), channel_id=1, source_target_pairs={{0,2},{1,3},{2,0},{3,1},{4,6},{5,7},{6,4},{7,5},{8,10},{9,11},{10,... | collective-permute-start | bytes 196616 | tf_op jit(solution)/shard_map/ppermute | solution.py:17
  40.3 0.5 shard_map.62
  40.8 1.8 %collective-permute-done.11 = bf16[2,128,128]{2,1,0:T(8,128)(2,1)S(1)} collective-permute-done((bf16[2,128,128]{2,1,0:T(8,128)(2,1)S(1)}, bf16[2,128,128]{2,1,0:T(8,128)(2,1)S(1)}, u32[]{:S(2)}, u32[]{:S(2)}) %collective-permute-start.11) | collective-permute-done | bytes 65568 | tf_op jit(solution)/shard_map/ppermute | solution.py:17
  42.6 0.1 collective-permute-start.12
  42.7 1.3 %collective-permute-done.13 = bf16[2,128,128]{2,1,0:T(8,128)(2,1)S(1)} collective-permute-done((bf16[2,128,128]{2,1,0:T(8,128)(2,1)S(1)}, bf16[2,128,128]{2,1,0:T(8,128)(2,1)S(1)}, u32[]{:S(2)}, u32[]{:S(2)}) %collective-permute-start.13) | collective-permute-done | bytes 65568 | tf_op jit(solution)/shard_map/ppermute | solution.py:17
  44.0 0.1 collective-permute-start.14
  44.1 0.0 collective-permute-done.12.refs_2_
  44.1 0.0 copy-done
  44.1 0.0 copy-done.1
  44.1 0.3 shard_map.61.refs_0_
  44.5 0.9 %collective-permute-done.14.refs_2_ = bf16[2,128,128]{2,1,0:T(8,128)(2,1)S(1)} collective-permute-done((bf16[2,128,128]{2,1,0:T(8,128)(2,1)S(1)}, bf16[2,128,128]{2,1,0:T(8,128)(2,1)S(1)}, u32[]{:S(2)}, u32[]{:S(2)}) %collective-permute-start.14) | collective-permute-done | bytes 65568 | tf_op jit(solution)/shard_map/ppermute | solution.py:17
  45.4 0.9 %shard_map.64 = bf16[128,512]{1,0:T(8,128)(2,1)} custom-call(f32[128,512]{1,0:T(8,128)S(1)} %shard_map.61.refs_0_, bf16[2,128,128]{2,1,0:T(8,128)(2,1)S(1)} %get-tuple-element.24.refs_1_, bf16[2,128,128]{2,1,0:T(8,128)(2,1)S(1)} %collective-permute-done.14.refs_2_, bf16[3,512,512]{2,1,0:T(8,128)(2,1)S(1)} %copy-done), custom_call_target="tpu_custom_call" | custom-call | bytes 1966080 | tf_op jit(solution)/shard_map/pallas_call | solution.py:48
  (13 shorter events, 0.1 us)
Async XLA Ops:
  0.0 1.9 %collective-permute-start = (bf16[128,512]{1,0:T(8,128)(2,1)}, bf16[128,512]{1,0:T(8,128)(2,1)S(1)}, u32[]{:S(2)}, u32[]{:S(2)}) collective-permute-start(bf16[128,512]{1,0:T(8,128)(2,1)} %refs_0_.3), channel_id=1, source_target_pairs={{0,1},{1,0},{2,3},{3,2},{4,5},{5,4},{6,7},{7,6},{8,9},{9,8},{10,11... | collective-permute-start | bytes 393224 | tf_op jit(solution)/shard_map/ppermute | solution.py:17
  1.8 7.5 %collective-permute-start.4 = (bf16[512,512]{1,0:T(8,128)(2,1)S(1)}, bf16[512,512]{1,0:T(8,128)(2,1)S(1)}, u32[]{:S(2)}, u32[]{:S(2)}) collective-permute-start(bf16[512,512]{1,0:T(8,128)(2,1)S(1)} %get-tuple-element.14.refs_0_), channel_id=1, source_target_pairs={{0,1},{1,0},{2,3},{3,2},{4,5},{5,4},{6,7},{7,6},{8,9},{9,8},{10,11... | collective-permute-start | bytes 1572872 | tf_op jit(solution)/shard_map/ppermute | solution.py:17
  1.9 5.3 %collective-permute-start.1 = (bf16[2,128,128]{2,1,0:T(8,128)(2,1)S(1)}, bf16[2,128,128]{2,1,0:T(8,128)(2,1)S(1)}, u32[]{:S(2)}, u32[]{:S(2)}) collective-permute-start(bf16[2,128,128]{2,1,0:T(8,128)(2,1)S(1)} %pad_maximum_fusion.3), channel_id=1, source_target_pairs={{0,2},{1,3},{2,0},{3,1},{4,6},{5,7},{6,4},{7,5},{8,10},{9,11},{10,... | collective-permute-start | bytes 196616 | tf_op jit(solution)/shard_map/ppermute | solution.py:17
  7.3 13.3 %collective-permute-start.2 = (bf16[512,512]{1,0:T(8,128)(2,1)S(1)}, bf16[512,512]{1,0:T(8,128)(2,1)S(1)}, u32[]{:S(2)}, u32[]{:S(2)}) collective-permute-start(bf16[512,512]{1,0:T(8,128)(2,1)S(1)} %shard_map.56), channel_id=1, source_target_pairs={{0,2},{1,3},{2,0},{3,1},{4,6},{5,7},{6,4},{7,5},{8,10},{9,11},{10,... | collective-permute-start | bytes 1572872 | tf_op jit(solution)/shard_map/ppermute | solution.py:17
  9.3 11.3 %collective-permute-start.7 = (bf16[2,2,128,128]{3,2,1,0:T(8,128)(2,1)S(1)}, bf16[2,2,128,128]{3,2,1,0:T(8,128)(2,1)S(1)}, u32[]{:S(2)}, u32[]{:S(2)}) collective-permute-start(bf16[2,2,128,128]{3,2,1,0:T(8,128)(2,1)S(1)} %get-tuple-element.16.refs_3_.refs_1_.refs_8_), channel_id=1, source_target_pairs={{0,12},{4,8},{8,4},{12,0},{1,13},{5,9},{9,5},{13,1},{2,14},{6,10},... | collective-permute-start | bytes 393224 | tf_op jit(solution)/shard_map/ppermute | solution.py:17
  12.9 9.9 %collective-permute-start.6 = (bf16[2,2,128,128]{3,2,1,0:T(8,128)(2,1)S(1)}, bf16[2,2,128,128]{3,2,1,0:T(8,128)(2,1)S(1)}, u32[]{:S(2)}, u32[]{:S(2)}) collective-permute-start(bf16[2,2,128,128]{3,2,1,0:T(8,128)(2,1)S(1)} %get-tuple-element.16.refs_3_.refs_1_.refs_8_), channel_id=1, source_target_pairs={{0,8},{4,12},{8,0},{12,4},{1,9},{5,13},{9,1},{13,5},{2,10},{6,14},... | collective-permute-start | bytes 393224 | tf_op jit(solution)/shard_map/ppermute | solution.py:17
  12.9 9.9 %collective-permute-start.5 = (bf16[2,2,128,128]{3,2,1,0:T(8,128)(2,1)S(1)}, bf16[2,2,128,128]{3,2,1,0:T(8,128)(2,1)S(1)}, u32[]{:S(2)}, u32[]{:S(2)}) collective-permute-start(bf16[2,2,128,128]{3,2,1,0:T(8,128)(2,1)S(1)} %get-tuple-element.16.refs_3_.refs_1_.refs_8_), channel_id=1, source_target_pairs={{0,4},{4,0},{8,12},{12,8},{1,5},{5,1},{9,13},{13,9},{2,6},{6,2},{1... | collective-permute-start | bytes 393224 | tf_op jit(solution)/shard_map/ppermute | solution.py:17
  20.6 2.8 %collective-permute-start.3 = (bf16[512,512]{1,0:T(8,128)(2,1)S(1)}, bf16[512,512]{1,0:T(8,128)(2,1)S(1)}, u32[]{:S(2)}, u32[]{:S(2)}) collective-permute-start(bf16[512,512]{1,0:T(8,128)(2,1)S(1)} %collective-permute-done.2.refs_2_), channel_id=1, source_target_pairs={{0,1},{1,0},{2,3},{3,2},{4,5},{5,4},{6,7},{7,6},{8,9},{9,8},{10,11... | collective-permute-start | bytes 1572872 | tf_op jit(solution)/shard_map/ppermute | solution.py:17
  23.7 8.3 %collective-permute-start.10 = (bf16[512,128]{1,0:T(8,128)(2,1)S(1)}, bf16[512,128]{1,0:T(8,128)(2,1)S(1)}, u32[]{:S(2)}, u32[]{:S(2)}) collective-permute-start(bf16[512,128]{1,0:T(8,128)(2,1)S(1)} %shard_map.59.refs_4_), channel_id=1, source_target_pairs={{0,12},{4,8},{8,4},{12,0},{1,13},{5,9},{9,5},{13,1},{2,14},{6,10},... | collective-permute-start | bytes 393224 | tf_op jit(solution)/shard_map/ppermute | solution.py:17
  26.3 11.4 %collective-permute-start.9 = (bf16[512,128]{1,0:T(8,128)(2,1)S(1)}, bf16[512,128]{1,0:T(8,128)(2,1)S(1)}, u32[]{:S(2)}, u32[]{:S(2)}) collective-permute-start(bf16[512,128]{1,0:T(8,128)(2,1)S(1)} %shard_map.59.refs_4_), channel_id=1, source_target_pairs={{0,8},{4,12},{8,0},{12,4},{1,9},{5,13},{9,1},{13,5},{2,10},{6,14},... | collective-permute-start | bytes 393224 | tf_op jit(solution)/shard_map/ppermute | solution.py:17
  26.3 11.4 %collective-permute-start.8 = (bf16[512,128]{1,0:T(8,128)(2,1)S(1)}, bf16[512,128]{1,0:T(8,128)(2,1)S(1)}, u32[]{:S(2)}, u32[]{:S(2)}) collective-permute-start(bf16[512,128]{1,0:T(8,128)(2,1)S(1)} %shard_map.59.refs_4_), channel_id=1, source_target_pairs={{0,4},{4,0},{8,12},{12,8},{1,5},{5,1},{9,13},{13,9},{2,6},{6,2},{1... | collective-permute-start | bytes 393224 | tf_op jit(solution)/shard_map/ppermute | solution.py:17
  37.7 4.9 %collective-permute-start.11 = (bf16[2,128,128]{2,1,0:T(8,128)(2,1)S(1)}, bf16[2,128,128]{2,1,0:T(8,128)(2,1)S(1)}, u32[]{:S(2)}, u32[]{:S(2)}) collective-permute-start(bf16[2,128,128]{2,1,0:T(8,128)(2,1)S(1)} %get-tuple-element.19), channel_id=1, source_target_pairs={{0,2},{1,3},{2,0},{3,1},{4,6},{5,7},{6,4},{7,5},{8,10},{9,11},{10,... | collective-permute-start | bytes 196616 | tf_op jit(solution)/shard_map/ppermute | solution.py:17
  39.7 4.5 %copy-start = (bf16[3,512,512]{2,1,0:T(8,128)(2,1)S(1)}, bf16[3,512,512]{2,1,0:T(8,128)(2,1)}, u32[]{:S(2)}) copy-start(bf16[3,512,512]{2,1,0:T(8,128)(2,1)} %refs_3_.5) | copy-start | bytes 4718596
  39.7 4.5 %copy-start.1 = (bf16[128,512]{1,0:T(8,128)(2,1)S(1)}, bf16[128,512]{1,0:T(8,128)(2,1)}, u32[]{:S(2)}) copy-start(bf16[128,512]{1,0:T(8,128)(2,1)} %refs_0_.3) | copy-start | bytes 393220
  39.7 4.3 %collective-permute-start.13 = (bf16[2,128,128]{2,1,0:T(8,128)(2,1)S(1)}, bf16[2,128,128]{2,1,0:T(8,128)(2,1)S(1)}, u32[]{:S(2)}, u32[]{:S(2)}) collective-permute-start(bf16[2,128,128]{2,1,0:T(8,128)(2,1)S(1)} %shard_map.63), channel_id=1, source_target_pairs={{0,2},{1,3},{2,0},{3,1},{4,6},{5,7},{6,4},{7,5},{8,10},{9,11},{10,... | collective-permute-start | bytes 196616 | tf_op jit(solution)/shard_map/ppermute | solution.py:17
  42.6 1.5 %collective-permute-start.12 = (bf16[2,128,128]{2,1,0:T(8,128)(2,1)S(1)}, bf16[2,128,128]{2,1,0:T(8,128)(2,1)S(1)}, u32[]{:S(2)}, u32[]{:S(2)}) collective-permute-start(bf16[2,128,128]{2,1,0:T(8,128)(2,1)S(1)} %get-tuple-element.25), channel_id=1, source_target_pairs={{0,1},{1,0},{2,3},{3,2},{4,5},{5,4},{6,7},{7,6},{8,9},{9,8},{10,11... | collective-permute-start | bytes 196616 | tf_op jit(solution)/shard_map/ppermute | solution.py:17
  44.0 1.3 %collective-permute-start.14 = (bf16[2,128,128]{2,1,0:T(8,128)(2,1)S(1)}, bf16[2,128,128]{2,1,0:T(8,128)(2,1)S(1)}, u32[]{:S(2)}, u32[]{:S(2)}) collective-permute-start(bf16[2,128,128]{2,1,0:T(8,128)(2,1)S(1)} %get-tuple-element.23), channel_id=1, source_target_pairs={{0,1},{1,0},{2,3},{3,2},{4,5},{5,4},{6,7},{7,6},{8,9},{9,8},{10,11... | collective-permute-start | bytes 196616 | tf_op jit(solution)/shard_map/ppermute | solution.py:17

commit v4 on v3

--- a/solution.py
+++ b/solution.py
@@ -118,46 +118,34 @@
     out_ref[...] = total.astype(out_ref.dtype)
 
 
-def second_kernel(n_blk, n_rep, tile, chip, *refs):
-    lanes, refs = refs[:n_rep], refs[n_rep:]
-    firsts, feats, out_ref, total_ref = refs[:n_blk], refs[n_blk], refs[n_blk + 1], refs[n_blk + 2]
+def second_kernel(n_blk, n_rep, tile, *refs):
+    lanes, refs = paired(refs[:n_rep], 1), refs[n_rep:]
+    firsts, feats, outs, total_ref = refs[:n_blk], refs[n_blk], refs[n_blk + 1 : -1], refs[-1]
     rep = lax.axis_index("rep")
-    size = 2 * tile
-    mine = pl.ds(pl.multiple_of((rep // 2 ^ chip) * size, size), size)
-    total = None
-    for m in range(n_blk):
-        left = jnp.concatenate([lane[mine, m * tile : (m + 1) * tile] for lane in lanes], axis=1)
-        rows = [pl.ds(pl.multiple_of((rep ^ k) * tile, tile), tile) for k in range(n_rep)]
-        part = dot(left, jnp.concatenate([firsts[m][r, :] for r in rows], axis=0))
-        total = part if total is None else total + part
-    total_ref[...] = total
+    rows = [pl.ds(pl.multiple_of((rep ^ k) * tile, tile), tile) for k in range(n_rep)]
+    total_ref[...] = apply_lanes(lanes, n_blk, tile, lambda m, k: firsts[m][rows[k], :])
+    for k, out_ref in enumerate(outs):
+        out_ref[0] = firsts[0][rows[k], :]
+        out_ref[1] = (2.0 * total_ref[rows[k], :] - feats[k // 2, k % 2].astype(F32)).astype(BF16)
+
+
+def weigh(pieces, weight_ref, order):
+    rep, width = lax.axis_index("rep"), pieces[0].shape[1]
+    rows = [pl.ds(pl.multiple_of((rep ^ k) * width, width), width) for k in range(len(pieces))]
+    weights = [weight_ref[order, r, :] for r in rows]
+    return dot(jnp.concatenate(pieces, axis=1), jnp.concatenate(weights, axis=0))
+
+
+def early_kernel(feats_ref, weight_ref, out_ref):
+    out_ref[...] = dot(feats_ref[...], weight_ref[0])
+
+
+def last_kernel(early_ref, weight_ref, *refs):
+    pieces, out_ref = refs[:-1], refs[-1]
+    total = early_ref[...]
     for i in range(2):
-        rows = pl.ds(pl.multiple_of((rep % 2 ^ i) * tile, tile), tile)
-        out_ref[i] = (2.0 * total_ref[rows, :] - feats[chip, i].astype(F32)).astype(BF16)
-
-
-def weigh(rep, n_rep, near_ref, far_ref, weight_ref, order):
-    width = near_ref.shape[2]
-    pieces, weights = [], []
-    for k in range(n_rep):
-        pieces.append(far_ref[k // 2] if k % 2 else near_ref[k // 2])
-        weights.append(weight_ref[order, pl.ds(pl.multiple_of((rep ^ k) * width, width), width), :])
-    return dot(jnp.concatenate(pieces, axis=1), jnp.concatenate(weights, axis=0))
-
-
-def early_kernel(n_rep, feats_ref, near_ref, far_ref, weight_ref, out_ref):
-    total = dot(feats_ref[...], weight_ref[0])
-    out_ref[...] = total + weigh(lax.axis_index("rep"), n_rep, near_ref, far_ref, weight_ref, 1)
-
-
-def last_kernel(n_rep, early_ref, near_ref, far_ref, weight_ref, out_ref):
-    total = early_ref[...] + weigh(lax.axis_index("rep"), n_rep, near_ref, far_ref, weight_ref, 2)
+        total = total + weigh([piece[i] for piece in pieces], weight_ref, 1 + i)
     out_ref[...] = total.astype(BF16)
-
-
-def to_owners(parts):
-    near = jnp.stack([swap(part, "rep", 2 * i) if i else part for i, part in enumerate(parts)])
-    return near[:, 0], swap(near[:, 1], "rep", 1)
 
 
 def per_device(features, order_weights, laplacian_blocks, tile_place, tile_count):
@@ -212,31 +200,17 @@
         vmem=vmem, flops=macs,
     )
     firsts = [swap(first, "blk", m) for m in range(1, n_blk)]
-    lane_rows = lambda k: lax.dynamic_slice_in_dim(first, (rep ^ k) * tile, tile, 0)
-    parts = [jnp.stack([lane_rows(2 * i), lane_rows(2 * i + 1)]) for i in range(chips)]
-    tied = after([*firsts, *parts])
-    firsts, parts = [first, *tied[: n_blk - 1]], tied[n_blk - 1 :]
-    early_near, early_far = to_owners(parts)
-    early = call(
-        functools.partial(early_kernel, n_rep),
-        jax.ShapeDtypeStruct((tile, feat), F32),
-        features, early_near, early_far, order_weights,
-    )
-    parts = [None] * chips
-    for i in [*range(1, chips), 0]:
-        parts[i] = call(
-            functools.partial(second_kernel, n_blk, n_rep, tile, i),
-            jax.ShapeDtypeStruct((2, tile, width), BF16),
-            *lanes, *firsts, own_rows,
-            vmem=vmem, flops=2 * macs // n_rep,
-            scratch=[pltpu.VMEM((2 * tile, width), F32)],
-        )
-    near, far = to_owners(parts)
-    return call(
-        functools.partial(last_kernel, n_rep),
-        jax.ShapeDtypeStruct((tile, feat), BF16),
-        early, near, far, order_weights,
-    )
+    firsts = [first, *firsts]
+    seconds = call(
+        functools.partial(second_kernel, n_blk, n_rep, tile),
+        (jax.ShapeDtypeStruct((2, tile, width), BF16),) * n_rep,
+        *lanes, *firsts, own_rows,
+        vmem=vmem, flops=macs,
+        scratch=[pltpu.VMEM((strip, width), F32)],
+    )
+    seconds = [swap(rows, "rep", k) if k else rows for k, rows in enumerate(seconds)]
+    early = call(early_kernel, jax.ShapeDtypeStruct((tile, feat), F32), features, order_weights)
+    return call(last_kernel, jax.ShapeDtypeStruct((tile, feat), BF16), early, order_weights, *seconds)
 
 
 def solution(mesh):

time: 46.4 us -> 45.3 us (0.976)
  waiting for transfers between devices: 24.9 us -> 24.4 us
    ppermute x15 -> x14, waiting for transfers between devices: 24.9 us -> 24.4 us  [swap(): return lax.ppermute(array, axis, [(i, i ^ mask) for i in range(peers)])]
    ppermute x15 -> x14, starting transfers between devices: 16.7 us -> 16.4 us  [swap(): return lax.ppermute(array, axis, [(i, i ^ mask) for i in range(peers)])]
    pallas_call x7 -> x6, Pallas kernels: 4.28 us -> 4.12 us  [call(): pl.pallas_call(body, out_shape=out_shapes, in_specs=[home] * hbm + [whole...]
  transfers between devices with their start and end apart: 15 -> 14, of which waited for: 8 -> 8; matrix products, arithmetic and copies ran while one was open for 0% -> 0% of each run, Pallas kernels for 7% -> 5%
where the time goes in v4:
time: 45.3 us; the launch traced here: 45.1 us
  waiting for transfers between devices  24.4 us (54%)
  starting transfers between devices  16.4 us (36%)
  Pallas kernels  4.12 us (9%)
    ppermute x14, waiting for transfers between devices, swap(): return lax.ppermute(array, axis, [(i, i ^ mask) for i in range(peers)])  24.4 us
    ppermute x14, starting transfers between devices, swap(): return lax.ppermute(array, axis, [(i, i ^ mask) for i in range(peers)])  16.4 us
    pallas_call x6, Pallas kernels, call(): pl.pallas_call(body, out_shape=out_shapes, in_specs=[home] * hbm + [whole...  4.12 us
  transfers between devices with their start and end apart: 14, of which 8 were waited for; matrix products, arithmetic and copies ran while one was open for 0% of the time, Pallas kernels for 5%

profile of v4, /device:TPU:0, one launch (start us, length us, event | category | flops | bytes accessed | tf_op | source)
XLA Modules:
  0.0 45.1 jit_solution(9185001920791679777)
XLA Ops:
  0.0 0.5 %collective-permute-start = (bf16[128,512]{1,0:T(8,128)(2,1)}, bf16[128,512]{1,0:T(8,128)(2,1)S(1)}, u32[]{:S(2)}, u32[]{:S(2)}) collective-permute-start(bf16[128,512]{1,0:T(8,128)(2,1)} %refs_3_.1), channel_id=1, source_target_pairs={{0,1},{1,0},{2,3},{3,2},{4,5},{5,4},{6,7},{7,6},{8,9},{9,8},{10,11... | collective-permute-start | bytes 393224 | tf_op jit(solution)/shard_map/ppermute | solution.py:17
  0.5 1.3 %shard_map.56 = (bf16[512,512]{1,0:T(8,128)(2,1)S(1)}, bf16[2,128,128]{2,1,0:T(8,128)(2,1)S(1)}) custom-call(s32[1,1,4,4]{3,2,1,0:T(4,128)} %refs_0_.3, s32[1,1,4]{2,1,0:T(1,128)} %refs_1_.4, bf16[1,1,4,4,128,128]{5,4,3,2,1,0:T(8,128)(2,1)} %refs_2_.1, bf16[128,512]{1,0:T(8,128)(2,1)} %refs_3_.1), custom_call_target="tpu_custom_call" | custom-call | bytes 655440 | tf_op jit(solution)/shard_map/pallas_call | solution.py:48
  1.8 0.1 collective-permute-start.2
  1.9 0.0 collective-permute-done
  1.9 3.0 %collective-permute-start.1 = (bf16[2,128,128]{2,1,0:T(8,128)(2,1)S(1)}, bf16[2,128,128]{2,1,0:T(8,128)(2,1)S(1)}, u32[]{:S(2)}, u32[]{:S(2)}) collective-permute-start(bf16[2,128,128]{2,1,0:T(8,128)(2,1)S(1)} %pad_maximum_fusion.1), channel_id=1, source_target_pairs={{0,2},{1,3},{2,0},{3,1},{4,6},{5,7},{6,4},{7,5},{8,10},{9,11},{10,... | collective-permute-start | bytes 196616 | tf_op jit(solution)/shard_map/ppermute | solution.py:17
  5.0 2.3 %collective-permute-done.1.refs_1_ = bf16[2,128,128]{2,1,0:T(8,128)(2,1)S(1)} collective-permute-done((bf16[2,128,128]{2,1,0:T(8,128)(2,1)S(1)}, bf16[2,128,128]{2,1,0:T(8,128)(2,1)S(1)}, u32[]{:S(2)}, u32[]{:S(2)}) %collective-permute-start.1) | collective-permute-done | bytes 65568 | tf_op jit(solution)/shard_map/ppermute | solution.py:17
  7.3 2.0 %collective-permute-start.3 = (bf16[512,512]{1,0:T(8,128)(2,1)S(1)}, bf16[512,512]{1,0:T(8,128)(2,1)S(1)}, u32[]{:S(2)}, u32[]{:S(2)}) collective-permute-start(bf16[512,512]{1,0:T(8,128)(2,1)S(1)} %shard_map.58), channel_id=1, source_target_pairs={{0,2},{1,3},{2,0},{3,1},{4,6},{5,7},{6,4},{7,5},{8,10},{9,11},{10,... | collective-permute-start | bytes 1572872 | tf_op jit(solution)/shard_map/ppermute | solution.py:17
  9.3 0.0 collective-permute-done.2.refs_1_
  9.3 1.6 %collective-permute-start.5 = (bf16[2,2,128,128]{3,2,1,0:T(8,128)(2,1)S(1)}, bf16[2,2,128,128]{3,2,1,0:T(8,128)(2,1)S(1)}, u32[]{:S(2)}, u32[]{:S(2)}) collective-permute-start(bf16[2,2,128,128]{3,2,1,0:T(8,128)(2,1)S(1)} %get-tuple-element.16.refs_3_.refs_1_.refs_8_), channel_id=1, source_target_pairs={{0,4},{4,0},{8,12},{12,8},{1,5},{5,1},{9,13},{13,9},{2,6},{6,2},{1... | collective-permute-start | bytes 393224 | tf_op jit(solution)/shard_map/ppermute | solution.py:17
  10.9 2.6 %collective-permute-start.6 = (bf16[2,2,128,128]{3,2,1,0:T(8,128)(2,1)S(1)}, bf16[2,2,128,128]{3,2,1,0:T(8,128)(2,1)S(1)}, u32[]{:S(2)}, u32[]{:S(2)}) collective-permute-start(bf16[2,2,128,128]{3,2,1,0:T(8,128)(2,1)S(1)} %get-tuple-element.16.refs_3_.refs_1_.refs_8_), channel_id=1, source_target_pairs={{0,8},{4,12},{8,0},{12,4},{1,9},{5,13},{9,1},{13,5},{2,10},{6,14},... | collective-permute-start | bytes 393224 | tf_op jit(solution)/shard_map/ppermute | solution.py:17
  13.5 0.2 collective-permute-start.7
  13.7 6.9 %collective-permute-done.3.refs_2_ = bf16[512,512]{1,0:T(8,128)(2,1)S(1)} collective-permute-done((bf16[512,512]{1,0:T(8,128)(2,1)S(1)}, bf16[512,512]{1,0:T(8,128)(2,1)S(1)}, u32[]{:S(2)}, u32[]{:S(2)}) %collective-permute-start.3) | collective-permute-done | bytes 524320 | tf_op jit(solution)/shard_map/ppermute | solution.py:17
  20.6 0.0 collective-permute-start.4
  20.6 0.0 collective-permute-done.5.refs_4_.refs_2_
  20.6 2.0 %collective-permute-done.6.refs_5_.refs_3_ = bf16[2,2,128,128]{3,2,1,0:T(8,128)(2,1)S(1)} collective-permute-done((bf16[2,2,128,128]{3,2,1,0:T(8,128)(2,1)S(1)}, bf16[2,2,128,128]{3,2,1,0:T(8,128)(2,1)S(1)}, u32[]{:S(2)}, u32[]{:S(2)}) %collective-permute-start.6) | collective-permute-done | bytes 131104 | tf_op jit(solution)/shard_map/ppermute | solution.py:17
  22.6 0.0 collective-permute-done.7.refs_6_.refs_4_
  22.6 0.6 %shard_map.59.refs_5_ = f32[512,128]{1,0:T(8,128)S(1)} custom-call(bf16[512,512]{1,0:T(8,128)(2,1)S(1)} %get-tuple-element.13.refs_0_, bf16[512,512]{1,0:T(8,128)(2,1)S(1)} %get-tuple-element.15.refs_1_, bf16[512,512]{1,0:T(8,128)(2,1)S(1)} %collective-permute-done.3.refs_2_, bf16[2,2,128,128]{3,2,1,0:T(8,128)(2,1)S(1)} %get-tuple-element.16.refs_3_.refs_1_.refs_8_, ...), custom_call_target="tpu_custom_call" | custom-call | flops 34359738368 | bytes 2097152 | tf_op jit(solution)/shard_map/pallas_call | solution.py:48
  23.1 0.0 collective-permute-done.4.refs_0_.refs_3_
  23.2 0.3 shard_map.60.refs_4_
  23.5 0.0 copy-start
  23.5 0.0 copy-start.1
  23.5 2.9 %collective-permute-start.10 = (bf16[512,128]{1,0:T(8,128)(2,1)S(1)}, bf16[512,128]{1,0:T(8,128)(2,1)S(1)}, u32[]{:S(2)}, u32[]{:S(2)}) collective-permute-start(bf16[512,128]{1,0:T(8,128)(2,1)S(1)} %shard_map.60.refs_4_), channel_id=1, source_target_pairs={{0,12},{4,8},{8,4},{12,0},{1,13},{5,9},{9,5},{13,1},{2,14},{6,10},... | collective-permute-start | bytes 393224 | tf_op jit(solution)/shard_map/ppermute | solution.py:17
  26.4 0.8 %collective-permute-start.8 = (bf16[512,128]{1,0:T(8,128)(2,1)S(1)}, bf16[512,128]{1,0:T(8,128)(2,1)S(1)}, u32[]{:S(2)}, u32[]{:S(2)}) collective-permute-start(bf16[512,128]{1,0:T(8,128)(2,1)S(1)} %shard_map.60.refs_4_), channel_id=1, source_target_pairs={{0,4},{4,0},{8,12},{12,8},{1,5},{5,1},{9,13},{13,9},{2,6},{6,2},{1... | collective-permute-start | bytes 393224 | tf_op jit(solution)/shard_map/ppermute | solution.py:17
  27.1 0.8 %collective-permute-start.9 = (bf16[512,128]{1,0:T(8,128)(2,1)S(1)}, bf16[512,128]{1,0:T(8,128)(2,1)S(1)}, u32[]{:S(2)}, u32[]{:S(2)}) collective-permute-start(bf16[512,128]{1,0:T(8,128)(2,1)S(1)} %shard_map.60.refs_4_), channel_id=1, source_target_pairs={{0,8},{4,12},{8,0},{12,4},{1,9},{5,13},{9,1},{13,5},{2,10},{6,14},... | collective-permute-start | bytes 393224 | tf_op jit(solution)/shard_map/ppermute | solution.py:17
  27.9 3.8 %collective-permute-done.10.refs_7_ = bf16[512,128]{1,0:T(8,128)(2,1)S(1)} collective-permute-done((bf16[512,128]{1,0:T(8,128)(2,1)S(1)}, bf16[512,128]{1,0:T(8,128)(2,1)S(1)}, u32[]{:S(2)}, u32[]{:S(2)}) %collective-permute-start.10) | collective-permute-done | bytes 131104 | tf_op jit(solution)/shard_map/ppermute | solution.py:17
  31.8 2.2 %collective-permute-done.8.refs_5_ = bf16[512,128]{1,0:T(8,128)(2,1)S(1)} collective-permute-done((bf16[512,128]{1,0:T(8,128)(2,1)S(1)}, bf16[512,128]{1,0:T(8,128)(2,1)S(1)}, u32[]{:S(2)}, u32[]{:S(2)}) %collective-permute-start.8) | collective-permute-done | bytes 131104 | tf_op jit(solution)/shard_map/ppermute | solution.py:17
  34.0 3.7 %collective-permute-done.9.refs_6_ = bf16[512,128]{1,0:T(8,128)(2,1)S(1)} collective-permute-done((bf16[512,128]{1,0:T(8,128)(2,1)S(1)}, bf16[512,128]{1,0:T(8,128)(2,1)S(1)}, u32[]{:S(2)}, u32[]{:S(2)}) %collective-permute-start.9) | collective-permute-done | bytes 131104 | tf_op jit(solution)/shard_map/ppermute | solution.py:17
  37.7 0.8 %shard_map.61 = (bf16[2,128,128]{2,1,0:T(8,128)(2,1)S(1)}, bf16[2,128,128]{2,1,0:T(8,128)(2,1)S(1)}, bf16[2,128,128]{2,1,0:T(8,128)(2,1)S(1)}, bf16[2,128,128]{2,1,0:T(8,128)(2,1)S(1)}) custom-call(bf16[512,512]{1,0:T(8,128)(2,1)S(1)} %get-tuple-element.13.refs_0_, bf16[512,512]{1,0:T(8,128)(2,1)S(1)} %get-tuple-element.15.refs_1_, ...), custom_call_target="tpu_custom_call" | custom-call | flops 268435456 | bytes 2752512 | tf_op jit(solution)/shard_map/pallas_call | solution.py:48
  38.5 0.1 collective-permute-start.11
  38.6 1.6 %collective-permute-start.12 = (bf16[2,128,128]{2,1,0:T(8,128)(2,1)S(1)}, bf16[2,128,128]{2,1,0:T(8,128)(2,1)S(1)}, u32[]{:S(2)}, u32[]{:S(2)}) collective-permute-start(bf16[2,128,128]{2,1,0:T(8,128)(2,1)S(1)} %get-tuple-element.19), channel_id=1, source_target_pairs={{0,2},{1,3},{2,0},{3,1},{4,6},{5,7},{6,4},{7,5},{8,10},{9,11},{10,... | collective-permute-start | bytes 196616 | tf_op jit(solution)/shard_map/ppermute | solution.py:17
  40.1 0.3 collective-permute-start.13
  40.4 0.0 copy-done
  40.4 0.0 copy-done.1
  40.4 0.2 shard_map.55.refs_0_
  40.7 0.0 collective-permute-done.11.refs_3_
  40.7 2.4 %collective-permute-done.12.refs_4_ = bf16[2,128,128]{2,1,0:T(8,128)(2,1)S(1)} collective-permute-done((bf16[2,128,128]{2,1,0:T(8,128)(2,1)S(1)}, bf16[2,128,128]{2,1,0:T(8,128)(2,1)S(1)}, u32[]{:S(2)}, u32[]{:S(2)}) %collective-permute-start.12) | collective-permute-done | bytes 65568 | tf_op jit(solution)/shard_map/ppermute | solution.py:17
  43.1 1.1 %collective-permute-done.13.refs_5_ = bf16[2,128,128]{2,1,0:T(8,128)(2,1)S(1)} collective-permute-done((bf16[2,128,128]{2,1,0:T(8,128)(2,1)S(1)}, bf16[2,128,128]{2,1,0:T(8,128)(2,1)S(1)}, u32[]{:S(2)}, u32[]{:S(2)}) %collective-permute-start.13) | collective-permute-done | bytes 65568 | tf_op jit(solution)/shard_map/ppermute | solution.py:17
  44.2 1.0 %shard_map.62 = bf16[128,512]{1,0:T(8,128)(2,1)} custom-call(f32[128,512]{1,0:T(8,128)S(1)} %shard_map.55.refs_0_, bf16[3,512,512]{2,1,0:T(8,128)(2,1)S(1)} %copy-done, bf16[2,128,128]{2,1,0:T(8,128)(2,1)S(1)} %get-tuple-element.17.refs_2_, bf16[2,128,128]{2,1,0:T(8,128)(2,1)S(1)} %collective-permute-done.11.refs_3_, ...), custom_call_target="tpu_custom_call" | custom-call | bytes 2097152 | tf_op jit(solution)/shard_map/pallas_call | solution.py:48
  (8 shorter events, 0.1 us)
Async XLA Ops:
  0.0 1.9 %collective-permute-start = (bf16[128,512]{1,0:T(8,128)(2,1)}, bf16[128,512]{1,0:T(8,128)(2,1)S(1)}, u32[]{:S(2)}, u32[]{:S(2)}) collective-permute-start(bf16[128,512]{1,0:T(8,128)(2,1)} %refs_3_.1), channel_id=1, source_target_pairs={{0,1},{1,0},{2,3},{3,2},{4,5},{5,4},{6,7},{7,6},{8,9},{9,8},{10,11... | collective-permute-start | bytes 393224 | tf_op jit(solution)/shard_map/ppermute | solution.py:17
  1.8 7.5 %collective-permute-start.2 = (bf16[512,512]{1,0:T(8,128)(2,1)S(1)}, bf16[512,512]{1,0:T(8,128)(2,1)S(1)}, u32[]{:S(2)}, u32[]{:S(2)}) collective-permute-start(bf16[512,512]{1,0:T(8,128)(2,1)S(1)} %get-tuple-element.13.refs_0_), channel_id=1, source_target_pairs={{0,1},{1,0},{2,3},{3,2},{4,5},{5,4},{6,7},{7,6},{8,9},{9,8},{10,11... | collective-permute-start | bytes 1572872 | tf_op jit(solution)/shard_map/ppermute | solution.py:17
  1.9 5.3 %collective-permute-start.1 = (bf16[2,128,128]{2,1,0:T(8,128)(2,1)S(1)}, bf16[2,128,128]{2,1,0:T(8,128)(2,1)S(1)}, u32[]{:S(2)}, u32[]{:S(2)}) collective-permute-start(bf16[2,128,128]{2,1,0:T(8,128)(2,1)S(1)} %pad_maximum_fusion.1), channel_id=1, source_target_pairs={{0,2},{1,3},{2,0},{3,1},{4,6},{5,7},{6,4},{7,5},{8,10},{9,11},{10,... | collective-permute-start | bytes 196616 | tf_op jit(solution)/shard_map/ppermute | solution.py:17
  7.3 13.3 %collective-permute-start.3 = (bf16[512,512]{1,0:T(8,128)(2,1)S(1)}, bf16[512,512]{1,0:T(8,128)(2,1)S(1)}, u32[]{:S(2)}, u32[]{:S(2)}) collective-permute-start(bf16[512,512]{1,0:T(8,128)(2,1)S(1)} %shard_map.58), channel_id=1, source_target_pairs={{0,2},{1,3},{2,0},{3,1},{4,6},{5,7},{6,4},{7,5},{8,10},{9,11},{10,... | collective-permute-start | bytes 1572872 | tf_op jit(solution)/shard_map/ppermute | solution.py:17
  9.3 11.3 %collective-permute-start.5 = (bf16[2,2,128,128]{3,2,1,0:T(8,128)(2,1)S(1)}, bf16[2,2,128,128]{3,2,1,0:T(8,128)(2,1)S(1)}, u32[]{:S(2)}, u32[]{:S(2)}) collective-permute-start(bf16[2,2,128,128]{3,2,1,0:T(8,128)(2,1)S(1)} %get-tuple-element.16.refs_3_.refs_1_.refs_8_), channel_id=1, source_target_pairs={{0,4},{4,0},{8,12},{12,8},{1,5},{5,1},{9,13},{13,9},{2,6},{6,2},{1... | collective-permute-start | bytes 393224 | tf_op jit(solution)/shard_map/ppermute | solution.py:17
  10.9 11.7 %collective-permute-start.6 = (bf16[2,2,128,128]{3,2,1,0:T(8,128)(2,1)S(1)}, bf16[2,2,128,128]{3,2,1,0:T(8,128)(2,1)S(1)}, u32[]{:S(2)}, u32[]{:S(2)}) collective-permute-start(bf16[2,2,128,128]{3,2,1,0:T(8,128)(2,1)S(1)} %get-tuple-element.16.refs_3_.refs_1_.refs_8_), channel_id=1, source_target_pairs={{0,8},{4,12},{8,0},{12,4},{1,9},{5,13},{9,1},{13,5},{2,10},{6,14},... | collective-permute-start | bytes 393224 | tf_op jit(solution)/shard_map/ppermute | solution.py:17
  13.5 9.1 %collective-permute-start.7 = (bf16[2,2,128,128]{3,2,1,0:T(8,128)(2,1)S(1)}, bf16[2,2,128,128]{3,2,1,0:T(8,128)(2,1)S(1)}, u32[]{:S(2)}, u32[]{:S(2)}) collective-permute-start(bf16[2,2,128,128]{3,2,1,0:T(8,128)(2,1)S(1)} %get-tuple-element.16.refs_3_.refs_1_.refs_8_), channel_id=1, source_target_pairs={{0,12},{4,8},{8,4},{12,0},{1,13},{5,9},{9,5},{13,1},{2,14},{6,10},... | collective-permute-start | bytes 393224 | tf_op jit(solution)/shard_map/ppermute | solution.py:17
  20.6 2.6 %collective-permute-start.4 = (bf16[512,512]{1,0:T(8,128)(2,1)S(1)}, bf16[512,512]{1,0:T(8,128)(2,1)S(1)}, u32[]{:S(2)}, u32[]{:S(2)}) collective-permute-start(bf16[512,512]{1,0:T(8,128)(2,1)S(1)} %collective-permute-done.3.refs_2_), channel_id=1, source_target_pairs={{0,1},{1,0},{2,3},{3,2},{4,5},{5,4},{6,7},{7,6},{8,9},{9,8},{10,11... | collective-permute-start | bytes 1572872 | tf_op jit(solution)/shard_map/ppermute | solution.py:17
  23.5 17.0 %copy-start = (bf16[3,512,512]{2,1,0:T(8,128)(2,1)S(1)}, bf16[3,512,512]{2,1,0:T(8,128)(2,1)}, u32[]{:S(2)}) copy-start(bf16[3,512,512]{2,1,0:T(8,128)(2,1)} %refs_1_.5) | copy-start | bytes 4718596
  23.5 17.0 %copy-start.1 = (bf16[128,512]{1,0:T(8,128)(2,1)S(1)}, bf16[128,512]{1,0:T(8,128)(2,1)}, u32[]{:S(2)}) copy-start(bf16[128,512]{1,0:T(8,128)(2,1)} %refs_3_.1) | copy-start | bytes 393220
  23.5 8.3 %collective-permute-start.10 = (bf16[512,128]{1,0:T(8,128)(2,1)S(1)}, bf16[512,128]{1,0:T(8,128)(2,1)S(1)}, u32[]{:S(2)}, u32[]{:S(2)}) collective-permute-start(bf16[512,128]{1,0:T(8,128)(2,1)S(1)} %shard_map.60.refs_4_), channel_id=1, source_target_pairs={{0,12},{4,8},{8,4},{12,0},{1,13},{5,9},{9,5},{13,1},{2,14},{6,10},... | collective-permute-start | bytes 393224 | tf_op jit(solution)/shard_map/ppermute | solution.py:17
  26.4 7.7 %collective-permute-start.8 = (bf16[512,128]{1,0:T(8,128)(2,1)S(1)}, bf16[512,128]{1,0:T(8,128)(2,1)S(1)}, u32[]{:S(2)}, u32[]{:S(2)}) collective-permute-start(bf16[512,128]{1,0:T(8,128)(2,1)S(1)} %shard_map.60.refs_4_), channel_id=1, source_target_pairs={{0,4},{4,0},{8,12},{12,8},{1,5},{5,1},{9,13},{13,9},{2,6},{6,2},{1... | collective-permute-start | bytes 393224 | tf_op jit(solution)/shard_map/ppermute | solution.py:17
  27.1 10.6 %collective-permute-start.9 = (bf16[512,128]{1,0:T(8,128)(2,1)S(1)}, bf16[512,128]{1,0:T(8,128)(2,1)S(1)}, u32[]{:S(2)}, u32[]{:S(2)}) collective-permute-start(bf16[512,128]{1,0:T(8,128)(2,1)S(1)} %shard_map.60.refs_4_), channel_id=1, source_target_pairs={{0,8},{4,12},{8,0},{12,4},{1,9},{5,13},{9,1},{13,5},{2,10},{6,14},... | collective-permute-start | bytes 393224 | tf_op jit(solution)/shard_map/ppermute | solution.py:17
  38.5 2.2 %collective-permute-start.11 = (bf16[2,128,128]{2,1,0:T(8,128)(2,1)S(1)}, bf16[2,128,128]{2,1,0:T(8,128)(2,1)S(1)}, u32[]{:S(2)}, u32[]{:S(2)}) collective-permute-start(bf16[2,128,128]{2,1,0:T(8,128)(2,1)S(1)} %get-tuple-element.18), channel_id=1, source_target_pairs={{0,1},{1,0},{2,3},{3,2},{4,5},{5,4},{6,7},{7,6},{8,9},{9,8},{10,11... | collective-permute-start | bytes 196616 | tf_op jit(solution)/shard_map/ppermute | solution.py:17
  38.6 4.5 %collective-permute-start.12 = (bf16[2,128,128]{2,1,0:T(8,128)(2,1)S(1)}, bf16[2,128,128]{2,1,0:T(8,128)(2,1)S(1)}, u32[]{:S(2)}, u32[]{:S(2)}) collective-permute-start(bf16[2,128,128]{2,1,0:T(8,128)(2,1)S(1)} %get-tuple-element.19), channel_id=1, source_target_pairs={{0,2},{1,3},{2,0},{3,1},{4,6},{5,7},{6,4},{7,5},{8,10},{9,11},{10,... | collective-permute-start | bytes 196616 | tf_op jit(solution)/shard_map/ppermute | solution.py:17
  40.1 4.0 %collective-permute-start.13 = (bf16[2,128,128]{2,1,0:T(8,128)(2,1)S(1)}, bf16[2,128,128]{2,1,0:T(8,128)(2,1)S(1)}, u32[]{:S(2)}, u32[]{:S(2)}) collective-permute-start(bf16[2,128,128]{2,1,0:T(8,128)(2,1)S(1)} %get-tuple-element.20), channel_id=1, source_target_pairs={{0,3},{1,2},{2,1},{3,0},{4,7},{5,6},{6,5},{7,4},{8,11},{9,10},{10,... | collective-permute-start | bytes 196616 | tf_op jit(solution)/shard_map/ppermute | solution.py:17

commit v5 on v4

--- a/solution.py
+++ b/solution.py
@@ -125,26 +125,27 @@
     rows = [pl.ds(pl.multiple_of((rep ^ k) * tile, tile), tile) for k in range(n_rep)]
     total_ref[...] = apply_lanes(lanes, n_blk, tile, lambda m, k: firsts[m][rows[k], :])
     for k, out_ref in enumerate(outs):
-        out_ref[0] = firsts[0][rows[k], :]
-        out_ref[1] = (2.0 * total_ref[rows[k], :] - feats[k // 2, k % 2].astype(F32)).astype(BF16)
-
-
-def weigh(pieces, weight_ref, order):
+        if k < 2:
+            out_ref[1] = firsts[0][rows[k], :]
+        out_ref[0] = (2.0 * total_ref[rows[k], :] - feats[k // 2, k % 2].astype(F32)).astype(BF16)
+
+
+def weigh(pieces, weight_ref, order, masks):
     rep, width = lax.axis_index("rep"), pieces[0].shape[1]
-    rows = [pl.ds(pl.multiple_of((rep ^ k) * width, width), width) for k in range(len(pieces))]
+    rows = [pl.ds(pl.multiple_of((rep ^ k) * width, width), width) for k in masks]
     weights = [weight_ref[order, r, :] for r in rows]
     return dot(jnp.concatenate(pieces, axis=1), jnp.concatenate(weights, axis=0))
 
 
-def early_kernel(feats_ref, weight_ref, out_ref):
-    out_ref[...] = dot(feats_ref[...], weight_ref[0])
-
-
-def last_kernel(early_ref, weight_ref, *refs):
+def early_kernel(n_rep, feats_ref, weight_ref, *refs):
+    others, out_ref = [ref[...] for ref in refs[:-1]], refs[-1]
+    out_ref[...] = dot(feats_ref[...], weight_ref[0]) + weigh(others, weight_ref, 1, range(2, n_rep))
+
+
+def last_kernel(n_rep, early_ref, weight_ref, *refs):
     pieces, out_ref = refs[:-1], refs[-1]
-    total = early_ref[...]
-    for i in range(2):
-        total = total + weigh([piece[i] for piece in pieces], weight_ref, 1 + i)
+    total = early_ref[...] + weigh([piece[1] for piece in pieces[:2]], weight_ref, 1, range(2))
+    total = total + weigh([piece[0] for piece in pieces], weight_ref, 2, range(n_rep))
     out_ref[...] = total.astype(BF16)
 
 
@@ -200,17 +201,27 @@
         vmem=vmem, flops=macs,
     )
     firsts = [swap(first, "blk", m) for m in range(1, n_blk)]
-    firsts = [first, *firsts]
+    others = [swap(lax.dynamic_slice_in_dim(first, (rep ^ k) * tile, tile, 0), "rep", k) for k in range(2, n_rep)]
+    tied = after([*firsts, *others])
+    firsts, others = [first, *tied[: n_blk - 1]], tied[n_blk - 1 :]
     seconds = call(
         functools.partial(second_kernel, n_blk, n_rep, tile),
-        (jax.ShapeDtypeStruct((2, tile, width), BF16),) * n_rep,
+        [jax.ShapeDtypeStruct((2 if k < 2 else 1, tile, width), BF16) for k in range(n_rep)],
         *lanes, *firsts, own_rows,
         vmem=vmem, flops=macs,
         scratch=[pltpu.VMEM((strip, width), F32)],
     )
     seconds = [swap(rows, "rep", k) if k else rows for k, rows in enumerate(seconds)]
-    early = call(early_kernel, jax.ShapeDtypeStruct((tile, feat), F32), features, order_weights)
-    return call(last_kernel, jax.ShapeDtypeStruct((tile, feat), BF16), early, order_weights, *seconds)
+    early = call(
+        functools.partial(early_kernel, n_rep),
+        jax.ShapeDtypeStruct((tile, feat), F32),
+        features, order_weights, *others,
+    )
+    return call(
+        functools.partial(last_kernel, n_rep),
+        jax.ShapeDtypeStruct((tile, feat), BF16),
+        early, order_weights, *seconds,
+    )
 
 
 def solution(mesh):

time: 45.3 us -> 44.5 us (0.982)
  waiting for transfers between devices: 24.4 us -> 23 us
  starting transfers between devices: 16.4 us -> 17 us
    ppermute x14 -> x16, waiting for transfers between devices: 24.4 us -> 23 us  [swap(): return lax.ppermute(array, axis, [(i, i ^ mask) for i in range(peers)])]
    ppermute x14 -> x16, starting transfers between devices: 16.4 us -> 17 us  [swap(): return lax.ppermute(array, axis, [(i, i ^ mask) for i in range(peers)])]
  transfers between devices with their start and end apart: 14 -> 16, of which waited for: 8 -> 8; matrix products, arithmetic and copies ran while one was open for 0% -> 0% of each run, Pallas kernels for 5% -> 5%
where the time goes in v5:
time: 44.5 us; the launch traced here: 44.4 us
  waiting for transfers between devices  23 us (52%)
  starting transfers between devices  17 us (38%)
  Pallas kernels  4.12 us (9%)
    ppermute x16, waiting for transfers between devices, swap(): return lax.ppermute(array, axis, [(i, i ^ mask) for i in range(peers)])  23 us
    ppermute x16, starting transfers between devices, swap(): return lax.ppermute(array, axis, [(i, i ^ mask) for i in range(peers)])  17 us
    pallas_call x6, Pallas kernels, call(): pl.pallas_call(body, out_shape=out_shapes, in_specs=[home] * hbm + [whole...  4.12 us
  transfers between devices with their start and end apart: 16, of which 8 were waited for; matrix products, arithmetic and copies ran while one was open for 0% of the time, Pallas kernels for 5%

profile of v5, /device:TPU:0, one launch (start us, length us, event | category | flops | bytes accessed | tf_op | source)
XLA Modules:
  0.0 44.4 jit_solution(13240963599249905195)
XLA Ops:
  0.0 0.5 %collective-permute-start = (bf16[128,512]{1,0:T(8,128)(2,1)}, bf16[128,512]{1,0:T(8,128)(2,1)S(1)}, u32[]{:S(2)}, u32[]{:S(2)}) collective-permute-start(bf16[128,512]{1,0:T(8,128)(2,1)} %refs_0_.3), channel_id=1, source_target_pairs={{0,1},{1,0},{2,3},{3,2},{4,5},{5,4},{6,7},{7,6},{8,9},{9,8},{10,11... | collective-permute-start | bytes 393224 | tf_op jit(solution)/shard_map/ppermute | solution.py:17
  0.5 1.3 %shard_map.55 = (bf16[512,512]{1,0:T(8,128)(2,1)S(1)}, bf16[2,128,128]{2,1,0:T(8,128)(2,1)S(1)}) custom-call(s32[1,1,4,4]{3,2,1,0:T(4,128)} %refs_0_.2, s32[1,1,4]{2,1,0:T(1,128)} %refs_1_.3, bf16[1,1,4,4,128,128]{5,4,3,2,1,0:T(8,128)(2,1)} %refs_2_.1, bf16[128,512]{1,0:T(8,128)(2,1)} %refs_0_.3), custom_call_target="tpu_custom_call" | custom-call | bytes 655440 | tf_op jit(solution)/shard_map/pallas_call | solution.py:48
  1.8 0.1 collective-permute-start.4
  1.9 0.0 collective-permute-done
  1.9 3.0 %collective-permute-start.1 = (bf16[2,128,128]{2,1,0:T(8,128)(2,1)S(1)}, bf16[2,128,128]{2,1,0:T(8,128)(2,1)S(1)}, u32[]{:S(2)}, u32[]{:S(2)}) collective-permute-start(bf16[2,128,128]{2,1,0:T(8,128)(2,1)S(1)} %pad_maximum_fusion.1), channel_id=1, source_target_pairs={{0,2},{1,3},{2,0},{3,1},{4,6},{5,7},{6,4},{7,5},{8,10},{9,11},{10,... | collective-permute-start | bytes 196616 | tf_op jit(solution)/shard_map/ppermute | solution.py:17
  5.0 2.3 %collective-permute-done.1.refs_1_ = bf16[2,128,128]{2,1,0:T(8,128)(2,1)S(1)} collective-permute-done((bf16[2,128,128]{2,1,0:T(8,128)(2,1)S(1)}, bf16[2,128,128]{2,1,0:T(8,128)(2,1)S(1)}, u32[]{:S(2)}, u32[]{:S(2)}) %collective-permute-start.1) | collective-permute-done | bytes 65568 | tf_op jit(solution)/shard_map/ppermute | solution.py:17
  7.2 2.0 %collective-permute-start.2 = (bf16[512,512]{1,0:T(8,128)(2,1)S(1)}, bf16[512,512]{1,0:T(8,128)(2,1)S(1)}, u32[]{:S(2)}, u32[]{:S(2)}) collective-permute-start(bf16[512,512]{1,0:T(8,128)(2,1)S(1)} %shard_map.56), channel_id=1, source_target_pairs={{0,2},{1,3},{2,0},{3,1},{4,6},{5,7},{6,4},{7,5},{8,10},{9,11},{10,... | collective-permute-start | bytes 1572872 | tf_op jit(solution)/shard_map/ppermute | solution.py:17
  9.2 0.0 collective-permute-done.4.refs_1_
  9.3 3.7 %collective-permute-start.7 = (bf16[2,2,128,128]{3,2,1,0:T(8,128)(2,1)S(1)}, bf16[2,2,128,128]{3,2,1,0:T(8,128)(2,1)S(1)}, u32[]{:S(2)}, u32[]{:S(2)}) collective-permute-start(bf16[2,2,128,128]{3,2,1,0:T(8,128)(2,1)S(1)} %get-tuple-element.20.refs_3_.refs_1_.refs_8_), channel_id=1, source_target_pairs={{0,12},{4,8},{8,4},{12,0},{1,13},{5,9},{9,5},{13,1},{2,14},{6,10},... | collective-permute-start | bytes 393224 | tf_op jit(solution)/shard_map/ppermute | solution.py:17
  12.9 0.0 collective-permute-start.6
  13.0 0.8 %collective-permute-start.5 = (bf16[2,2,128,128]{3,2,1,0:T(8,128)(2,1)S(1)}, bf16[2,2,128,128]{3,2,1,0:T(8,128)(2,1)S(1)}, u32[]{:S(2)}, u32[]{:S(2)}) collective-permute-start(bf16[2,2,128,128]{3,2,1,0:T(8,128)(2,1)S(1)} %get-tuple-element.20.refs_3_.refs_1_.refs_8_), channel_id=1, source_target_pairs={{0,4},{4,0},{8,12},{12,8},{1,5},{5,1},{9,13},{13,9},{2,6},{6,2},{1... | collective-permute-start | bytes 393224 | tf_op jit(solution)/shard_map/ppermute | solution.py:17
  13.7 6.9 %collective-permute-done.2.refs_2_ = bf16[512,512]{1,0:T(8,128)(2,1)S(1)} collective-permute-done((bf16[512,512]{1,0:T(8,128)(2,1)S(1)}, bf16[512,512]{1,0:T(8,128)(2,1)S(1)}, u32[]{:S(2)}, u32[]{:S(2)}) %collective-permute-start.2) | collective-permute-done | bytes 524320 | tf_op jit(solution)/shard_map/ppermute | solution.py:17
  20.6 0.0 collective-permute-start.3
  20.6 0.0 collective-permute-done.7.refs_6_.refs_4_
  20.6 2.2 %collective-permute-done.6.refs_5_.refs_3_ = bf16[2,2,128,128]{3,2,1,0:T(8,128)(2,1)S(1)} collective-permute-done((bf16[2,2,128,128]{3,2,1,0:T(8,128)(2,1)S(1)}, bf16[2,2,128,128]{3,2,1,0:T(8,128)(2,1)S(1)}, u32[]{:S(2)}, u32[]{:S(2)}) %collective-permute-start.6) | collective-permute-done | bytes 131104 | tf_op jit(solution)/shard_map/ppermute | solution.py:17
  22.8 0.0 collective-permute-done.5.refs_4_.refs_2_
  22.8 0.6 %shard_map.58.refs_5_ = f32[512,128]{1,0:T(8,128)S(1)} custom-call(bf16[512,512]{1,0:T(8,128)(2,1)S(1)} %get-tuple-element.18.refs_0_, bf16[512,512]{1,0:T(8,128)(2,1)S(1)} %get-tuple-element.21.refs_1_, bf16[512,512]{1,0:T(8,128)(2,1)S(1)} %collective-permute-done.2.refs_2_, bf16[2,2,128,128]{3,2,1,0:T(8,128)(2,1)S(1)} %get-tuple-element.20.refs_3_.refs_1_.refs_8_, ...), custom_call_target="tpu_custom_call" | custom-call | flops 34359738368 | bytes 2097152 | tf_op jit(solution)/shard_map/pallas_call | solution.py:48
  23.4 0.0 collective-permute-done.3.refs_0_.refs_3_
  23.4 0.3 shard_map.59.refs_4_
  23.7 2.6 %collective-permute-start.10 = (bf16[512,128]{1,0:T(8,128)(2,1)S(1)}, bf16[512,128]{1,0:T(8,128)(2,1)S(1)}, u32[]{:S(2)}, u32[]{:S(2)}) collective-permute-start(bf16[512,128]{1,0:T(8,128)(2,1)S(1)} %shard_map.59.refs_4_), channel_id=1, source_target_pairs={{0,12},{4,8},{8,4},{12,0},{1,13},{5,9},{9,5},{13,1},{2,14},{6,10},... | collective-permute-start | bytes 393224 | tf_op jit(solution)/shard_map/ppermute | solution.py:17
  26.3 0.0 collective-permute-start.9
  26.3 1.8 %collective-permute-start.8 = (bf16[512,128]{1,0:T(8,128)(2,1)S(1)}, bf16[512,128]{1,0:T(8,128)(2,1)S(1)}, u32[]{:S(2)}, u32[]{:S(2)}) collective-permute-start(bf16[512,128]{1,0:T(8,128)(2,1)S(1)} %shard_map.59.refs_4_), channel_id=1, source_target_pairs={{0,4},{4,0},{8,12},{12,8},{1,5},{5,1},{9,13},{13,9},{2,6},{6,2},{1... | collective-permute-start | bytes 393224 | tf_op jit(solution)/shard_map/ppermute | solution.py:17
  28.1 0.0 collective-permute-start.12
  28.1 0.0 copy-start
  28.1 0.0 copy-start.1
  28.2 0.6 %collective-permute-start.11 = (bf16[128,128]{1,0:T(8,128)(2,1)S(1)}, bf16[128,128]{1,0:T(8,128)(2,1)S(1)}, u32[]{:S(2)}, u32[]{:S(2)}) collective-permute-start(bf16[128,128]{1,0:T(8,128)(2,1)S(1)} %get-tuple-element.32), channel_id=1, source_target_pairs={{0,2},{1,3},{2,0},{3,1},{4,6},{5,7},{6,4},{7,5},{8,10},{9,11},{10,... | collective-permute-start | bytes 98312 | tf_op jit(solution)/shard_map/ppermute | solution.py:17
  28.8 2.7 %collective-permute-done.12.refs_4_ = bf16[128,128]{1,0:T(8,128)(2,1)S(1)} collective-permute-done((bf16[128,128]{1,0:T(8,128)(2,1)S(1)}, bf16[128,128]{1,0:T(8,128)(2,1)S(1)}, u32[]{:S(2)}, u32[]{:S(2)}) %collective-permute-start.12) | collective-permute-done | bytes 32800 | tf_op jit(solution)/shard_map/ppermute | solution.py:17
  31.5 0.7 %collective-permute-done.11.refs_3_ = bf16[128,128]{1,0:T(8,128)(2,1)S(1)} collective-permute-done((bf16[128,128]{1,0:T(8,128)(2,1)S(1)}, bf16[128,128]{1,0:T(8,128)(2,1)S(1)}, u32[]{:S(2)}, u32[]{:S(2)}) %collective-permute-start.11) | collective-permute-done | bytes 32800 | tf_op jit(solution)/shard_map/ppermute | solution.py:17
  32.2 0.0 collective-permute-done.10.refs_2_
  32.2 5.5 %collective-permute-done.9.refs_1_ = bf16[512,128]{1,0:T(8,128)(2,1)S(1)} collective-permute-done((bf16[512,128]{1,0:T(8,128)(2,1)S(1)}, bf16[512,128]{1,0:T(8,128)(2,1)S(1)}, u32[]{:S(2)}, u32[]{:S(2)}) %collective-permute-start.9) | collective-permute-done | bytes 131104 | tf_op jit(solution)/shard_map/ppermute | solution.py:17
  37.7 0.0 collective-permute-done.8.refs_0_
  37.7 0.8 %shard_map.62 = (bf16[2,128,128]{2,1,0:T(8,128)(2,1)S(1)}, bf16[2,128,128]{2,1,0:T(8,128)(2,1)S(1)}, bf16[1,128,128]{2,1,0:T(8,128)(2,1)S(1)}, bf16[1,128,128]{2,1,0:T(8,128)(2,1)S(1)}) custom-call(bf16[512,512]{1,0:T(8,128)(2,1)S(1)} %get-tuple-element.18.refs_0_, bf16[512,512]{1,0:T(8,128)(2,1)S(1)} %get-tuple-element.21.refs_1_, ...), custom_call_target="tpu_custom_call" | custom-call | flops 268435456 | bytes 2752512 | tf_op jit(solution)/shard_map/pallas_call | solution.py:48
  38.5 0.1 collective-permute-start.13
  38.6 1.5 %collective-permute-start.14 = (bf16[1,128,128]{2,1,0:T(8,128)(2,1)S(1)}, bf16[1,128,128]{2,1,0:T(8,128)(2,1)S(1)}, u32[]{:S(2)}, u32[]{:S(2)}) collective-permute-start(bf16[1,128,128]{2,1,0:T(8,128)(2,1)S(1)} %get-tuple-element.29), channel_id=1, source_target_pairs={{0,2},{1,3},{2,0},{3,1},{4,6},{5,7},{6,4},{7,5},{8,10},{9,11},{10,... | collective-permute-start | bytes 98312 | tf_op jit(solution)/shard_map/ppermute | solution.py:17
  40.1 0.3 collective-permute-start.15
  40.4 0.0 copy-done
  40.4 0.0 copy-done.1
  40.4 0.3 shard_map.61.refs_0_
  40.7 1.8 %collective-permute-done.14.refs_4_ = bf16[1,128,128]{2,1,0:T(8,128)(2,1)S(1)} collective-permute-done((bf16[1,128,128]{2,1,0:T(8,128)(2,1)S(1)}, bf16[1,128,128]{2,1,0:T(8,128)(2,1)S(1)}, u32[]{:S(2)}, u32[]{:S(2)}) %collective-permute-start.14) | collective-permute-done | bytes 32800 | tf_op jit(solution)/shard_map/ppermute | solution.py:17
  42.5 0.9 %collective-permute-done.15.refs_5_ = bf16[1,128,128]{2,1,0:T(8,128)(2,1)S(1)} collective-permute-done((bf16[1,128,128]{2,1,0:T(8,128)(2,1)S(1)}, bf16[1,128,128]{2,1,0:T(8,128)(2,1)S(1)}, u32[]{:S(2)}, u32[]{:S(2)}) %collective-permute-start.15) | collective-permute-done | bytes 32800 | tf_op jit(solution)/shard_map/ppermute | solution.py:17
  43.5 0.0 collective-permute-done.13.refs_3_
  43.5 0.9 %shard_map.63 = bf16[128,512]{1,0:T(8,128)(2,1)} custom-call(f32[128,512]{1,0:T(8,128)S(1)} %shard_map.61.refs_0_, bf16[3,512,512]{2,1,0:T(8,128)(2,1)S(1)} %copy-done, bf16[2,128,128]{2,1,0:T(8,128)(2,1)S(1)} %get-tuple-element.27.refs_2_, bf16[2,128,128]{2,1,0:T(8,128)(2,1)S(1)} %collective-permute-done.13.refs_3_, ...), custom_call_target="tpu_custom_call" | custom-call | bytes 2031616 | tf_op jit(solution)/shard_map/pallas_call | solution.py:48
  (10 shorter events, 0.1 us)
Async XLA Ops:
  0.0 1.9 %collective-permute-start = (bf16[128,512]{1,0:T(8,128)(2,1)}, bf16[128,512]{1,0:T(8,128)(2,1)S(1)}, u32[]{:S(2)}, u32[]{:S(2)}) collective-permute-start(bf16[128,512]{1,0:T(8,128)(2,1)} %refs_0_.3), channel_id=1, source_target_pairs={{0,1},{1,0},{2,3},{3,2},{4,5},{5,4},{6,7},{7,6},{8,9},{9,8},{10,11... | collective-permute-start | bytes 393224 | tf_op jit(solution)/shard_map/ppermute | solution.py:17
  1.8 7.5 %collective-permute-start.4 = (bf16[512,512]{1,0:T(8,128)(2,1)S(1)}, bf16[512,512]{1,0:T(8,128)(2,1)S(1)}, u32[]{:S(2)}, u32[]{:S(2)}) collective-permute-start(bf16[512,512]{1,0:T(8,128)(2,1)S(1)} %get-tuple-element.18.refs_0_), channel_id=1, source_target_pairs={{0,1},{1,0},{2,3},{3,2},{4,5},{5,4},{6,7},{7,6},{8,9},{9,8},{10,11... | collective-permute-start | bytes 1572872 | tf_op jit(solution)/shard_map/ppermute | solution.py:17
  1.9 5.3 %collective-permute-start.1 = (bf16[2,128,128]{2,1,0:T(8,128)(2,1)S(1)}, bf16[2,128,128]{2,1,0:T(8,128)(2,1)S(1)}, u32[]{:S(2)}, u32[]{:S(2)}) collective-permute-start(bf16[2,128,128]{2,1,0:T(8,128)(2,1)S(1)} %pad_maximum_fusion.1), channel_id=1, source_target_pairs={{0,2},{1,3},{2,0},{3,1},{4,6},{5,7},{6,4},{7,5},{8,10},{9,11},{10,... | collective-permute-start | bytes 196616 | tf_op jit(solution)/shard_map/ppermute | solution.py:17
  7.2 13.3 %collective-permute-start.2 = (bf16[512,512]{1,0:T(8,128)(2,1)S(1)}, bf16[512,512]{1,0:T(8,128)(2,1)S(1)}, u32[]{:S(2)}, u32[]{:S(2)}) collective-permute-start(bf16[512,512]{1,0:T(8,128)(2,1)S(1)} %shard_map.56), channel_id=1, source_target_pairs={{0,2},{1,3},{2,0},{3,1},{4,6},{5,7},{6,4},{7,5},{8,10},{9,11},{10,... | collective-permute-start | bytes 1572872 | tf_op jit(solution)/shard_map/ppermute | solution.py:17
  9.3 11.3 %collective-permute-start.7 = (bf16[2,2,128,128]{3,2,1,0:T(8,128)(2,1)S(1)}, bf16[2,2,128,128]{3,2,1,0:T(8,128)(2,1)S(1)}, u32[]{:S(2)}, u32[]{:S(2)}) collective-permute-start(bf16[2,2,128,128]{3,2,1,0:T(8,128)(2,1)S(1)} %get-tuple-element.20.refs_3_.refs_1_.refs_8_), channel_id=1, source_target_pairs={{0,12},{4,8},{8,4},{12,0},{1,13},{5,9},{9,5},{13,1},{2,14},{6,10},... | collective-permute-start | bytes 393224 | tf_op jit(solution)/shard_map/ppermute | solution.py:17
  12.9 9.8 %collective-permute-start.6 = (bf16[2,2,128,128]{3,2,1,0:T(8,128)(2,1)S(1)}, bf16[2,2,128,128]{3,2,1,0:T(8,128)(2,1)S(1)}, u32[]{:S(2)}, u32[]{:S(2)}) collective-permute-start(bf16[2,2,128,128]{3,2,1,0:T(8,128)(2,1)S(1)} %get-tuple-element.20.refs_3_.refs_1_.refs_8_), channel_id=1, source_target_pairs={{0,8},{4,12},{8,0},{12,4},{1,9},{5,13},{9,1},{13,5},{2,10},{6,14},... | collective-permute-start | bytes 393224 | tf_op jit(solution)/shard_map/ppermute | solution.py:17
  13.0 9.8 %collective-permute-start.5 = (bf16[2,2,128,128]{3,2,1,0:T(8,128)(2,1)S(1)}, bf16[2,2,128,128]{3,2,1,0:T(8,128)(2,1)S(1)}, u32[]{:S(2)}, u32[]{:S(2)}) collective-permute-start(bf16[2,2,128,128]{3,2,1,0:T(8,128)(2,1)S(1)} %get-tuple-element.20.refs_3_.refs_1_.refs_8_), channel_id=1, source_target_pairs={{0,4},{4,0},{8,12},{12,8},{1,5},{5,1},{9,13},{13,9},{2,6},{6,2},{1... | collective-permute-start | bytes 393224 | tf_op jit(solution)/shard_map/ppermute | solution.py:17
  20.6 2.8 %collective-permute-start.3 = (bf16[512,512]{1,0:T(8,128)(2,1)S(1)}, bf16[512,512]{1,0:T(8,128)(2,1)S(1)}, u32[]{:S(2)}, u32[]{:S(2)}) collective-permute-start(bf16[512,512]{1,0:T(8,128)(2,1)S(1)} %collective-permute-done.2.refs_2_), channel_id=1, source_target_pairs={{0,1},{1,0},{2,3},{3,2},{4,5},{5,4},{6,7},{7,6},{8,9},{9,8},{10,11... | collective-permute-start | bytes 1572872 | tf_op jit(solution)/shard_map/ppermute | solution.py:17
  23.7 8.5 %collective-permute-start.10 = (bf16[512,128]{1,0:T(8,128)(2,1)S(1)}, bf16[512,128]{1,0:T(8,128)(2,1)S(1)}, u32[]{:S(2)}, u32[]{:S(2)}) collective-permute-start(bf16[512,128]{1,0:T(8,128)(2,1)S(1)} %shard_map.59.refs_4_), channel_id=1, source_target_pairs={{0,12},{4,8},{8,4},{12,0},{1,13},{5,9},{9,5},{13,1},{2,14},{6,10},... | collective-permute-start | bytes 393224 | tf_op jit(solution)/shard_map/ppermute | solution.py:17
  26.3 11.4 %collective-permute-start.9 = (bf16[512,128]{1,0:T(8,128)(2,1)S(1)}, bf16[512,128]{1,0:T(8,128)(2,1)S(1)}, u32[]{:S(2)}, u32[]{:S(2)}) collective-permute-start(bf16[512,128]{1,0:T(8,128)(2,1)S(1)} %shard_map.59.refs_4_), channel_id=1, source_target_pairs={{0,8},{4,12},{8,0},{12,4},{1,9},{5,13},{9,1},{13,5},{2,10},{6,14},... | collective-permute-start | bytes 393224 | tf_op jit(solution)/shard_map/ppermute | solution.py:17
  26.3 11.4 %collective-permute-start.8 = (bf16[512,128]{1,0:T(8,128)(2,1)S(1)}, bf16[512,128]{1,0:T(8,128)(2,1)S(1)}, u32[]{:S(2)}, u32[]{:S(2)}) collective-permute-start(bf16[512,128]{1,0:T(8,128)(2,1)S(1)} %shard_map.59.refs_4_), channel_id=1, source_target_pairs={{0,4},{4,0},{8,12},{12,8},{1,5},{5,1},{9,13},{13,9},{2,6},{6,2},{1... | collective-permute-start | bytes 393224 | tf_op jit(solution)/shard_map/ppermute | solution.py:17
  28.1 3.3 %collective-permute-start.12 = (bf16[128,128]{1,0:T(8,128)(2,1)S(1)}, bf16[128,128]{1,0:T(8,128)(2,1)S(1)}, u32[]{:S(2)}, u32[]{:S(2)}) collective-permute-start(bf16[128,128]{1,0:T(8,128)(2,1)S(1)} %get-tuple-element.31), channel_id=1, source_target_pairs={{0,3},{1,2},{2,1},{3,0},{4,7},{5,6},{6,5},{7,4},{8,11},{9,10},{10,... | collective-permute-start | bytes 98312 | tf_op jit(solution)/shard_map/ppermute | solution.py:17
  28.1 12.3 %copy-start = (bf16[3,512,512]{2,1,0:T(8,128)(2,1)S(1)}, bf16[3,512,512]{2,1,0:T(8,128)(2,1)}, u32[]{:S(2)}) copy-start(bf16[3,512,512]{2,1,0:T(8,128)(2,1)} %refs_1_.5) | copy-start | bytes 4718596
  28.1 12.3 %copy-start.1 = (bf16[128,512]{1,0:T(8,128)(2,1)S(1)}, bf16[128,512]{1,0:T(8,128)(2,1)}, u32[]{:S(2)}) copy-start(bf16[128,512]{1,0:T(8,128)(2,1)} %refs_0_.3) | copy-start | bytes 393220
  28.2 4.0 %collective-permute-start.11 = (bf16[128,128]{1,0:T(8,128)(2,1)S(1)}, bf16[128,128]{1,0:T(8,128)(2,1)S(1)}, u32[]{:S(2)}, u32[]{:S(2)}) collective-permute-start(bf16[128,128]{1,0:T(8,128)(2,1)S(1)} %get-tuple-element.32), channel_id=1, source_target_pairs={{0,2},{1,3},{2,0},{3,1},{4,6},{5,7},{6,4},{7,5},{8,10},{9,11},{10,... | collective-permute-start | bytes 98312 | tf_op jit(solution)/shard_map/ppermute | solution.py:17
  38.5 5.0 %collective-permute-start.13 = (bf16[2,128,128]{2,1,0:T(8,128)(2,1)S(1)}, bf16[2,128,128]{2,1,0:T(8,128)(2,1)S(1)}, u32[]{:S(2)}, u32[]{:S(2)}) collective-permute-start(bf16[2,128,128]{2,1,0:T(8,128)(2,1)S(1)} %get-tuple-element.28), channel_id=1, source_target_pairs={{0,1},{1,0},{2,3},{3,2},{4,5},{5,4},{6,7},{7,6},{8,9},{9,8},{10,11... | collective-permute-start | bytes 196616 | tf_op jit(solution)/shard_map/ppermute | solution.py:17
  38.6 4.0 %collective-permute-start.14 = (bf16[1,128,128]{2,1,0:T(8,128)(2,1)S(1)}, bf16[1,128,128]{2,1,0:T(8,128)(2,1)S(1)}, u32[]{:S(2)}, u32[]{:S(2)}) collective-permute-start(bf16[1,128,128]{2,1,0:T(8,128)(2,1)S(1)} %get-tuple-element.29), channel_id=1, source_target_pairs={{0,2},{1,3},{2,0},{3,1},{4,6},{5,7},{6,4},{7,5},{8,10},{9,11},{10,... | collective-permute-start | bytes 98312 | tf_op jit(solution)/shard_map/ppermute | solution.py:17
  40.1 3.3 %collective-permute-start.15 = (bf16[1,128,128]{2,1,0:T(8,128)(2,1)S(1)}, bf16[1,128,128]{2,1,0:T(8,128)(2,1)S(1)}, u32[]{:S(2)}, u32[]{:S(2)}) collective-permute-start(bf16[1,128,128]{2,1,0:T(8,128)(2,1)S(1)} %get-tuple-element.30), channel_id=1, source_target_pairs={{0,3},{1,2},{2,1},{3,0},{4,7},{5,6},{6,5},{7,4},{8,11},{9,10},{10,... | collective-permute-start | bytes 98312 | tf_op jit(solution)/shard_map/ppermute | solution.py:17

commit v6 on v5

--- a/solution.py
+++ b/solution.py
@@ -95,31 +95,38 @@
 
 def apply_lanes(lanes, n_blk, tile, rows_of):
     total = None
-    each = n_blk // len(lanes[0])
     for m in range(n_blk):
-        at = (m % each) * tile
-        left = jnp.concatenate([halves[m // each][:, at : at + tile] for halves in lanes], axis=1)
+        columns = []
+        for halves in lanes:
+            each = n_blk // len(halves)
+            at = (m % each) * tile
+            columns.append(halves[m // each][:, at : at + tile])
+        left = jnp.concatenate(columns, axis=1)
         right = jnp.concatenate([rows_of(m, k) for k in range(len(lanes))], axis=0)
         part = dot(left, right)
         total = part if total is None else total + part
     return total
 
 
-def paired(refs, n):
-    return [refs[i : i + n] for i in range(0, len(refs), n)]
-
-
-def part_kernel(n_blk, tile, masks, *refs):
-    n = len(masks)
-    lanes, pieces, more, out_ref = paired(refs[:n], 1), refs[n : n + n_blk], refs[n + n_blk : -1], refs[-1]
+def grouped(refs, sizes):
+    lists, refs = [], list(refs)
+    for size in sizes:
+        lists.append(refs[:size])
+        refs = refs[size:]
+    return lists, refs
+
+
+def part_kernel(n_blk, tile, masks, sizes, *refs):
+    lanes, refs = grouped(refs, sizes)
+    pieces, more, out_ref = refs[:n_blk], refs[n_blk:-1], refs[-1]
     total = apply_lanes(lanes, n_blk, tile, lambda m, i: pieces[m][masks[i] // 2, masks[i] % 2])
     if more:
         total = total + more[0][...]
     out_ref[...] = total.astype(out_ref.dtype)
 
 
-def second_kernel(n_blk, n_rep, tile, *refs):
-    lanes, refs = paired(refs[:n_rep], 1), refs[n_rep:]
+def second_kernel(n_blk, n_rep, tile, sizes, *refs):
+    lanes, refs = grouped(refs, sizes)
     firsts, feats, outs, total_ref = refs[:n_blk], refs[n_blk], refs[n_blk + 1 : -1], refs[-1]
     rep = lax.axis_index("rep")
     rows = [pl.ds(pl.multiple_of((rep ^ k) * tile, tile), tile) for k in range(n_rep)]
@@ -180,10 +187,12 @@
     own_rows, mate = after([jnp.stack(pieces), swap(dense, "rep", 1)])
     own_chip = [dense, mate]
     rows = [swap(own_rows, "blk", m) if m else own_rows for m in range(n_blk)]
-    arrived = [swap(after([dense], pieces[i])[0], "rep", 2 * i) for i in range(1, chips)]
-    lanes = [*own_chip]
-    for got in arrived:
-        lanes += [got, swap(got, "rep", 1)]
+    lanes = [[lane] for lane in own_chip]
+    middle = n_blk // 2 * tile
+    for i in range(1, chips):
+        parts = after([p for p in (dense[:, :middle], dense[:, middle:])], pieces[i])
+        arrived = [swap(part, "rep", 2 * i) for part in parts]
+        lanes += [arrived, [swap(got, "rep", 1) for got in arrived]]
 
     strip_shape = jax.ShapeDtypeStruct((strip, width), BF16)
     vmem = n_rep * lane_bytes + 2 * rows_bytes + 4 * MIB
@@ -191,13 +200,13 @@
     soon = [0, 1, *range(2, n_rep, 2)]
     late = [*range(3, n_rep, 2)]
     part = call(
-        functools.partial(part_kernel, n_blk, tile, soon), jax.ShapeDtypeStruct((strip, width), F32),
-        *[lanes[k] for k in soon], *rows,
+        functools.partial(part_kernel, n_blk, tile, soon, [len(lanes[k]) for k in soon]), jax.ShapeDtypeStruct((strip, width), F32),
+        *[h for k in soon for h in lanes[k]], *rows,
         vmem=vmem, flops=1 << 35,
     )
     first = call(
-        functools.partial(part_kernel, n_blk, tile, late), strip_shape,
-        *[lanes[k] for k in late], *rows, part,
+        functools.partial(part_kernel, n_blk, tile, late, [len(lanes[k]) for k in late]), strip_shape,
+        *[h for k in late for h in lanes[k]], *rows, part,
         vmem=vmem, flops=macs,
     )
     firsts = [swap(first, "blk", m) for m in range(1, n_blk)]
@@ -205,9 +214,9 @@
     tied = after([*firsts, *others])
     firsts, others = [first, *tied[: n_blk - 1]], tied[n_blk - 1 :]
     seconds = call(
-        functools.partial(second_kernel, n_blk, n_rep, tile),
+        functools.partial(second_kernel, n_blk, n_rep, tile, [len(lane) for lane in lanes]),
         [jax.ShapeDtypeStruct((2 if k < 2 else 1, tile, width), BF16) for k in range(n_rep)],
-        *lanes, *firsts, own_rows,
+        *[h for lane in lanes for h in lane], *firsts, own_rows,
         vmem=vmem, flops=macs,
         scratch=[pltpu.VMEM((strip, width), F32)],
     )

time: 44.5 us -> 44.2 us (level)
  waiting for transfers between devices: 23 us -> 21.3 us
  starting transfers between devices: 17 us -> 18.4 us
    ppermute x16 -> x18, waiting for transfers between devices: 23 us -> 21.3 us  [swap(): return lax.ppermute(array, axis, [(i, i ^ mask) for i in range(peers)])]
    ppermute x16 -> x18, starting transfers between devices: 17 us -> 18.4 us  [swap(): return lax.ppermute(array, axis, [(i, i ^ mask) for i in range(peers)])]
  transfers between devices with their start and end apart: 16 -> 18, of which waited for: 8 -> 9; matrix products, arithmetic and copies ran while one was open for 0% -> 0% of each run, Pallas kernels for 5% -> 5%
where the time goes in v6:
time: 44.2 us; the launch traced here: 44 us
  waiting for transfers between devices  21.3 us (48%)
  starting transfers between devices  18.4 us (42%)
  Pallas kernels  4.13 us (9%)
    ppermute x18, waiting for transfers between devices, swap(): return lax.ppermute(array, axis, [(i, i ^ mask) for i in range(peers)])  21.3 us
    ppermute x18, starting transfers between devices, swap(): return lax.ppermute(array, axis, [(i, i ^ mask) for i in range(peers)])  18.4 us
    pallas_call x6, Pallas kernels, call(): pl.pallas_call(body, out_shape=out_shapes, in_specs=[home] * hbm + [whole...  4.12 us
  transfers between devices with their start and end apart: 18, of which 9 were waited for; matrix products, arithmetic and copies ran while one was open for 0% of the time, Pallas kernels for 5%

profile of v6, /device:TPU:0, one launch (start us, length us, event | category | flops | bytes accessed | tf_op | source)
XLA Modules:
  0.0 44.0 jit_solution(17625381871457864099)
XLA Ops:
  0.0 0.5 %collective-permute-start = (bf16[128,512]{1,0:T(8,128)(2,1)}, bf16[128,512]{1,0:T(8,128)(2,1)S(1)}, u32[]{:S(2)}, u32[]{:S(2)}) collective-permute-start(bf16[128,512]{1,0:T(8,128)(2,1)} %refs_0_.3), channel_id=1, source_target_pairs={{0,1},{1,0},{2,3},{3,2},{4,5},{5,4},{6,7},{7,6},{8,9},{9,8},{10,11... | collective-permute-start | bytes 393224 | tf_op jit(solution)/shard_map/ppermute | solution.py:17
  0.5 1.3 %shard_map.55 = (bf16[512,512]{1,0:T(8,128)(2,1)S(1)}, bf16[2,128,128]{2,1,0:T(8,128)(2,1)S(1)}) custom-call(s32[1,1,4,4]{3,2,1,0:T(4,128)} %refs_0_.2, s32[1,1,4]{2,1,0:T(1,128)} %refs_1_.3, bf16[1,1,4,4,128,128]{5,4,3,2,1,0:T(8,128)(2,1)} %refs_2_.1, bf16[128,512]{1,0:T(8,128)(2,1)} %refs_0_.3), custom_call_target="tpu_custom_call" | custom-call | bytes 655440 | tf_op jit(solution)/shard_map/pallas_call | solution.py:48
  1.8 0.1 collective-permute-start.6
  1.9 0.0 collective-permute-done
  2.0 3.0 %collective-permute-start.1 = (bf16[2,128,128]{2,1,0:T(8,128)(2,1)S(1)}, bf16[2,128,128]{2,1,0:T(8,128)(2,1)S(1)}, u32[]{:S(2)}, u32[]{:S(2)}) collective-permute-start(bf16[2,128,128]{2,1,0:T(8,128)(2,1)S(1)} %pad_maximum_fusion.1), channel_id=1, source_target_pairs={{0,2},{1,3},{2,0},{3,1},{4,6},{5,7},{6,4},{7,5},{8,10},{9,11},{10,... | collective-permute-start | bytes 196616 | tf_op jit(solution)/shard_map/ppermute | solution.py:17
  5.0 2.3 %collective-permute-done.1.refs_2_ = bf16[2,128,128]{2,1,0:T(8,128)(2,1)S(1)} collective-permute-done((bf16[2,128,128]{2,1,0:T(8,128)(2,1)S(1)}, bf16[2,128,128]{2,1,0:T(8,128)(2,1)S(1)}, u32[]{:S(2)}, u32[]{:S(2)}) %collective-permute-start.1) | collective-permute-done | bytes 65568 | tf_op jit(solution)/shard_map/ppermute | solution.py:17
  7.2 2.0 %collective-permute-start.2 = (bf16[512,256]{1,0:T(8,128)(2,1)S(1)}, bf16[512,256]{1,0:T(8,128)(2,1)S(1)}, u32[]{:S(2)}, u32[]{:S(2)}) collective-permute-start(bf16[512,256]{1,0:T(8,128)(2,1)S(1)} %get-tuple-element.22), channel_id=1, source_target_pairs={{0,2},{1,3},{2,0},{3,1},{4,6},{5,7},{6,4},{7,5},{8,10},{9,11},{10,... | collective-permute-start | bytes 786440 | tf_op jit(solution)/shard_map/ppermute | solution.py:17
  9.2 0.1 collective-permute-start.4
  9.3 0.0 collective-permute-done.6.refs_1_
  9.3 4.2 %collective-permute-start.9 = (bf16[2,2,128,128]{3,2,1,0:T(8,128)(2,1)S(1)}, bf16[2,2,128,128]{3,2,1,0:T(8,128)(2,1)S(1)}, u32[]{:S(2)}, u32[]{:S(2)}) collective-permute-start(bf16[2,2,128,128]{3,2,1,0:T(8,128)(2,1)S(1)} %get-tuple-element.24.refs_4_.refs_2_.refs_10_), channel_id=1, source_target_pairs={{0,12},{4,8},{8,4},{12,0},{1,13},{5,9},{9,5},{13,1},{2,14},{6,10},... | collective-permute-start | bytes 393224 | tf_op jit(solution)/shard_map/ppermute | solution.py:17
  13.5 0.0 collective-permute-start.8
  13.5 0.6 %collective-permute-start.7 = (bf16[2,2,128,128]{3,2,1,0:T(8,128)(2,1)S(1)}, bf16[2,2,128,128]{3,2,1,0:T(8,128)(2,1)S(1)}, u32[]{:S(2)}, u32[]{:S(2)}) collective-permute-start(bf16[2,2,128,128]{3,2,1,0:T(8,128)(2,1)S(1)} %get-tuple-element.24.refs_4_.refs_2_.refs_10_), channel_id=1, source_target_pairs={{0,4},{4,0},{8,12},{12,8},{1,5},{5,1},{9,13},{13,9},{2,6},{6,2},{1... | collective-permute-start | bytes 393224 | tf_op jit(solution)/shard_map/ppermute | solution.py:17
  14.1 2.4 %collective-permute-done.2.refs_2_ = bf16[512,256]{1,0:T(8,128)(2,1)S(1)} collective-permute-done((bf16[512,256]{1,0:T(8,128)(2,1)S(1)}, bf16[512,256]{1,0:T(8,128)(2,1)S(1)}, u32[]{:S(2)}, u32[]{:S(2)}) %collective-permute-start.2) | collective-permute-done | bytes 262176 | tf_op jit(solution)/shard_map/ppermute | solution.py:17
  16.5 0.0 collective-permute-start.3
  16.5 4.1 %collective-permute-done.4.refs_3_ = bf16[512,256]{1,0:T(8,128)(2,1)S(1)} collective-permute-done((bf16[512,256]{1,0:T(8,128)(2,1)S(1)}, bf16[512,256]{1,0:T(8,128)(2,1)S(1)}, u32[]{:S(2)}, u32[]{:S(2)}) %collective-permute-start.4) | collective-permute-done | bytes 262176 | tf_op jit(solution)/shard_map/ppermute | solution.py:17
  20.6 0.0 collective-permute-start.5
  20.6 0.0 collective-permute-done.9.refs_7_.refs_5_
  20.6 2.4 %collective-permute-done.8.refs_6_.refs_4_ = bf16[2,2,128,128]{3,2,1,0:T(8,128)(2,1)S(1)} collective-permute-done((bf16[2,2,128,128]{3,2,1,0:T(8,128)(2,1)S(1)}, bf16[2,2,128,128]{3,2,1,0:T(8,128)(2,1)S(1)}, u32[]{:S(2)}, u32[]{:S(2)}) %collective-permute-start.8) | collective-permute-done | bytes 131104 | tf_op jit(solution)/shard_map/ppermute | solution.py:17
  23.0 0.0 collective-permute-done.7.refs_5_.refs_3_
  23.0 0.6 %shard_map.58.refs_6_ = f32[512,128]{1,0:T(8,128)S(1)} custom-call(bf16[512,512]{1,0:T(8,128)(2,1)S(1)} %get-tuple-element.20.refs_0_, bf16[512,512]{1,0:T(8,128)(2,1)S(1)} %get-tuple-element.25.refs_1_, bf16[512,256]{1,0:T(8,128)(2,1)S(1)} %collective-permute-done.2.refs_2_, bf16[512,256]{1,0:T(8,128)(2,1)S(1)} %collective-permute-done.4.refs_3_, ...), custom_call_target="tpu_custom_call" | custom-call | flops 34359738368 | bytes 2097152 | tf_op jit(solution)/shard_map/pallas_call | solution.py:48
  23.6 0.0 collective-permute-done.3.refs_0_.refs_4_
  23.6 0.0 collective-permute-done.5.refs_1_.refs_5_
  23.6 0.3 shard_map.59.refs_6_
  23.9 2.6 %collective-permute-start.12 = (bf16[512,128]{1,0:T(8,128)(2,1)S(1)}, bf16[512,128]{1,0:T(8,128)(2,1)S(1)}, u32[]{:S(2)}, u32[]{:S(2)}) collective-permute-start(bf16[512,128]{1,0:T(8,128)(2,1)S(1)} %shard_map.59.refs_6_), channel_id=1, source_target_pairs={{0,12},{4,8},{8,4},{12,0},{1,13},{5,9},{9,5},{13,1},{2,14},{6,10},... | collective-permute-start | bytes 393224 | tf_op jit(solution)/shard_map/ppermute | solution.py:17
  26.5 0.0 collective-permute-start.11
  26.5 1.9 %collective-permute-start.10 = (bf16[512,128]{1,0:T(8,128)(2,1)S(1)}, bf16[512,128]{1,0:T(8,128)(2,1)S(1)}, u32[]{:S(2)}, u32[]{:S(2)}) collective-permute-start(bf16[512,128]{1,0:T(8,128)(2,1)S(1)} %shard_map.59.refs_6_), channel_id=1, source_target_pairs={{0,4},{4,0},{8,12},{12,8},{1,5},{5,1},{9,13},{13,9},{2,6},{6,2},{1... | collective-permute-start | bytes 393224 | tf_op jit(solution)/shard_map/ppermute | solution.py:17
  28.4 0.0 collective-permute-start.14
  28.4 0.0 copy-start
  28.4 0.0 copy-start.1
  28.4 1.6 %collective-permute-start.13 = (bf16[128,128]{1,0:T(8,128)(2,1)S(1)}, bf16[128,128]{1,0:T(8,128)(2,1)S(1)}, u32[]{:S(2)}, u32[]{:S(2)}) collective-permute-start(bf16[128,128]{1,0:T(8,128)(2,1)S(1)} %get-tuple-element.38), channel_id=1, source_target_pairs={{0,2},{1,3},{2,0},{3,1},{4,6},{5,7},{6,4},{7,5},{8,10},{9,11},{10,... | collective-permute-start | bytes 98312 | tf_op jit(solution)/shard_map/ppermute | solution.py:17
  30.0 2.0 %collective-permute-done.14.refs_4_ = bf16[128,128]{1,0:T(8,128)(2,1)S(1)} collective-permute-done((bf16[128,128]{1,0:T(8,128)(2,1)S(1)}, bf16[128,128]{1,0:T(8,128)(2,1)S(1)}, u32[]{:S(2)}, u32[]{:S(2)}) %collective-permute-start.14) | collective-permute-done | bytes 32800 | tf_op jit(solution)/shard_map/ppermute | solution.py:17
  32.0 0.4 collective-permute-done.13.refs_3_
  32.4 0.0 collective-permute-done.12.refs_2_
  32.4 4.9 %collective-permute-done.11.refs_1_ = bf16[512,128]{1,0:T(8,128)(2,1)S(1)} collective-permute-done((bf16[512,128]{1,0:T(8,128)(2,1)S(1)}, bf16[512,128]{1,0:T(8,128)(2,1)S(1)}, u32[]{:S(2)}, u32[]{:S(2)}) %collective-permute-start.11) | collective-permute-done | bytes 131104 | tf_op jit(solution)/shard_map/ppermute | solution.py:17
  37.3 0.0 collective-permute-done.10.refs_0_
  37.3 0.8 %shard_map.62 = (bf16[2,128,128]{2,1,0:T(8,128)(2,1)S(1)}, bf16[2,128,128]{2,1,0:T(8,128)(2,1)S(1)}, bf16[1,128,128]{2,1,0:T(8,128)(2,1)S(1)}, bf16[1,128,128]{2,1,0:T(8,128)(2,1)S(1)}) custom-call(bf16[512,512]{1,0:T(8,128)(2,1)S(1)} %get-tuple-element.20.refs_0_, bf16[512,512]{1,0:T(8,128)(2,1)S(1)} %get-tuple-element.25.refs_1_, ...), custom_call_target="tpu_custom_call" | custom-call | flops 268435456 | bytes 2752512 | tf_op jit(solution)/shard_map/pallas_call | solution.py:48
  38.1 0.1 collective-permute-start.15
  38.1 1.6 %collective-permute-start.16 = (bf16[1,128,128]{2,1,0:T(8,128)(2,1)S(1)}, bf16[1,128,128]{2,1,0:T(8,128)(2,1)S(1)}, u32[]{:S(2)}, u32[]{:S(2)}) collective-permute-start(bf16[1,128,128]{2,1,0:T(8,128)(2,1)S(1)} %get-tuple-element.33), channel_id=1, source_target_pairs={{0,2},{1,3},{2,0},{3,1},{4,6},{5,7},{6,4},{7,5},{8,10},{9,11},{10,... | collective-permute-start | bytes 98312 | tf_op jit(solution)/shard_map/ppermute | solution.py:17
  39.7 0.3 collective-permute-start.17
  40.0 0.0 copy-done
  40.0 0.0 copy-done.1
  40.0 0.3 shard_map.61.refs_0_
  40.3 1.8 %collective-permute-done.16.refs_4_ = bf16[1,128,128]{2,1,0:T(8,128)(2,1)S(1)} collective-permute-done((bf16[1,128,128]{2,1,0:T(8,128)(2,1)S(1)}, bf16[1,128,128]{2,1,0:T(8,128)(2,1)S(1)}, u32[]{:S(2)}, u32[]{:S(2)}) %collective-permute-start.16) | collective-permute-done | bytes 32800 | tf_op jit(solution)/shard_map/ppermute | solution.py:17
  42.1 0.9 %collective-permute-done.17.refs_5_ = bf16[1,128,128]{2,1,0:T(8,128)(2,1)S(1)} collective-permute-done((bf16[1,128,128]{2,1,0:T(8,128)(2,1)S(1)}, bf16[1,128,128]{2,1,0:T(8,128)(2,1)S(1)}, u32[]{:S(2)}, u32[]{:S(2)}) %collective-permute-start.17) | collective-permute-done | bytes 32800 | tf_op jit(solution)/shard_map/ppermute | solution.py:17
  43.1 0.0 collective-permute-done.15.refs_3_
  43.1 0.9 %shard_map.63 = bf16[128,512]{1,0:T(8,128)(2,1)} custom-call(f32[128,512]{1,0:T(8,128)S(1)} %shard_map.61.refs_0_, bf16[3,512,512]{2,1,0:T(8,128)(2,1)S(1)} %copy-done, bf16[2,128,128]{2,1,0:T(8,128)(2,1)S(1)} %get-tuple-element.31.refs_2_, bf16[2,128,128]{2,1,0:T(8,128)(2,1)S(1)} %collective-permute-done.15.refs_3_, ...), custom_call_target="tpu_custom_call" | custom-call | bytes 2031616 | tf_op jit(solution)/shard_map/pallas_call | solution.py:48
  (10 shorter events, 0.1 us)
Async XLA Ops:
  0.0 1.9 %collective-permute-start = (bf16[128,512]{1,0:T(8,128)(2,1)}, bf16[128,512]{1,0:T(8,128)(2,1)S(1)}, u32[]{:S(2)}, u32[]{:S(2)}) collective-permute-start(bf16[128,512]{1,0:T(8,128)(2,1)} %refs_0_.3), channel_id=1, source_target_pairs={{0,1},{1,0},{2,3},{3,2},{4,5},{5,4},{6,7},{7,6},{8,9},{9,8},{10,11... | collective-permute-start | bytes 393224 | tf_op jit(solution)/shard_map/ppermute | solution.py:17
  1.8 7.5 %collective-permute-start.6 = (bf16[512,512]{1,0:T(8,128)(2,1)S(1)}, bf16[512,512]{1,0:T(8,128)(2,1)S(1)}, u32[]{:S(2)}, u32[]{:S(2)}) collective-permute-start(bf16[512,512]{1,0:T(8,128)(2,1)S(1)} %get-tuple-element.20.refs_0_), channel_id=1, source_target_pairs={{0,1},{1,0},{2,3},{3,2},{4,5},{5,4},{6,7},{7,6},{8,9},{9,8},{10,11... | collective-permute-start | bytes 1572872 | tf_op jit(solution)/shard_map/ppermute | solution.py:17
  2.0 5.3 %collective-permute-start.1 = (bf16[2,128,128]{2,1,0:T(8,128)(2,1)S(1)}, bf16[2,128,128]{2,1,0:T(8,128)(2,1)S(1)}, u32[]{:S(2)}, u32[]{:S(2)}) collective-permute-start(bf16[2,128,128]{2,1,0:T(8,128)(2,1)S(1)} %pad_maximum_fusion.1), channel_id=1, source_target_pairs={{0,2},{1,3},{2,0},{3,1},{4,6},{5,7},{6,4},{7,5},{8,10},{9,11},{10,... | collective-permute-start | bytes 196616 | tf_op jit(solution)/shard_map/ppermute | solution.py:17
  7.2 9.2 %collective-permute-start.2 = (bf16[512,256]{1,0:T(8,128)(2,1)S(1)}, bf16[512,256]{1,0:T(8,128)(2,1)S(1)}, u32[]{:S(2)}, u32[]{:S(2)}) collective-permute-start(bf16[512,256]{1,0:T(8,128)(2,1)S(1)} %get-tuple-element.22), channel_id=1, source_target_pairs={{0,2},{1,3},{2,0},{3,1},{4,6},{5,7},{6,4},{7,5},{8,10},{9,11},{10,... | collective-permute-start | bytes 786440 | tf_op jit(solution)/shard_map/ppermute | solution.py:17
  9.2 11.4 %collective-permute-start.4 = (bf16[512,256]{1,0:T(8,128)(2,1)S(1)}, bf16[512,256]{1,0:T(8,128)(2,1)S(1)}, u32[]{:S(2)}, u32[]{:S(2)}) collective-permute-start(bf16[512,256]{1,0:T(8,128)(2,1)S(1)} %get-tuple-element.23), channel_id=1, source_target_pairs={{0,2},{1,3},{2,0},{3,1},{4,6},{5,7},{6,4},{7,5},{8,10},{9,11},{10,... | collective-permute-start | bytes 786440 | tf_op jit(solution)/shard_map/ppermute | solution.py:17
  9.3 11.3 %collective-permute-start.9 = (bf16[2,2,128,128]{3,2,1,0:T(8,128)(2,1)S(1)}, bf16[2,2,128,128]{3,2,1,0:T(8,128)(2,1)S(1)}, u32[]{:S(2)}, u32[]{:S(2)}) collective-permute-start(bf16[2,2,128,128]{3,2,1,0:T(8,128)(2,1)S(1)} %get-tuple-element.24.refs_4_.refs_2_.refs_10_), channel_id=1, source_target_pairs={{0,12},{4,8},{8,4},{12,0},{1,13},{5,9},{9,5},{13,1},{2,14},{6,10},... | collective-permute-start | bytes 393224 | tf_op jit(solution)/shard_map/ppermute | solution.py:17
  13.5 9.5 %collective-permute-start.8 = (bf16[2,2,128,128]{3,2,1,0:T(8,128)(2,1)S(1)}, bf16[2,2,128,128]{3,2,1,0:T(8,128)(2,1)S(1)}, u32[]{:S(2)}, u32[]{:S(2)}) collective-permute-start(bf16[2,2,128,128]{3,2,1,0:T(8,128)(2,1)S(1)} %get-tuple-element.24.refs_4_.refs_2_.refs_10_), channel_id=1, source_target_pairs={{0,8},{4,12},{8,0},{12,4},{1,9},{5,13},{9,1},{13,5},{2,10},{6,14},... | collective-permute-start | bytes 393224 | tf_op jit(solution)/shard_map/ppermute | solution.py:17
  13.5 9.5 %collective-permute-start.7 = (bf16[2,2,128,128]{3,2,1,0:T(8,128)(2,1)S(1)}, bf16[2,2,128,128]{3,2,1,0:T(8,128)(2,1)S(1)}, u32[]{:S(2)}, u32[]{:S(2)}) collective-permute-start(bf16[2,2,128,128]{3,2,1,0:T(8,128)(2,1)S(1)} %get-tuple-element.24.refs_4_.refs_2_.refs_10_), channel_id=1, source_target_pairs={{0,4},{4,0},{8,12},{12,8},{1,5},{5,1},{9,13},{13,9},{2,6},{6,2},{1... | collective-permute-start | bytes 393224 | tf_op jit(solution)/shard_map/ppermute | solution.py:17
  16.5 7.1 %collective-permute-start.3 = (bf16[512,256]{1,0:T(8,128)(2,1)S(1)}, bf16[512,256]{1,0:T(8,128)(2,1)S(1)}, u32[]{:S(2)}, u32[]{:S(2)}) collective-permute-start(bf16[512,256]{1,0:T(8,128)(2,1)S(1)} %collective-permute-done.2.refs_2_), channel_id=1, source_target_pairs={{0,1},{1,0},{2,3},{3,2},{4,5},{5,4},{6,7},{7,6},{8,9},{9,8},{10,11... | collective-permute-start | bytes 786440 | tf_op jit(solution)/shard_map/ppermute | solution.py:17
  20.6 3.0 %collective-permute-start.5 = (bf16[512,256]{1,0:T(8,128)(2,1)S(1)}, bf16[512,256]{1,0:T(8,128)(2,1)S(1)}, u32[]{:S(2)}, u32[]{:S(2)}) collective-permute-start(bf16[512,256]{1,0:T(8,128)(2,1)S(1)} %collective-permute-done.4.refs_3_), channel_id=1, source_target_pairs={{0,1},{1,0},{2,3},{3,2},{4,5},{5,4},{6,7},{7,6},{8,9},{9,8},{10,11... | collective-permute-start | bytes 786440 | tf_op jit(solution)/shard_map/ppermute | solution.py:17
  23.9 8.5 %collective-permute-start.12 = (bf16[512,128]{1,0:T(8,128)(2,1)S(1)}, bf16[512,128]{1,0:T(8,128)(2,1)S(1)}, u32[]{:S(2)}, u32[]{:S(2)}) collective-permute-start(bf16[512,128]{1,0:T(8,128)(2,1)S(1)} %shard_map.59.refs_6_), channel_id=1, source_target_pairs={{0,12},{4,8},{8,4},{12,0},{1,13},{5,9},{9,5},{13,1},{2,14},{6,10},... | collective-permute-start | bytes 393224 | tf_op jit(solution)/shard_map/ppermute | solution.py:17
  26.5 10.8 %collective-permute-start.11 = (bf16[512,128]{1,0:T(8,128)(2,1)S(1)}, bf16[512,128]{1,0:T(8,128)(2,1)S(1)}, u32[]{:S(2)}, u32[]{:S(2)}) collective-permute-start(bf16[512,128]{1,0:T(8,128)(2,1)S(1)} %shard_map.59.refs_6_), channel_id=1, source_target_pairs={{0,8},{4,12},{8,0},{12,4},{1,9},{5,13},{9,1},{13,5},{2,10},{6,14},... | collective-permute-start | bytes 393224 | tf_op jit(solution)/shard_map/ppermute | solution.py:17
  26.5 10.8 %collective-permute-start.10 = (bf16[512,128]{1,0:T(8,128)(2,1)S(1)}, bf16[512,128]{1,0:T(8,128)(2,1)S(1)}, u32[]{:S(2)}, u32[]{:S(2)}) collective-permute-start(bf16[512,128]{1,0:T(8,128)(2,1)S(1)} %shard_map.59.refs_6_), channel_id=1, source_target_pairs={{0,4},{4,0},{8,12},{12,8},{1,5},{5,1},{9,13},{13,9},{2,6},{6,2},{1... | collective-permute-start | bytes 393224 | tf_op jit(solution)/shard_map/ppermute | solution.py:17
  28.4 3.6 %collective-permute-start.14 = (bf16[128,128]{1,0:T(8,128)(2,1)S(1)}, bf16[128,128]{1,0:T(8,128)(2,1)S(1)}, u32[]{:S(2)}, u32[]{:S(2)}) collective-permute-start(bf16[128,128]{1,0:T(8,128)(2,1)S(1)} %get-tuple-element.37), channel_id=1, source_target_pairs={{0,3},{1,2},{2,1},{3,0},{4,7},{5,6},{6,5},{7,4},{8,11},{9,10},{10,... | collective-permute-start | bytes 98312 | tf_op jit(solution)/shard_map/ppermute | solution.py:17
  28.4 11.6 %copy-start = (bf16[3,512,512]{2,1,0:T(8,128)(2,1)S(1)}, bf16[3,512,512]{2,1,0:T(8,128)(2,1)}, u32[]{:S(2)}) copy-start(bf16[3,512,512]{2,1,0:T(8,128)(2,1)} %refs_1_.5) | copy-start | bytes 4718596
  28.4 11.6 %copy-start.1 = (bf16[128,512]{1,0:T(8,128)(2,1)S(1)}, bf16[128,512]{1,0:T(8,128)(2,1)}, u32[]{:S(2)}) copy-start(bf16[128,512]{1,0:T(8,128)(2,1)} %refs_0_.3) | copy-start | bytes 393220
  28.4 4.0 %collective-permute-start.13 = (bf16[128,128]{1,0:T(8,128)(2,1)S(1)}, bf16[128,128]{1,0:T(8,128)(2,1)S(1)}, u32[]{:S(2)}, u32[]{:S(2)}) collective-permute-start(bf16[128,128]{1,0:T(8,128)(2,1)S(1)} %get-tuple-element.38), channel_id=1, source_target_pairs={{0,2},{1,3},{2,0},{3,1},{4,6},{5,7},{6,4},{7,5},{8,10},{9,11},{10,... | collective-permute-start | bytes 98312 | tf_op jit(solution)/shard_map/ppermute | solution.py:17
  38.1 5.0 %collective-permute-start.15 = (bf16[2,128,128]{2,1,0:T(8,128)(2,1)S(1)}, bf16[2,128,128]{2,1,0:T(8,128)(2,1)S(1)}, u32[]{:S(2)}, u32[]{:S(2)}) collective-permute-start(bf16[2,128,128]{2,1,0:T(8,128)(2,1)S(1)} %get-tuple-element.32), channel_id=1, source_target_pairs={{0,1},{1,0},{2,3},{3,2},{4,5},{5,4},{6,7},{7,6},{8,9},{9,8},{10,11... | collective-permute-start | bytes 196616 | tf_op jit(solution)/shard_map/ppermute | solution.py:17
  38.1 4.0 %collective-permute-start.16 = (bf16[1,128,128]{2,1,0:T(8,128)(2,1)S(1)}, bf16[1,128,128]{2,1,0:T(8,128)(2,1)S(1)}, u32[]{:S(2)}, u32[]{:S(2)}) collective-permute-start(bf16[1,128,128]{2,1,0:T(8,128)(2,1)S(1)} %get-tuple-element.33), channel_id=1, source_target_pairs={{0,2},{1,3},{2,0},{3,1},{4,6},{5,7},{6,4},{7,5},{8,10},{9,11},{10,... | collective-permute-start | bytes 98312 | tf_op jit(solution)/shard_map/ppermute | solution.py:17
  39.7 3.3 %collective-permute-start.17 = (bf16[1,128,128]{2,1,0:T(8,128)(2,1)S(1)}, bf16[1,128,128]{2,1,0:T(8,128)(2,1)S(1)}, u32[]{:S(2)}, u32[]{:S(2)}) collective-permute-start(bf16[1,128,128]{2,1,0:T(8,128)(2,1)S(1)} %get-tuple-element.34), channel_id=1, source_target_pairs={{0,3},{1,2},{2,1},{3,0},{4,7},{5,6},{6,5},{7,4},{8,11},{9,10},{10,... | collective-permute-start | bytes 98312 | tf_op jit(solution)/shard_map/ppermute | solution.py:17
